TPU v7x, 512 devices: a whole 4x4x16 slice. The times are simulated.
512 devices in a mesh: clip: 8 (over y, core), blk: 16 (over x, z_hi), uly: 4 (over z_lo).
Axes of the slice: x: 4, y: 4, z: 16 (z_hi: 4, z_lo: 4; z = z_hi * 4 + z_lo), core: 2. Of those that a mesh axis runs over, the one named last changes fastest.
Arguments:
- queries: bfloat16 [49152, 2560], P(('clip', 'blk', 'uly')), parts along dimension 0, may hold values from -8 to 8
- keys: bfloat16 [49152, 2560], P(('clip', 'blk', 'uly')), parts along dimension 0, may hold values from -8 to 8
- values: bfloat16 [49152, 2560], P(('clip', 'blk', 'uly')), parts along dimension 0, may hold values from -6 to 6
- text_keys: bfloat16 [4096, 2560], P('clip', 'uly'), parts along dimension 0, may hold values from -8 to 8
- text_values: bfloat16 [4096, 2560], P('clip', 'uly'), parts along dimension 0, may hold values from -6 to 6
- text_len: int32 [8], P('clip'), parts along dimension 0, may hold values from 128 to 512
- tile_map: int32 [128], P('clip'), parts along dimension 0, may hold values from 0 to 15, as said below
- mod_gain: float32 [2560], replicated, may hold values from 0.1 to 1.9
- mod_shift: float32 [2560], replicated, may hold values from -3 to 3
- head_weight: bfloat16 [2560, 64], replicated, may hold values from -0.125 to 0.125
- head_bias: float32 [64], replicated, may hold values from -3 to 3
- conv_weight: bfloat16 [432, 384], replicated, may hold values from -0.3125 to 0.3125
- conv_bias: float32 [384], replicated, may hold values from -3 to 3
- norm_gain: float32 [384], replicated, may hold values from 0.1 to 1.9
Outputs:
- video_features: bfloat16 [128, 32, 48, 384], P(('clip', 'blk'), 'uly'), parts along dimension 0
There are 8 independent parts, one for each index of `clip`. A program takes and returns all parts, laid end to end along the dimension named above; an argument that names none is the same for every part. Nothing has to cross between parts.
Inputs may be any that keep to these rules, and one draw needn't show every extreme that they name: Text keys at index text_len or later are padding. A permutation: token block b, the tokens on index b of blk, holds latent frame tile_map[b].
All inputs are finite; a program needn't handle non-finite values.
Results may differ from a plain program's by a relative error of at most 0.012.
Values may be sent and summed in bfloat16 or wider, within the bound.
No kernel may reach another device: no remote copies, remote signals or barrier semaphores. Data moves between devices by JAX's collectives and lax.ppermute only.
A program may use at most 192 MiB of HBM per device.

v0:
```python
import jax
import jax.numpy as jnp
from jax import lax
from jax.sharding import PartitionSpec as P

PCOL = 24
HDIM = 128
TXT = 512
LAT = 16


def shifted(block, axis, distance):
    devices = range(lax.axis_size(axis))
    route = [((i - distance) % len(devices), i) for i in devices]
    return lax.ppermute(block, axis, route)


def padded(block, sides, width):
    for axis, dim in sides:
        count = lax.axis_size(axis)
        forward = [(i, i + 1) for i in range(count - 1)]
        backward = [(target, source) for source, target in forward]
        low = lax.ppermute(
            lax.slice_in_dim(block, block.shape[dim] - width, None, axis=dim), axis, forward
        )
        high = lax.ppermute(lax.slice_in_dim(block, 0, width, axis=dim), axis, backward)
        block = jnp.concatenate([low, block, high], axis=dim)
    return block


def absorb(carried, key_part, value_part, query_heads, scaling):
    running_max, running_sum, weighted = carried
    heads_local = query_heads.shape[1]
    key_heads = key_part.reshape(key_part.shape[0], heads_local, HDIM)
    value_heads = value_part.reshape(value_part.shape[0], heads_local, HDIM)
    scores = (
        jnp.einsum("qhd,khd->hqk", query_heads, key_heads, preferred_element_type=jnp.float32)
        * scaling
    )
    newest = jnp.maximum(running_max, jnp.max(scores, axis=-1))
    factor = jnp.exp(running_max - newest)
    weights = jnp.exp(scores - newest[..., None])
    running_sum = running_sum * factor + jnp.sum(weights, axis=-1)
    weighted = weighted * factor[..., None] + jnp.einsum(
        "hqk,khd->hqd",
        weights.astype(jnp.bfloat16),
        value_heads,
        preferred_element_type=jnp.float32,
    )
    return (newest, running_sum, weighted)


def per_device(
    queries,
    keys,
    values,
    text_keys,
    text_values,
    text_len,
    tile_map,
    mod_gain,
    mod_shift,
    head_weight,
    head_bias,
    conv_weight,
    conv_bias,
    norm_gain,
):
    scaling = HDIM ** (-0.5)
    heads_local = text_keys.shape[1] // HDIM
    query_all, key_all, value_all = (
        lax.all_to_all(queries, "uly", split_axis=1, concat_axis=0, tiled=True),
        lax.all_to_all(keys, "uly", split_axis=1, concat_axis=0, tiled=True),
        lax.all_to_all(values, "uly", split_axis=1, concat_axis=0, tiled=True),
    )
    row_count = query_all.shape[0]
    query_heads = query_all.reshape(row_count, heads_local, HDIM)
    initial = (
        jnp.full((heads_local, row_count), -1e30, jnp.float32),
        jnp.zeros((heads_local, row_count), jnp.float32),
        jnp.zeros((heads_local, row_count, HDIM), jnp.float32),
    )
    first_state = absorb(initial, key_all, value_all, query_heads, scaling)
    paired = jnp.stack([key_all, value_all])

    def advance(turn_index, loop_state):
        state_now, pair_now = loop_state
        pair_now = shifted(pair_now, "blk", 1)
        return (absorb(state_now, pair_now[0], pair_now[1], query_heads, scaling), pair_now)

    final_state, paired = lax.fori_loop(0, lax.axis_size("blk") - 1, advance, (first_state, paired))
    self_out = final_state[2] / final_state[1][..., None]
    text_key_heads = text_keys.reshape(TXT, heads_local, HDIM)
    text_value_heads = text_values.reshape(TXT, heads_local, HDIM)
    usable = (jnp.arange(TXT) < text_len[0])[None, None, :]
    text_scores = (
        jnp.einsum("qhd,khd->hqk", query_heads, text_key_heads, preferred_element_type=jnp.float32)
        * scaling
    )
    text_scores = jnp.where(usable, text_scores, -1e30)
    text_weights = jnp.where(
        usable, jnp.exp(text_scores - jnp.max(text_scores, axis=-1, keepdims=True)), 0.0
    )
    text_total = jnp.sum(text_weights, axis=-1)
    cross_out = (
        jnp.einsum(
            "hqk,khd->hqd",
            text_weights.astype(jnp.bfloat16),
            text_value_heads,
            preferred_element_type=jnp.float32,
        )
        / text_total[..., None]
    )
    attended = (
        (self_out + cross_out)
        .transpose(1, 0, 2)
        .reshape(row_count, heads_local * HDIM)
        .astype(jnp.bfloat16)
    )
    mine = lax.all_to_all(attended, "uly", split_axis=0, concat_axis=1, tiled=True)
    features = mine.astype(jnp.float32)
    average = jnp.mean(features, axis=-1, keepdims=True)
    variance = jnp.mean((features - average) ** 2, axis=-1, keepdims=True)
    normed = ((features - average) * lax.rsqrt(variance + 1e-06) * mod_gain + mod_shift).astype(
        jnp.bfloat16
    )
    patches = (jnp.dot(normed, head_weight, preferred_element_type=jnp.float32) + head_bias).astype(
        jnp.bfloat16
    )
    patch_rows = mine.shape[0] // PCOL
    latent_rows = 2 * patch_rows
    latent_cols = 2 * PCOL
    own_block = (
        patches.reshape(patch_rows, PCOL, 2, 2, LAT)
        .transpose(0, 2, 1, 3, 4)
        .reshape(latent_rows, latent_cols, LAT)
    )
    wanted = lax.axis_index("blk") - 2 + jnp.arange(3, dtype=jnp.int32)
    selector = (tile_map[None, :] == wanted[:, None]).astype(jnp.bfloat16)
    gathered = lax.all_gather(own_block[None], "blk", axis=0, tiled=True)
    picked = jnp.einsum(
        "fb,bhwc->fhwc", selector, gathered, preferred_element_type=jnp.float32
    ).astype(jnp.bfloat16)
    rimmed = padded(picked, (("uly", 1),), 1)
    framed = jnp.pad(rimmed, ((0, 0), (0, 0), (1, 1), (0, 0)))
    stacked_taps = []
    for frame_tap in range(3):
        for row_tap in range(3):
            for col_tap in range(3):
                stacked_taps.append(
                    framed[
                        frame_tap, row_tap : row_tap + latent_rows, col_tap : col_tap + latent_cols
                    ]
                )
    stacked = jnp.concatenate(stacked_taps, axis=-1).reshape(latent_rows * latent_cols, 27 * LAT)
    pre = jnp.dot(stacked, conv_weight, preferred_element_type=jnp.float32) + conv_bias
    normalized = pre * lax.rsqrt(jnp.mean(pre * pre, axis=-1, keepdims=True) + 1e-06) * norm_gain
    return (
        jax.nn.silu(normalized)
        .astype(jnp.bfloat16)
        .reshape(1, latent_rows, latent_cols, conv_weight.shape[1])
    )


def solution(mesh):
    placed = (
        P(("clip", "blk", "uly"), None),
        P(("clip", "blk", "uly"), None),
        P(("clip", "blk", "uly"), None),
        P("clip", "uly"),
        P("clip", "uly"),
        P("clip"),
        P("clip"),
        P(),
        P(),
        P(),
        P(),
        P(),
        P(),
        P(),
    )
    return jax.shard_map(
        per_device,
        mesh=mesh,
        in_specs=placed,
        out_specs=P(("clip", "blk"), "uly", None, None),
        check_vma=False,
    )
```

profile of v0, /device:TPU:24, one launch (start us, length us, event | category | flops | bytes accessed | tf_op | source)
XLA Modules:
  0.0 1468.7 jit_solution(11414425900511841105)
XLA Ops:
  0.0 2.0 copy.307
  2.0 6.0 all-to-all-start
  8.0 1.9 copy.308
  9.9 11.9 all-to-all-done
  21.8 3.5 all-to-all-start.1
  26.1 12.4 all-to-all-done.1
  38.5 3.5 all-to-all-start.2
  47.6 1.6 copy-done.1
  49.7 5.5 all-to-all-done.2
  55.2 1.4 reshape.159
  58.1 3.0 fusion.23
  61.1 2.9 fusion.67
  64.0 1316.0 %while.16 = (s32[]{:T(128)}, f32[5,384]{1,0:T(8,128)S(1)}, f32[5,384]{1,0:T(8,128)S(1)}, f32[5,384,128]{2,1,0:T(8,128)S(1)}, bf16[2,384,640]{1,2,0:T(8,128)(2,1)}, /*index=5*/bf16[384,5,128]{2,0,1:T(8,128)(2,1)S(1)}, s32[]{:T(128)}) while((s32[]{:T(128)}, f32[5,384]{1,0:T(8,128)S(1)}, f32[5,384]{1,0:T(8,128)S(1)}, ...), condition=%wide.region_5.0_spmd, body=%wide.region_2.0_spmd.sunk | while | flops 383880960 | bytes 20275316 | solution.py:91
  64.0 9.2 collective-permute-start
  73.2 88.4 %collective-permute-done = bf16[2,384,640]{1,2,0:T(8,128)(2,1)S(1)} collective-permute-done((bf16[2,384,640]{1,2,0:T(8,128)(2,1)}, bf16[2,384,640]{1,2,0:T(8,128)(2,1)S(1)}, u32[]{:S(2)}, u32[]{:S(2)}) %collective-permute-start) | collective-permute-done | bytes 983072 | tf_op jit(solution)/shard_map/while/body/eval_jaxpr/ppermute | solution.py:15
  165.0 2.3 collective-permute-start
  167.3 84.2 %collective-permute-done = bf16[2,384,640]{1,2,0:T(8,128)(2,1)S(1)} collective-permute-done((bf16[2,384,640]{1,2,0:T(8,128)(2,1)}, bf16[2,384,640]{1,2,0:T(8,128)(2,1)S(1)}, u32[]{:S(2)}, u32[]{:S(2)}) %collective-permute-start) | collective-permute-done | bytes 983072 | tf_op jit(solution)/shard_map/while/body/eval_jaxpr/ppermute | solution.py:15
  254.8 1.9 collective-permute-start
  256.8 79.5 %collective-permute-done = bf16[2,384,640]{1,2,0:T(8,128)(2,1)S(1)} collective-permute-done((bf16[2,384,640]{1,2,0:T(8,128)(2,1)}, bf16[2,384,640]{1,2,0:T(8,128)(2,1)S(1)}, u32[]{:S(2)}, u32[]{:S(2)}) %collective-permute-start) | collective-permute-done | bytes 983072 | tf_op jit(solution)/shard_map/while/body/eval_jaxpr/ppermute | solution.py:15
  339.6 4.4 collective-permute-start
  344.0 77.8 %collective-permute-done = bf16[2,384,640]{1,2,0:T(8,128)(2,1)S(1)} collective-permute-done((bf16[2,384,640]{1,2,0:T(8,128)(2,1)}, bf16[2,384,640]{1,2,0:T(8,128)(2,1)S(1)}, u32[]{:S(2)}, u32[]{:S(2)}) %collective-permute-start) | collective-permute-done | bytes 983072 | tf_op jit(solution)/shard_map/while/body/eval_jaxpr/ppermute | solution.py:15
  425.1 3.8 collective-permute-start
  428.9 79.8 %collective-permute-done = bf16[2,384,640]{1,2,0:T(8,128)(2,1)S(1)} collective-permute-done((bf16[2,384,640]{1,2,0:T(8,128)(2,1)}, bf16[2,384,640]{1,2,0:T(8,128)(2,1)S(1)}, u32[]{:S(2)}, u32[]{:S(2)}) %collective-permute-start) | collective-permute-done | bytes 983072 | tf_op jit(solution)/shard_map/while/body/eval_jaxpr/ppermute | solution.py:15
  512.1 2.4 collective-permute-start
  514.5 83.6 %collective-permute-done = bf16[2,384,640]{1,2,0:T(8,128)(2,1)S(1)} collective-permute-done((bf16[2,384,640]{1,2,0:T(8,128)(2,1)}, bf16[2,384,640]{1,2,0:T(8,128)(2,1)S(1)}, u32[]{:S(2)}, u32[]{:S(2)}) %collective-permute-start) | collective-permute-done | bytes 983072 | tf_op jit(solution)/shard_map/while/body/eval_jaxpr/ppermute | solution.py:15
  601.5 1.9 collective-permute-start
  603.4 79.9 %collective-permute-done = bf16[2,384,640]{1,2,0:T(8,128)(2,1)S(1)} collective-permute-done((bf16[2,384,640]{1,2,0:T(8,128)(2,1)}, bf16[2,384,640]{1,2,0:T(8,128)(2,1)S(1)}, u32[]{:S(2)}, u32[]{:S(2)}) %collective-permute-start) | collective-permute-done | bytes 983072 | tf_op jit(solution)/shard_map/while/body/eval_jaxpr/ppermute | solution.py:15
  686.7 4.0 collective-permute-start
  690.7 77.9 %collective-permute-done = bf16[2,384,640]{1,2,0:T(8,128)(2,1)S(1)} collective-permute-done((bf16[2,384,640]{1,2,0:T(8,128)(2,1)}, bf16[2,384,640]{1,2,0:T(8,128)(2,1)S(1)}, u32[]{:S(2)}, u32[]{:S(2)}) %collective-permute-start) | collective-permute-done | bytes 983072 | tf_op jit(solution)/shard_map/while/body/eval_jaxpr/ppermute | solution.py:15
  772.0 3.7 collective-permute-start
  775.8 79.6 %collective-permute-done = bf16[2,384,640]{1,2,0:T(8,128)(2,1)S(1)} collective-permute-done((bf16[2,384,640]{1,2,0:T(8,128)(2,1)}, bf16[2,384,640]{1,2,0:T(8,128)(2,1)S(1)}, u32[]{:S(2)}, u32[]{:S(2)}) %collective-permute-start) | collective-permute-done | bytes 983072 | tf_op jit(solution)/shard_map/while/body/eval_jaxpr/ppermute | solution.py:15
  858.8 2.4 collective-permute-start
  861.2 83.6 %collective-permute-done = bf16[2,384,640]{1,2,0:T(8,128)(2,1)S(1)} collective-permute-done((bf16[2,384,640]{1,2,0:T(8,128)(2,1)}, bf16[2,384,640]{1,2,0:T(8,128)(2,1)S(1)}, u32[]{:S(2)}, u32[]{:S(2)}) %collective-permute-start) | collective-permute-done | bytes 983072 | tf_op jit(solution)/shard_map/while/body/eval_jaxpr/ppermute | solution.py:15
  948.2 1.9 collective-permute-start
  950.1 80.2 %collective-permute-done = bf16[2,384,640]{1,2,0:T(8,128)(2,1)S(1)} collective-permute-done((bf16[2,384,640]{1,2,0:T(8,128)(2,1)}, bf16[2,384,640]{1,2,0:T(8,128)(2,1)S(1)}, u32[]{:S(2)}, u32[]{:S(2)}) %collective-permute-start) | collective-permute-done | bytes 983072 | tf_op jit(solution)/shard_map/while/body/eval_jaxpr/ppermute | solution.py:15
  1033.7 3.7 collective-permute-start
  1037.4 78.3 %collective-permute-done = bf16[2,384,640]{1,2,0:T(8,128)(2,1)S(1)} collective-permute-done((bf16[2,384,640]{1,2,0:T(8,128)(2,1)}, bf16[2,384,640]{1,2,0:T(8,128)(2,1)S(1)}, u32[]{:S(2)}, u32[]{:S(2)}) %collective-permute-start) | collective-permute-done | bytes 983072 | tf_op jit(solution)/shard_map/while/body/eval_jaxpr/ppermute | solution.py:15
  1119.1 3.4 collective-permute-start
  1122.5 79.6 %collective-permute-done = bf16[2,384,640]{1,2,0:T(8,128)(2,1)S(1)} collective-permute-done((bf16[2,384,640]{1,2,0:T(8,128)(2,1)}, bf16[2,384,640]{1,2,0:T(8,128)(2,1)S(1)}, u32[]{:S(2)}, u32[]{:S(2)}) %collective-permute-start) | collective-permute-done | bytes 983072 | tf_op jit(solution)/shard_map/while/body/eval_jaxpr/ppermute | solution.py:15
  1205.5 2.3 collective-permute-start
  1207.8 83.7 %collective-permute-done = bf16[2,384,640]{1,2,0:T(8,128)(2,1)S(1)} collective-permute-done((bf16[2,384,640]{1,2,0:T(8,128)(2,1)}, bf16[2,384,640]{1,2,0:T(8,128)(2,1)S(1)}, u32[]{:S(2)}, u32[]{:S(2)}) %collective-permute-start) | collective-permute-done | bytes 983072 | tf_op jit(solution)/shard_map/while/body/eval_jaxpr/ppermute | solution.py:15
  1294.9 1.9 collective-permute-start
  1296.8 79.8 %collective-permute-done = bf16[2,384,640]{1,2,0:T(8,128)(2,1)S(1)} collective-permute-done((bf16[2,384,640]{1,2,0:T(8,128)(2,1)}, bf16[2,384,640]{1,2,0:T(8,128)(2,1)S(1)}, u32[]{:S(2)}, u32[]{:S(2)}) %collective-permute-start) | collective-permute-done | bytes 983072 | tf_op jit(solution)/shard_map/while/body/eval_jaxpr/ppermute | solution.py:15
  1380.0 2.3 fusion.35
  1384.0 3.8 all-to-all-start.3
  1387.8 14.0 all-to-all-done.3
  1403.2 51.2 %all_gather.3 = bf16[16,8,48,16]{2,3,1,0:T(8,128)(2,1)S(1)} all-gather(bf16[1,8,48,16]{2,3,1,0:T(8,128)(2,1)S(1)} %copy.243), channel_id=1, replica_groups=mesh['clip'=8,'blk'=16,'uly'=4] {'blk'}, dimensions={0}, use_global_device_ids=true | all-gather | bytes 208896 | tf_op jit(solution)/shard_map/all_gather | solution.py:140
  1457.6 4.2 collective-permute-done.2
  (266 shorter events, 70.4 us)
Async XLA Ops:
  0.0 1467.2 %copy-start = (bf16[432,384]{1,0:T(8,128)(2,1)S(1)}, bf16[432,384]{1,0:T(8,128)(2,1)}, u32[]{:S(2)}) copy-start(bf16[432,384]{1,0:T(8,128)(2,1)} %param.27) | copy-start | bytes 995332
  0.0 25.3 %copy-start.6 = (bf16[96,2560]{1,0:T(8,128)(2,1)S(1)}, bf16[96,2560]{1,0:T(8,128)(2,1)}, u32[]{:S(2)}) copy-start(bf16[96,2560]{1,0:T(8,128)(2,1)} %param.18) | copy-start | bytes 1474564
  0.0 42.0 %copy-start.2 = (bf16[512,640]{1,0:T(8,128)(2,1)S(1)}, bf16[512,640]{1,0:T(8,128)(2,1)}, u32[]{:S(2)}) copy-start(bf16[512,640]{1,0:T(8,128)(2,1)} %param.19) | copy-start | bytes 1966084
  2.0 41.8 %copy-start.3 = (bf16[512,640]{1,0:T(8,128)(2,1)S(1)}, bf16[512,640]{1,0:T(8,128)(2,1)}, u32[]{:S(2)}) copy-start(bf16[512,640]{1,0:T(8,128)(2,1)} %param.20) | copy-start | bytes 1966084
  2.0 19.8 %all-to-all-start = ((bf16[96,4,640]{2,0,1:T(8,128)(2,1)}), bf16[96,4,640]{2,0,1:T(8,128)(2,1)S(1)}, u32[]{:S(2)}, u32[]{:S(2)}) async-start(bf16[96,4,640]{2,0,1:T(8,128)(2,1)} %bitcast.162), calls=%async_computation | async-start | bytes 983040 | tf_op jit(solution)/shard_map/all_to_all | solution.py:72
  21.8 16.7 %all-to-all-start.1 = ((bf16[96,4,640]{2,0,1:T(8,128)(2,1)}), bf16[96,4,640]{2,0,1:T(8,128)(2,1)S(1)}, u32[]{:S(2)}, u32[]{:S(2)}) async-start(bf16[96,4,640]{2,0,1:T(8,128)(2,1)} %bitcast.163), calls=%async_computation.1 | async-start | bytes 983040 | tf_op jit(solution)/shard_map/all_to_all | solution.py:73
  38.5 16.7 %all-to-all-start.2 = ((bf16[96,4,640]{2,0,1:T(8,128)(2,1)}), bf16[96,4,640]{2,0,1:T(8,128)(2,1)S(1)}, u32[]{:S(2)}, u32[]{:S(2)}) async-start(bf16[96,4,640]{2,0,1:T(8,128)(2,1)} %bitcast.161), calls=%async_computation.2 | async-start | bytes 983040 | tf_op jit(solution)/shard_map/all_to_all | solution.py:74
  47.6 1.6 copy-start.1
  58.1 3.0 copy-start.5
  64.0 1316.0 %copy-start.4 = (bf16[512,640]{0,1:T(8,128)(2,1)S(1)}, bf16[512,640]{0,1:T(8,128)(2,1)}, u32[]{:S(2)}) copy-start(bf16[512,640]{0,1:T(8,128)(2,1)} %copy.237) | copy-start | bytes 1966084
  64.0 97.7 %collective-permute-start = (bf16[2,384,640]{1,2,0:T(8,128)(2,1)}, bf16[2,384,640]{1,2,0:T(8,128)(2,1)S(1)}, u32[]{:S(2)}, u32[]{:S(2)}) collective-permute-start(bf16[2,384,640]{1,2,0:T(8,128)(2,1)} %get-tuple-element.190), channel_id=1, source_target_pairs={{60,0},{0,4},{4,8},{8,12},{12,16},{16,20},{20,24},{24,28},{28,32},... | collective-permute-start | bytes 2949128 | tf_op jit(solution)/shard_map/while/body/eval_jaxpr/ppermute | solution.py:15
  165.0 86.4 %collective-permute-start = (bf16[2,384,640]{1,2,0:T(8,128)(2,1)}, bf16[2,384,640]{1,2,0:T(8,128)(2,1)S(1)}, u32[]{:S(2)}, u32[]{:S(2)}) collective-permute-start(bf16[2,384,640]{1,2,0:T(8,128)(2,1)} %get-tuple-element.190), channel_id=1, source_target_pairs={{60,0},{0,4},{4,8},{8,12},{12,16},{16,20},{20,24},{24,28},{28,32},... | collective-permute-start | bytes 2949128 | tf_op jit(solution)/shard_map/while/body/eval_jaxpr/ppermute | solution.py:15
  254.8 81.4 %collective-permute-start = (bf16[2,384,640]{1,2,0:T(8,128)(2,1)}, bf16[2,384,640]{1,2,0:T(8,128)(2,1)S(1)}, u32[]{:S(2)}, u32[]{:S(2)}) collective-permute-start(bf16[2,384,640]{1,2,0:T(8,128)(2,1)} %get-tuple-element.190), channel_id=1, source_target_pairs={{60,0},{0,4},{4,8},{8,12},{12,16},{16,20},{20,24},{24,28},{28,32},... | collective-permute-start | bytes 2949128 | tf_op jit(solution)/shard_map/while/body/eval_jaxpr/ppermute | solution.py:15
  339.6 82.1 %collective-permute-start = (bf16[2,384,640]{1,2,0:T(8,128)(2,1)}, bf16[2,384,640]{1,2,0:T(8,128)(2,1)S(1)}, u32[]{:S(2)}, u32[]{:S(2)}) collective-permute-start(bf16[2,384,640]{1,2,0:T(8,128)(2,1)} %get-tuple-element.190), channel_id=1, source_target_pairs={{60,0},{0,4},{4,8},{8,12},{12,16},{16,20},{20,24},{24,28},{28,32},... | collective-permute-start | bytes 2949128 | tf_op jit(solution)/shard_map/while/body/eval_jaxpr/ppermute | solution.py:15
  425.1 83.6 %collective-permute-start = (bf16[2,384,640]{1,2,0:T(8,128)(2,1)}, bf16[2,384,640]{1,2,0:T(8,128)(2,1)S(1)}, u32[]{:S(2)}, u32[]{:S(2)}) collective-permute-start(bf16[2,384,640]{1,2,0:T(8,128)(2,1)} %get-tuple-element.190), channel_id=1, source_target_pairs={{60,0},{0,4},{4,8},{8,12},{12,16},{16,20},{20,24},{24,28},{28,32},... | collective-permute-start | bytes 2949128 | tf_op jit(solution)/shard_map/while/body/eval_jaxpr/ppermute | solution.py:15
  512.1 86.0 %collective-permute-start = (bf16[2,384,640]{1,2,0:T(8,128)(2,1)}, bf16[2,384,640]{1,2,0:T(8,128)(2,1)S(1)}, u32[]{:S(2)}, u32[]{:S(2)}) collective-permute-start(bf16[2,384,640]{1,2,0:T(8,128)(2,1)} %get-tuple-element.190), channel_id=1, source_target_pairs={{60,0},{0,4},{4,8},{8,12},{12,16},{16,20},{20,24},{24,28},{28,32},... | collective-permute-start | bytes 2949128 | tf_op jit(solution)/shard_map/while/body/eval_jaxpr/ppermute | solution.py:15
  601.5 81.8 %collective-permute-start = (bf16[2,384,640]{1,2,0:T(8,128)(2,1)}, bf16[2,384,640]{1,2,0:T(8,128)(2,1)S(1)}, u32[]{:S(2)}, u32[]{:S(2)}) collective-permute-start(bf16[2,384,640]{1,2,0:T(8,128)(2,1)} %get-tuple-element.190), channel_id=1, source_target_pairs={{60,0},{0,4},{4,8},{8,12},{12,16},{16,20},{20,24},{24,28},{28,32},... | collective-permute-start | bytes 2949128 | tf_op jit(solution)/shard_map/while/body/eval_jaxpr/ppermute | solution.py:15
  686.7 82.0 %collective-permute-start = (bf16[2,384,640]{1,2,0:T(8,128)(2,1)}, bf16[2,384,640]{1,2,0:T(8,128)(2,1)S(1)}, u32[]{:S(2)}, u32[]{:S(2)}) collective-permute-start(bf16[2,384,640]{1,2,0:T(8,128)(2,1)} %get-tuple-element.190), channel_id=1, source_target_pairs={{60,0},{0,4},{4,8},{8,12},{12,16},{16,20},{20,24},{24,28},{28,32},... | collective-permute-start | bytes 2949128 | tf_op jit(solution)/shard_map/while/body/eval_jaxpr/ppermute | solution.py:15
  772.0 83.4 %collective-permute-start = (bf16[2,384,640]{1,2,0:T(8,128)(2,1)}, bf16[2,384,640]{1,2,0:T(8,128)(2,1)S(1)}, u32[]{:S(2)}, u32[]{:S(2)}) collective-permute-start(bf16[2,384,640]{1,2,0:T(8,128)(2,1)} %get-tuple-element.190), channel_id=1, source_target_pairs={{60,0},{0,4},{4,8},{8,12},{12,16},{16,20},{20,24},{24,28},{28,32},... | collective-permute-start | bytes 2949128 | tf_op jit(solution)/shard_map/while/body/eval_jaxpr/ppermute | solution.py:15
  858.8 86.0 %collective-permute-start = (bf16[2,384,640]{1,2,0:T(8,128)(2,1)}, bf16[2,384,640]{1,2,0:T(8,128)(2,1)S(1)}, u32[]{:S(2)}, u32[]{:S(2)}) collective-permute-start(bf16[2,384,640]{1,2,0:T(8,128)(2,1)} %get-tuple-element.190), channel_id=1, source_target_pairs={{60,0},{0,4},{4,8},{8,12},{12,16},{16,20},{20,24},{24,28},{28,32},... | collective-permute-start | bytes 2949128 | tf_op jit(solution)/shard_map/while/body/eval_jaxpr/ppermute | solution.py:15
  948.2 82.2 %collective-permute-start = (bf16[2,384,640]{1,2,0:T(8,128)(2,1)}, bf16[2,384,640]{1,2,0:T(8,128)(2,1)S(1)}, u32[]{:S(2)}, u32[]{:S(2)}) collective-permute-start(bf16[2,384,640]{1,2,0:T(8,128)(2,1)} %get-tuple-element.190), channel_id=1, source_target_pairs={{60,0},{0,4},{4,8},{8,12},{12,16},{16,20},{20,24},{24,28},{28,32},... | collective-permute-start | bytes 2949128 | tf_op jit(solution)/shard_map/while/body/eval_jaxpr/ppermute | solution.py:15
  1033.7 82.0 %collective-permute-start = (bf16[2,384,640]{1,2,0:T(8,128)(2,1)}, bf16[2,384,640]{1,2,0:T(8,128)(2,1)S(1)}, u32[]{:S(2)}, u32[]{:S(2)}) collective-permute-start(bf16[2,384,640]{1,2,0:T(8,128)(2,1)} %get-tuple-element.190), channel_id=1, source_target_pairs={{60,0},{0,4},{4,8},{8,12},{12,16},{16,20},{20,24},{24,28},{28,32},... | collective-permute-start | bytes 2949128 | tf_op jit(solution)/shard_map/while/body/eval_jaxpr/ppermute | solution.py:15
  1119.1 83.0 %collective-permute-start = (bf16[2,384,640]{1,2,0:T(8,128)(2,1)}, bf16[2,384,640]{1,2,0:T(8,128)(2,1)S(1)}, u32[]{:S(2)}, u32[]{:S(2)}) collective-permute-start(bf16[2,384,640]{1,2,0:T(8,128)(2,1)} %get-tuple-element.190), channel_id=1, source_target_pairs={{60,0},{0,4},{4,8},{8,12},{12,16},{16,20},{20,24},{24,28},{28,32},... | collective-permute-start | bytes 2949128 | tf_op jit(solution)/shard_map/while/body/eval_jaxpr/ppermute | solution.py:15
  1205.5 86.0 %collective-permute-start = (bf16[2,384,640]{1,2,0:T(8,128)(2,1)}, bf16[2,384,640]{1,2,0:T(8,128)(2,1)S(1)}, u32[]{:S(2)}, u32[]{:S(2)}) collective-permute-start(bf16[2,384,640]{1,2,0:T(8,128)(2,1)} %get-tuple-element.190), channel_id=1, source_target_pairs={{60,0},{0,4},{4,8},{8,12},{12,16},{16,20},{20,24},{24,28},{28,32},... | collective-permute-start | bytes 2949128 | tf_op jit(solution)/shard_map/while/body/eval_jaxpr/ppermute | solution.py:15
  1294.9 81.7 %collective-permute-start = (bf16[2,384,640]{1,2,0:T(8,128)(2,1)}, bf16[2,384,640]{1,2,0:T(8,128)(2,1)S(1)}, u32[]{:S(2)}, u32[]{:S(2)}) collective-permute-start(bf16[2,384,640]{1,2,0:T(8,128)(2,1)} %get-tuple-element.190), channel_id=1, source_target_pairs={{60,0},{0,4},{4,8},{8,12},{12,16},{16,20},{20,24},{24,28},{28,32},... | collective-permute-start | bytes 2949128 | tf_op jit(solution)/shard_map/while/body/eval_jaxpr/ppermute | solution.py:15
  1384.0 18.5 %copy-start.9 = (bf16[2560,64]{0,1:T(8,128)(2,1)S(1)}, bf16[2560,64]{0,1:T(8,128)(2,1)}, u32[]{:S(2)}) copy-start(bf16[2560,64]{0,1:T(8,128)(2,1)} %param.25) | copy-start | bytes 983044
  1384.0 18.5 %copy-start.10 = (f32[2560]{0:T(1024)S(1)}, f32[2560]{0:T(1024)}, u32[]{:S(2)}) copy-start(f32[2560]{0:T(1024)} %param.24) | copy-start | bytes 30724
  1384.0 18.5 %copy-start.11 = (f32[2560]{0:T(1024)S(1)}, f32[2560]{0:T(1024)}, u32[]{:S(2)}) copy-start(f32[2560]{0:T(1024)} %param.23) | copy-start | bytes 30724
  1384.0 18.5 %copy-start.13 = (f32[64]{0:T(128)S(1)}, f32[64]{0:T(128)}, u32[]{:S(2)}) copy-start(f32[64]{0:T(128)} %param.26) | copy-start | bytes 772
  1384.0 17.8 %all-to-all-start.3 = ((bf16[4,96,640]{2,1,0:T(8,128)(2,1)}), bf16[4,96,640]{2,1,0:T(8,128)(2,1)S(1)}, u32[]{:S(2)}, u32[]{:S(2)}) async-start(bf16[4,96,640]{2,1,0:T(8,128)(2,1)} %reshape.160), calls=%async_computation.3 | async-start | bytes 983040 | tf_op jit(solution)/shard_map/all_to_all | solution.py:120
  1402.3 52.1 %copy-start.8 = (s32[16]{0:T(128)S(1)}, s32[16]{0:T(128)}, u32[]{:S(2)}) copy-start(s32[16]{0:T(128)} %param.22) | copy-start | bytes 196
  1454.8 2.7 collective-permute-start.1
  1456.1 5.6 collective-permute-start.2
  1462.6 4.7 copy-start.12
  1463.6 4.2 copy-start.7
where the time goes:
time: 1470 us
  waiting for transfers between devices  1260 us (86%)
  starting transfers between devices  68.6 us (5%)
  blocking collectives  51.2 us (3%)
  matrix products  36.3 us (2%)
  local copies, waits for them, and re-layouts  35.9 us (2%)
    ppermute x15, waiting for transfers between devices, shifted(): return lax.ppermute(block, axis, route)  1220 us
    all_gather x1, blocking collectives, per_device(): gathered = lax.all_gather(own_block[None], 'blk', axis=0, tiled=True)  51.2 us
    ppermute x15, starting transfers between devices, shifted(): return lax.ppermute(block, axis, route)  49.3 us
  transfers between devices with their start and end apart: 21, of which 21 were waited for; matrix products, arithmetic and copies ran while one was open for 1% of the time, Pallas kernels for 0%

commit v1 on v0

v1 whole, which is shorter than its diff:
```python
import functools

import jax
import jax.numpy as jnp
from jax import lax
from jax.experimental import pallas as pl
from jax.experimental.pallas import tpu as pltpu
from jax.sharding import Mesh, PartitionSpec as P

PCOL = 24
HDIM = 128
TXT = 512
LAT = 16
ROWS = 96
NZ = 16
C_OUT = 384
LOG2E = 1.4426950408889634
SCALE2 = HDIM ** (-0.5) * LOG2E
Z = ("zh", "zl")
F32 = jnp.float32
BF = jnp.bfloat16
VMEM_LIMIT = 50 * 1024 * 1024


def params():
    return pltpu.CompilerParams(vmem_limit_bytes=VMEM_LIMIT)


def vmem():
    return pl.BlockSpec(memory_space=pltpu.VMEM)


def smem():
    return pl.BlockSpec(memory_space=pltpu.SMEM)


def pack_kernel(q_ref, k_ref, v_ref, kvm_ref, kve_ref, q_out):
    for zl in range(4):
        last = (5 * zl + 4) * HDIM
        queries_last = q_ref[:, last : last + HDIM].astype(F32)
        for zh in range(4):
            z = zh * 4 + zl
            lo = (5 * zl + zh) * HDIM
            kvm_ref[z, 0:ROWS, :] = k_ref[:, lo : lo + HDIM]
            kvm_ref[z, ROWS : 2 * ROWS, :] = v_ref[:, lo : lo + HDIM]
            kve_ref[z, 0:ROWS, :] = k_ref[:, last : last + HDIM]
            kve_ref[z, ROWS : 2 * ROWS, :] = v_ref[:, last : last + HDIM]
            q_out[z, 0:ROWS, :] = q_ref[:, lo : lo + HDIM]
            part = queries_last[24 * zh : 24 * zh + 24]
            q_out[z, ROWS : ROWS + 32, :] = jnp.concatenate(
                [part, jnp.zeros((8, HDIM), F32)], axis=0
            ).astype(BF)


def pack(queries, keys, values):
    return pl.pallas_call(
        pack_kernel,
        out_shape=(
            jax.ShapeDtypeStruct((NZ, 2 * ROWS, HDIM), BF),
            jax.ShapeDtypeStruct((NZ, 2 * ROWS, HDIM), BF),
            jax.ShapeDtypeStruct((NZ, ROWS + 32, HDIM), BF),
        ),
        in_specs=[vmem()] * 3,
        out_specs=(vmem(),) * 3,
        compiler_params=params(),
    )(queries, keys, values)


def dot_t(a, b):
    return lax.dot_general(a, b, (((1,), (1,)), ((), ())), preferred_element_type=F32)


def attend(query, pieces, text_key, text_value, text_len, scores_ref):
    rows = query.shape[0]
    top = None
    at = 0
    spans = []
    for ref, lo, hi in pieces:
        key = ref[lo:hi, 0:ROWS, :].reshape((hi - lo) * ROWS, HDIM)
        scores = dot_t(query, key)
        width = scores.shape[1]
        scores_ref[:, at : at + width] = scores
        for col in range(0, width, HDIM):
            part = scores[:, col : col + HDIM]
            top = part if top is None else jnp.maximum(top, part)
        spans.append((at, width))
        at += width
    peak = jnp.max(top, axis=-1, keepdims=True) * SCALE2
    total = jnp.zeros((rows, 2 * HDIM), F32)
    for (ref, lo, hi), (start, width) in zip(pieces, spans):
        weights = jnp.exp2(scores_ref[:, start : start + width] * SCALE2 - peak).astype(BF)
        value = ref[lo:hi, ROWS : 2 * ROWS, :].reshape(width, HDIM)
        wide = jnp.concatenate([value, jnp.ones((width, HDIM), BF)], axis=1)
        total = total + jnp.dot(weights, wide, preferred_element_type=F32)
    self_out = total[:, :HDIM] / total[:, HDIM:]
    text_scores = dot_t(query, text_key) * SCALE2
    usable = lax.broadcasted_iota(jnp.int32, text_scores.shape, 1) < text_len
    text_scores = jnp.where(usable, text_scores, -1e30)
    text_peak = jnp.max(text_scores, axis=-1, keepdims=True)
    text_weights = jnp.where(usable, jnp.exp2(text_scores - text_peak), 0.0).astype(BF)
    wide = jnp.concatenate([text_value, jnp.ones((TXT, HDIM), BF)], axis=1)
    text_total = jnp.dot(text_weights, wide, preferred_element_type=F32)
    return self_out + text_total[:, :HDIM] / text_total[:, HDIM:]


def pieces_of(refs):
    pieces = []
    for ref in refs:
        count = ref.shape[0]
        for lo in range(0, count, 8):
            pieces.append((ref, lo, lo + 8))
    return pieces


def main_kernel(info, q_ref, k0, k1, k2, k3, k4, tk_ref, tv_ref, out_ref, scores_ref):
    query = q_ref[:, 0:ROWS, :].reshape(4 * ROWS, HDIM)
    column = pl.ds(pl.multiple_of(info[0] * HDIM, HDIM), HDIM)
    result = attend(
        query,
        pieces_of((k0, k1, k2, k3, k4)),
        tk_ref[:, column],
        tv_ref[:, column],
        info[1],
        scores_ref,
    )
    out_ref[...] = result.astype(BF).reshape(4, ROWS, HDIM)


def extra_kernel(info, q_ref, k0, k1, k2, k3, k4, tk_ref, tv_ref, main_ref, out_ref, scores_ref):
    query = q_ref[:, ROWS : ROWS + 32, :].astype(F32)[:, :24].reshape(NZ * 24, HDIM).astype(BF)
    column = slice(4 * HDIM, 5 * HDIM)
    result = attend(
        query,
        pieces_of((k0, k1, k2, k3, k4)),
        tk_ref[:, column],
        tv_ref[:, column],
        info[1],
        scores_ref,
    )
    padded = jnp.concatenate(
        [result.reshape(NZ, 24, HDIM), jnp.zeros((NZ, 8, HDIM), F32)], axis=1
    )
    out_ref[:, 0:ROWS, :] = main_ref[...]
    out_ref[:, ROWS : ROWS + 32, :] = padded.astype(BF)


KEYS = 6144


def cost(rows):
    return pl.CostEstimate(
        flops=rows * (KEYS + TXT) * HDIM * 8,
        bytes_accessed=2 * KEYS * HDIM * 2,
        transcendentals=rows * (KEYS + TXT),
    )


def main_attention(info, q_all, kv, text_keys, text_values):
    whole = lambda a: pl.BlockSpec(a.shape, lambda i, n=a.ndim: (0,) * n)
    return pl.pallas_call(
        main_kernel,
        grid=(4,),
        out_shape=jax.ShapeDtypeStruct((NZ, ROWS, HDIM), BF),
        in_specs=[smem(), pl.BlockSpec((4, ROWS + 32, HDIM), lambda i: (i, 0, 0))]
        + [whole(a) for a in kv]
        + [whole(text_keys), whole(text_values)],
        out_specs=pl.BlockSpec((4, ROWS, HDIM), lambda i: (i, 0, 0)),
        scratch_shapes=[pltpu.VMEM((4 * ROWS, KEYS), F32)],
        compiler_params=params(),
        cost_estimate=cost(1536),
    )(info, q_all, *kv, text_keys, text_values)


def extra_attention(info, q_all, kv, text_keys, text_values, main_out):
    return pl.pallas_call(
        extra_kernel,
        out_shape=jax.ShapeDtypeStruct((NZ, ROWS + 32, HDIM), BF),
        in_specs=[smem()] + [vmem()] * 9,
        out_specs=vmem(),
        scratch_shapes=[pltpu.VMEM((NZ * 24, KEYS), F32)],
        compiler_params=params(),
        cost_estimate=cost(384),
    )(info, q_all, *kv, text_keys, text_values, main_out)


def head_kernel(back_ref, gain_ref, shift_ref, weight_ref, bias_ref, out_ref):
    blocks = []
    for head in range(20):
        zl, zh = head // 5, head % 5
        if zh < 4:
            blocks.append(back_ref[zh * 4 + zl, 0:ROWS, :].astype(F32))
        else:
            blocks.append(
                jnp.concatenate(
                    [
                        back_ref[part * 4 + zl, ROWS : ROWS + 32, :].astype(F32)[:24]
                        for part in range(4)
                    ],
                    axis=0,
                )
            )
    count = 20 * HDIM
    average = jnp.sum(sum(blocks), axis=-1, keepdims=True) / count
    blocks = [block - average for block in blocks]
    variance = jnp.sum(sum(block * block for block in blocks), axis=-1, keepdims=True) / count
    scale = lax.rsqrt(variance + 1e-06)
    patches = jnp.zeros((ROWS, 64), F32)
    for head in range(20):
        span = slice(head * HDIM, (head + 1) * HDIM)
        normed = (blocks[head] * scale * gain_ref[:, span] + shift_ref[:, span]).astype(BF)
        patches = patches + jnp.dot(normed, weight_ref[span, :], preferred_element_type=F32)
    out_ref[...] = (patches + bias_ref[...]).astype(BF)


def head(back, mod_gain, mod_shift, head_weight, head_bias):
    return pl.pallas_call(
        head_kernel,
        out_shape=jax.ShapeDtypeStruct((ROWS, 64), BF),
        in_specs=[vmem()] * 5,
        out_specs=vmem(),
        compiler_params=params(),
    )(back, mod_gain[None], mod_shift[None], head_weight, head_bias[None])


def conv_kernel(
    info, tile_map, g0, g1, g2, g3, weight_ref, bias_ref, gain_ref, out_ref, wide_ref, slab_ref, pix_ref
):
    wide_ref[...] = jnp.zeros_like(wide_ref)
    for a in range(3):
        for di in (-1, 0, 1):
            for dj in (-1, 0, 1):
                for p in range(2):
                    for q in range(2):
                        row = ((dj + 1) * 4 + p * 2 + q) * LAT
                        for pp in range(2):
                            for qq in range(2):
                                r = 2 * di + p - pp + 1
                                s = 2 * dj + q - qq + 1
                                if 0 <= r < 3 and 0 <= s < 3:
                                    tap = ((a * 3 + r) * 3 + s) * LAT
                                    col = (pp * 2 + qq) * C_OUT
                                    wide_ref[
                                        a * 3 + di + 1, row : row + LAT, col : col + C_OUT
                                    ] = weight_ref[tap : tap + LAT, :]
    for d, ref in enumerate((g0, g1, g2, g3)):
        slab_ref[4 * d : 4 * d + 4] = ref[...]
    x, zh = info[2], info[0]
    pre = jnp.zeros((ROWS, 4 * C_OUT), F32)
    column = lax.broadcasted_iota(jnp.int32, (6 * PCOL, 64), 0) % PCOL
    for a in range(3):
        wanted = 4 * x + zh - 2 + a
        source = jnp.int32(0)
        for b in range(16):
            source = jnp.where(tile_map[b] == wanted, b, source)
        place = lax.rem(x - source // 4 + 4, 4) * 4 + lax.rem(zh - lax.rem(source, 4) + 4, 4)
        slab = slab_ref[place].astype(F32)
        slab = jnp.where(wanted >= 0, slab, 0.0)
        zero = jnp.zeros((8, 64), F32)
        tall = jnp.concatenate([zero, slab, zero], axis=0)
        left = jnp.where(column == 0, 0.0, tall[7 : 7 + 6 * PCOL])
        right = jnp.where(column == PCOL - 1, 0.0, tall[9 : 9 + 6 * PCOL])
        joined = jnp.concatenate([left, slab, right], axis=1)
        for di in range(3):
            part = joined[di * PCOL : di * PCOL + ROWS].astype(BF)
            pre = pre + jnp.dot(part, wide_ref[a * 3 + di], preferred_element_type=F32)
    for pp in range(2):
        for qq in range(2):
            at = (pp * 2 + qq) * C_OUT
            value = pre[:, at : at + C_OUT] + bias_ref[...]
            mean = jnp.mean(value * value, axis=-1, keepdims=True)
            value = value * lax.rsqrt(mean + 1e-06) * gain_ref[...]
            value = value / (1.0 + jnp.exp(-value))
            for i in range(4):
                for part in range(3):
                    pix_ref[part, 2 * i + pp, pl.ds(qq, PCOL, 2), :] = value[
                        i * PCOL : (i + 1) * PCOL, part * HDIM : (part + 1) * HDIM
                    ]
    for part in range(3):
        out_ref[:, :, part * HDIM : (part + 1) * HDIM] = pix_ref[part].astype(BF)


def conv(info, tile_map, gathered, conv_weight, conv_bias, norm_gain):
    return pl.pallas_call(
        conv_kernel,
        out_shape=jax.ShapeDtypeStruct((8, 48, C_OUT), BF),
        in_specs=[smem(), smem()] + [vmem()] * 7,
        out_specs=vmem(),
        scratch_shapes=[
            pltpu.VMEM((9, 192, 4 * C_OUT), BF),
            pltpu.VMEM((16, 6 * PCOL, 64), BF),
            pltpu.VMEM((3, 8, 48, HDIM), F32),
        ],
        compiler_params=params(),
    )(info, tile_map, *gathered, conv_weight, conv_bias[None], norm_gain[None])


def shift(block, axis, distance):
    return lax.ppermute(block, axis, [(i, (i + distance) % 4) for i in range(4)])


def around_x(block):
    right = shift(block, "x", 1)
    left = shift(block, "x", -1)
    half = block.shape[0] // 2
    return (block, right, left, shift(right[:half], "x", 1), shift(left[half:], "x", -1))


def per_device(
    queries,
    keys,
    values,
    text_keys,
    text_values,
    text_len,
    tile_map,
    mod_gain,
    mod_shift,
    head_weight,
    head_bias,
    conv_weight,
    conv_bias,
    norm_gain,
):
    exchange = functools.partial(
        lax.all_to_all, axis_name=Z, split_axis=0, concat_axis=0, tiled=True
    )
    x, zh = lax.axis_index("x"), lax.axis_index("zh")
    info = jnp.stack([zh, text_len[0], x]).astype(jnp.int32)
    main_send, extra_send, q_send = pack(queries, keys, values)
    main_kv = around_x(exchange(main_send))
    extra_kv = around_x(exchange(extra_send))
    q_all = exchange(q_send)
    main_out = main_attention(info, q_all, main_kv, text_keys, text_values)
    out = extra_attention(info, q_all, extra_kv, text_keys, text_values, main_out)
    back = exchange(out)
    patches = head(back, mod_gain, mod_shift, head_weight, head_bias)
    above = lax.ppermute(patches[ROWS - PCOL :], "zl", [(i, i + 1) for i in range(3)])
    below = lax.ppermute(patches[:PCOL], "zl", [(i + 1, i) for i in range(3)])
    slab = jnp.concatenate([above, patches, below], axis=0)
    line = jnp.stack([slab] + [shift(slab, "zh", d) for d in (1, 2, 3)])
    gathered = [line] + [shift(line, "x", d) for d in (1, 2, 3)]
    out = conv(info, tile_map, gathered, conv_weight, conv_bias, norm_gain)
    return out[None]


def solution(mesh):
    inner = Mesh(mesh.devices.reshape(8, 4, 4, 4), ("clip", "x", "zh", "zl"))
    tokens = P(("clip", "x", "zh", "zl"), None)
    placed = (
        tokens,
        tokens,
        tokens,
        P("clip", "zl"),
        P("clip", "zl"),
        P("clip"),
        P("clip"),
    ) + (P(),) * 7
    return jax.shard_map(
        per_device,
        mesh=inner,
        in_specs=placed,
        out_specs=P(("clip", "x", "zh"), "zl", None, None),
        check_vma=False,
    )
```

time: 1470 us -> 290 us (0.20)
  waiting for transfers between devices: 1260 us -> 58.1 us
  blocking collectives: 51.2 us -> 103 us
  Pallas kernels: 0 us -> 40.7 us
  matrix products: 36.3 us -> 0 us
  local copies, waits for them, and re-layouts: 35.9 us -> 9.79 us
    ppermute x17 -> x16, waiting for transfers between devices: 1220 us -> 33.9 us  [the longest x14 28.2 us: shift(): lax.ppermute(block, axis, [(i, (i + distance) % 4) for i in range(4)])]
    all_to_all x0 -> x2, blocking collectives: none -> 103 us  [the longest x1 56.3 us: per_device(): main_kv = around_x(exchange(main_send))]
    all_gather x1 -> x0, blocking collectives: 51.2 us -> none  [per_device(): gathered = lax.all_gather(own_block[None], 'blk', axis=0, tiled=True)]
    pallas_call x0 -> x5, Pallas kernels: none -> 40.7 us  [the longest x1 27.3 us: main_attention(): pl.pallas_call(main_kernel, grid=(4,), out_shape=jax.ShapeDtypeStruct((NZ...]
    dot_general x36 -> x0, matrix products: 33.4 us -> none  [the longest x16 20.1 us: absorb(): jnp.einsum('hqk,khd->hqd', weights.astype(jnp.bfloat16), value_heads, pre...]
    all_to_all x4 -> x2, waiting for transfers between devices: 43.9 us -> 24.2 us  [the longest x1 24.2 us: per_device(): back = exchange(out)]
    while x32 -> x0, local copies, waits for them, and re-layouts: 16 us -> none
    ppermute x17 -> x16, starting transfers between devices: 51.9 us -> 59 us  [the longest x14 55.8 us: shift(): lax.ppermute(block, axis, [(i, (i + distance) % 4) for i in range(4)])]
  transfers between devices with their start and end apart: 21 -> 18, of which waited for: 21 -> 8; matrix products, arithmetic and copies ran while one was open for 1% -> 2% of each run, Pallas kernels for 0% -> 9%
where the time goes in v1:
time: 290 us; the launch traced here: 289 us
  blocking collectives  103 us (36%)
  starting transfers between devices  76.6 us (26%)
  waiting for transfers between devices  58.1 us (20%)
  Pallas kernels  40.7 us (14%)
  local copies, waits for them, and re-layouts  9.79 us (3%)
    all_to_all x1, blocking collectives, per_device(): main_kv = around_x(exchange(main_send))  56.3 us
    ppermute x14, starting transfers between devices, shift(): lax.ppermute(block, axis, [(i, (i + distance) % 4) for i in range(4)])  55.8 us
    all_to_all x1, blocking collectives, per_device(): extra_kv = around_x(exchange(extra_send))  46.5 us
    ppermute x14, waiting for transfers between devices, shift(): lax.ppermute(block, axis, [(i, (i + distance) % 4) for i in range(4)])  28.2 us
    pallas_call x1, Pallas kernels, main_attention(): pl.pallas_call(main_kernel, grid=(4,), out_shape=jax.ShapeDtypeStruct((NZ...  27.3 us
    all_to_all x1, waiting for transfers between devices, per_device(): back = exchange(out)  24.2 us
    all_to_all x1, starting transfers between devices, per_device(): back = exchange(out)  12.1 us
    pallas_call x1, Pallas kernels, extra_attention(): pl.pallas_call(extra_kernel, out_shape=jax.ShapeDtypeStruct((NZ, ROWS + 3...  9.08 us
  transfers between devices with their start and end apart: 18, of which 8 were waited for; matrix products, arithmetic and copies ran while one was open for 2% of the time, Pallas kernels for 9%

profile of v1, /device:TPU:24, one launch (start us, length us, event | category | flops | bytes accessed | tf_op | source)
XLA Modules:
  0.0 289.2 jit_solution(15856520391368283554)
XLA Ops:
  0.0 1.0 copy-done
  1.0 1.0 copy-done.1
  2.1 1.0 copy-done.2
  3.1 1.1 shard_map.136
  4.2 56.3 %all_to_all.20.k0 = bf16[16,192,128]{2,1,0:T(8,128)(2,1)S(1)} all-to-all(bf16[16,192,128]{2,1,0:T(8,128)(2,1)S(1)} %get-tuple-element.10), channel_id=1, replica_groups=mesh['clip'=8,'x'=4,'zh'=4,'zl'=4] {'zh','zl'}, dimensions={0} | all-to-all | bytes 1572864 | tf_op jit(solution)/shard_map/all_to_all | solution.py:330
  60.5 46.5 %all_to_all.21.k0 = bf16[16,192,128]{2,1,0:T(8,128)(2,1)} all-to-all(bf16[16,192,128]{2,1,0:T(8,128)(2,1)S(1)} %get-tuple-element.9), channel_id=1, replica_groups=mesh['clip'=8,'x'=4,'zh'=4,'zl'=4] {'zh','zl'}, dimensions={0} | all-to-all | bytes 1572864 | tf_op jit(solution)/shard_map/all_to_all | solution.py:331
  107.0 5.4 %all-to-all-start = ((bf16[16,128,128]{2,1,0:T(8,128)(2,1)}), bf16[16,128,128]{2,1,0:T(8,128)(2,1)S(1)}, u32[]{:S(2)}, u32[]{:S(2)}) async-start(bf16[16,128,128]{2,1,0:T(8,128)(2,1)} %get-tuple-element.8), calls=%async_computation | async-start | bytes 1048576 | tf_op jit(solution)/shard_map/all_to_all | solution.py:332
  112.5 3.4 %collective-permute-start.4 = (bf16[16,192,128]{2,1,0:T(8,128)(2,1)S(1)}, bf16[16,192,128]{2,1,0:T(8,128)(2,1)S(1)}, u32[]{:S(2)}, u32[]{:S(2)}) collective-permute-start(bf16[16,192,128]{2,1,0:T(8,128)(2,1)S(1)} %all_to_all.20.k0), channel_id=1, source_target_pairs={{0,16},{16,32},{32,48},{48,0},{1,17},{17,33},{33,49},{49,1},{2,18}... | collective-permute-start | bytes 2359304 | tf_op jit(solution)/shard_map/ppermute | solution.py:298
  115.9 3.7 %collective-permute-start.5 = (bf16[16,192,128]{2,1,0:T(8,128)(2,1)S(1)}, bf16[16,192,128]{2,1,0:T(8,128)(2,1)S(1)}, u32[]{:S(2)}, u32[]{:S(2)}) collective-permute-start(bf16[16,192,128]{2,1,0:T(8,128)(2,1)S(1)} %all_to_all.20.k0), channel_id=1, source_target_pairs={{0,48},{16,0},{32,16},{48,32},{1,49},{17,1},{33,17},{49,33},{2,50}... | collective-permute-start | bytes 2359304 | tf_op jit(solution)/shard_map/ppermute | solution.py:298
  119.6 2.2 collective-permute-start
  121.8 4.9 %collective-permute-start.1 = (bf16[16,192,128]{2,1,0:T(8,128)(2,1)}, bf16[16,192,128]{2,1,0:T(8,128)(2,1)}, u32[]{:S(2)}, u32[]{:S(2)}) collective-permute-start(bf16[16,192,128]{2,1,0:T(8,128)(2,1)} %all_to_all.21.k0), channel_id=1, source_target_pairs={{0,48},{16,0},{32,16},{48,32},{1,49},{17,1},{33,17},{49,33},{2,50}... | collective-permute-start | bytes 2359304 | tf_op jit(solution)/shard_map/ppermute | solution.py:298
  126.6 9.4 %collective-permute-done.4.k1 = bf16[16,192,128]{2,1,0:T(8,128)(2,1)S(1)} collective-permute-done((bf16[16,192,128]{2,1,0:T(8,128)(2,1)S(1)}, bf16[16,192,128]{2,1,0:T(8,128)(2,1)S(1)}, u32[]{:S(2)}, u32[]{:S(2)}) %collective-permute-start.4) | collective-permute-done | bytes 786464 | tf_op jit(solution)/shard_map/ppermute | solution.py:298
  136.0 0.8 slice.26
  136.9 2.2 collective-permute-start.6
  139.1 0.8 slice.27
  139.9 4.9 %collective-permute-start.7 = (bf16[8,192,128]{2,1,0:T(8,128)(2,1)}, bf16[8,192,128]{2,1,0:T(8,128)(2,1)S(1)}, u32[]{:S(2)}, u32[]{:S(2)}) collective-permute-start(bf16[8,192,128]{2,1,0:T(8,128)(2,1)} %slice.27), channel_id=1, source_target_pairs={{0,48},{16,0},{32,16},{48,32},{1,49},{17,1},{33,17},{49,33},{2,50}... | collective-permute-start | bytes 1179656 | tf_op jit(solution)/shard_map/ppermute | solution.py:298
  145.4 0.1 pad_add_fusion.info
  145.5 7.5 %collective-permute-done.k1 = bf16[16,192,128]{2,1,0:T(8,128)(2,1)} collective-permute-done((bf16[16,192,128]{2,1,0:T(8,128)(2,1)}, bf16[16,192,128]{2,1,0:T(8,128)(2,1)}, u32[]{:S(2)}, u32[]{:S(2)}) %collective-permute-start) | collective-permute-done | bytes 786464 | tf_op jit(solution)/shard_map/ppermute | solution.py:298
  153.0 1.8 slice.24
  154.8 2.2 collective-permute-start.2
  157.0 1.8 slice.25
  158.8 4.9 %collective-permute-start.3 = (bf16[8,192,128]{2,1,0:T(8,128)(2,1)}, bf16[8,192,128]{2,1,0:T(8,128)(2,1)}, u32[]{:S(2)}, u32[]{:S(2)}) collective-permute-start(bf16[8,192,128]{2,1,0:T(8,128)(2,1)} %slice.25), channel_id=1, source_target_pairs={{0,48},{16,0},{32,16},{48,32},{1,49},{17,1},{33,17},{49,33},{2,50}... | collective-permute-start | bytes 1179656 | tf_op jit(solution)/shard_map/ppermute | solution.py:298
  163.7 27.3 %shard_map.137.main_ref = bf16[16,96,128]{2,1,0:T(8,128)(2,1)S(1)} custom-call(s32[3]{0:T(128)S(1)} %pad_add_fusion.info, bf16[16,128,128]{2,1,0:T(8,128)(2,1)S(1)} %all-to-all-done.q_ref, bf16[16,192,128]{2,1,0:T(8,128)(2,1)S(1)} %all_to_all.20.k0, bf16[16,192,128]{2,1,0:T(8,128)(2,1)} %copy-done.9, bf16[16,192,128]{2,1,0:T(8,128)(2,1)} %copy-done.10, ...), custom_call_target="tpu_custom_call" | custom-call | flops 10468982784 | bytes 3145728 | tf_op jit(solution)/shard_map/pallas_call | solution.py:160
  191.0 9.1 %shard_map.138 = bf16[16,128,128]{2,1,0:T(8,128)(2,1)} custom-call(s32[3]{0:T(128)S(1)} %pad_add_fusion.info, bf16[16,128,128]{2,1,0:T(8,128)(2,1)S(1)} %all-to-all-done.q_ref, bf16[16,192,128]{2,1,0:T(8,128)(2,1)} %all_to_all.21.k0, bf16[16,192,128]{2,1,0:T(8,128)(2,1)} %collective-permute-done.k1, bf16[16,192,128]{2,1,0:T(8,128)(2,1)} %collective-permute-done.1.k2, ...), custom_call_target="tpu_custom_call" | custom-call | flops 2617245696 | bytes 3145728 | tf_op jit(solution)/shard_map/pallas_call | solution.py:175
  200.1 12.1 %all-to-all-start.3 = ((bf16[16,128,128]{2,1,0:T(8,128)(2,1)}), bf16[16,128,128]{2,1,0:T(8,128)(2,1)S(1)}, u32[]{:S(2)}, u32[]{:S(2)}) async-start(bf16[16,128,128]{2,1,0:T(8,128)(2,1)} %shard_map.138), calls=%async_computation.3 | async-start | bytes 1048576 | tf_op jit(solution)/shard_map/all_to_all | solution.py:335
  212.2 0.0 copy-start.11
  212.2 0.3 copy.15.weight_ref
  212.6 0.4 copy-done.11
  213.0 0.7 copy-done.12
  213.7 0.0 copy-start.4
  213.7 24.2 %all-to-all-done.3.back_ref = bf16[16,128,128]{2,1,0:T(8,128)(2,1)S(1)} async-done(((bf16[16,128,128]{2,1,0:T(8,128)(2,1)}), bf16[16,128,128]{2,1,0:T(8,128)(2,1)S(1)}, u32[]{:S(2)}, u32[]{:S(2)}) %all-to-all-start.3) | async-done | bytes 524320 | tf_op jit(solution)/shard_map/all_to_all | solution.py:335
  237.9 0.6 shard_map.139
  238.5 1.9 collective-permute-start.8
  240.4 1.3 collective-permute-start.9
  241.7 0.0 collective-permute-done.8
  241.7 5.7 %collective-permute-done.9 = bf16[24,64]{1,0:T(8,128)(2,1)S(1)} collective-permute-done((bf16[24,64]{1,0:T(8,128)(2,1)S(1)}, bf16[24,64]{1,0:T(8,128)(2,1)S(1)}, u32[]{:S(2)}, u32[]{:S(2)}) %collective-permute-start.9) | collective-permute-done | bytes 3104 | tf_op jit(solution)/shard_map/ppermute | solution.py:338
  247.4 5.5 %collective-permute-start.10 = (bf16[144,64]{1,0:T(8,128)(2,1)S(1)}, bf16[144,64]{1,0:T(8,128)(2,1)S(1)}, u32[]{:S(2)}, u32[]{:S(2)}) collective-permute-start(bf16[144,64]{1,0:T(8,128)(2,1)S(1)} %get-tuple-element.12), channel_id=1, source_target_pairs={{0,4},{4,8},{8,12},{12,0},{1,5},{5,9},{9,13},{13,1},{2,6},{6,10},{... | collective-permute-start | bytes 55304 | tf_op jit(solution)/shard_map/ppermute | solution.py:298
  252.9 7.7 %collective-permute-start.11 = (bf16[144,64]{1,0:T(8,128)(2,1)S(1)}, bf16[144,64]{1,0:T(8,128)(2,1)S(1)}, u32[]{:S(2)}, u32[]{:S(2)}) collective-permute-start(bf16[144,64]{1,0:T(8,128)(2,1)S(1)} %get-tuple-element.12), channel_id=1, source_target_pairs={{0,8},{4,12},{8,0},{12,4},{1,9},{5,13},{9,1},{13,5},{2,10},{6,14},... | collective-permute-start | bytes 55304 | tf_op jit(solution)/shard_map/ppermute | solution.py:298
  260.6 3.1 %collective-permute-start.12 = (bf16[144,64]{1,0:T(8,128)(2,1)S(1)}, bf16[144,64]{1,0:T(8,128)(2,1)S(1)}, u32[]{:S(2)}, u32[]{:S(2)}) collective-permute-start(bf16[144,64]{1,0:T(8,128)(2,1)S(1)} %get-tuple-element.12), channel_id=1, source_target_pairs={{0,12},{4,0},{8,4},{12,8},{1,13},{5,1},{9,5},{13,9},{2,14},{6,2},{... | collective-permute-start | bytes 55304 | tf_op jit(solution)/shard_map/ppermute | solution.py:298
  263.8 3.7 %collective-permute-done.11 = bf16[144,64]{1,0:T(8,128)(2,1)S(1)} collective-permute-done((bf16[144,64]{1,0:T(8,128)(2,1)S(1)}, bf16[144,64]{1,0:T(8,128)(2,1)S(1)}, u32[]{:S(2)}, u32[]{:S(2)}) %collective-permute-start.11) | collective-permute-done | bytes 18464 | tf_op jit(solution)/shard_map/ppermute | solution.py:298
  267.5 3.3 %collective-permute-done.12 = bf16[144,64]{1,0:T(8,128)(2,1)S(1)} collective-permute-done((bf16[144,64]{1,0:T(8,128)(2,1)S(1)}, bf16[144,64]{1,0:T(8,128)(2,1)S(1)}, u32[]{:S(2)}, u32[]{:S(2)}) %collective-permute-start.12) | collective-permute-done | bytes 18464 | tf_op jit(solution)/shard_map/ppermute | solution.py:298
  270.8 0.0 copy-start.14
  270.8 3.7 %collective-permute-start.13 = (bf16[4,144,64]{2,1,0:T(8,128)(2,1)S(1)}, bf16[4,144,64]{2,1,0:T(8,128)(2,1)S(1)}, u32[]{:S(2)}, u32[]{:S(2)}) collective-permute-start(bf16[4,144,64]{2,1,0:T(8,128)(2,1)S(1)} %pad_maximum_fusion.g0), channel_id=1, source_target_pairs={{0,16},{16,32},{32,48},{48,0},{1,17},{17,33},{33,49},{49,1},{2,18}... | collective-permute-start | bytes 221192 | tf_op jit(solution)/shard_map/ppermute | solution.py:298
  274.5 5.0 %collective-permute-start.14 = (bf16[4,144,64]{2,1,0:T(8,128)(2,1)S(1)}, bf16[4,144,64]{2,1,0:T(8,128)(2,1)S(1)}, u32[]{:S(2)}, u32[]{:S(2)}) collective-permute-start(bf16[4,144,64]{2,1,0:T(8,128)(2,1)S(1)} %pad_maximum_fusion.g0), channel_id=1, source_target_pairs={{0,32},{16,48},{32,0},{48,16},{1,33},{17,49},{33,1},{49,17},{2,34}... | collective-permute-start | bytes 221192 | tf_op jit(solution)/shard_map/ppermute | solution.py:298
  279.5 2.7 collective-permute-start.15
  282.3 0.8 collective-permute-done.14.g2
  283.1 3.5 %collective-permute-done.15.g3 = bf16[4,144,64]{2,1,0:T(8,128)(2,1)S(1)} collective-permute-done((bf16[4,144,64]{2,1,0:T(8,128)(2,1)S(1)}, bf16[4,144,64]{2,1,0:T(8,128)(2,1)S(1)}, u32[]{:S(2)}, u32[]{:S(2)}) %collective-permute-start.15) | collective-permute-done | bytes 73760 | tf_op jit(solution)/shard_map/ppermute | solution.py:298
  286.6 2.6 shard_map.140
  (38 shorter events, 0.2 us)
Async XLA Ops:
  0.0 1.0 copy-start
  1.0 1.0 copy-start.1
  2.1 1.0 copy-start.2
  107.0 56.6 %all-to-all-start = ((bf16[16,128,128]{2,1,0:T(8,128)(2,1)}), bf16[16,128,128]{2,1,0:T(8,128)(2,1)S(1)}, u32[]{:S(2)}, u32[]{:S(2)}) async-start(bf16[16,128,128]{2,1,0:T(8,128)(2,1)} %get-tuple-element.8), calls=%async_computation | async-start | bytes 1048576 | tf_op jit(solution)/shard_map/all_to_all | solution.py:332
  112.5 23.6 %collective-permute-start.4 = (bf16[16,192,128]{2,1,0:T(8,128)(2,1)S(1)}, bf16[16,192,128]{2,1,0:T(8,128)(2,1)S(1)}, u32[]{:S(2)}, u32[]{:S(2)}) collective-permute-start(bf16[16,192,128]{2,1,0:T(8,128)(2,1)S(1)} %all_to_all.20.k0), channel_id=1, source_target_pairs={{0,16},{16,32},{32,48},{48,0},{1,17},{17,33},{33,49},{49,1},{2,18}... | collective-permute-start | bytes 2359304 | tf_op jit(solution)/shard_map/ppermute | solution.py:298
  115.9 23.2 %collective-permute-start.5 = (bf16[16,192,128]{2,1,0:T(8,128)(2,1)S(1)}, bf16[16,192,128]{2,1,0:T(8,128)(2,1)S(1)}, u32[]{:S(2)}, u32[]{:S(2)}) collective-permute-start(bf16[16,192,128]{2,1,0:T(8,128)(2,1)S(1)} %all_to_all.20.k0), channel_id=1, source_target_pairs={{0,48},{16,0},{32,16},{48,32},{1,49},{17,1},{33,17},{49,33},{2,50}... | collective-permute-start | bytes 2359304 | tf_op jit(solution)/shard_map/ppermute | solution.py:298
  119.6 33.4 %collective-permute-start = (bf16[16,192,128]{2,1,0:T(8,128)(2,1)}, bf16[16,192,128]{2,1,0:T(8,128)(2,1)}, u32[]{:S(2)}, u32[]{:S(2)}) collective-permute-start(bf16[16,192,128]{2,1,0:T(8,128)(2,1)} %all_to_all.21.k0), channel_id=1, source_target_pairs={{0,16},{16,32},{32,48},{48,0},{1,17},{17,33},{33,49},{49,1},{2,18}... | collective-permute-start | bytes 2359304 | tf_op jit(solution)/shard_map/ppermute | solution.py:298
  121.8 35.2 %collective-permute-start.1 = (bf16[16,192,128]{2,1,0:T(8,128)(2,1)}, bf16[16,192,128]{2,1,0:T(8,128)(2,1)}, u32[]{:S(2)}, u32[]{:S(2)}) collective-permute-start(bf16[16,192,128]{2,1,0:T(8,128)(2,1)} %all_to_all.21.k0), channel_id=1, source_target_pairs={{0,48},{16,0},{32,16},{48,32},{1,49},{17,1},{33,17},{49,33},{2,50}... | collective-permute-start | bytes 2359304 | tf_op jit(solution)/shard_map/ppermute | solution.py:298
  136.0 3.9 %copy-start.9 = (bf16[16,192,128]{2,1,0:T(8,128)(2,1)}, bf16[16,192,128]{2,1,0:T(8,128)(2,1)S(1)}, u32[]{:S(2)}) copy-start(bf16[16,192,128]{2,1,0:T(8,128)(2,1)S(1)} %collective-permute-done.4.k1) | copy-start | bytes 2359300
  136.9 26.8 %collective-permute-start.6 = (bf16[8,192,128]{2,1,0:T(8,128)(2,1)}, bf16[8,192,128]{2,1,0:T(8,128)(2,1)S(1)}, u32[]{:S(2)}, u32[]{:S(2)}) collective-permute-start(bf16[8,192,128]{2,1,0:T(8,128)(2,1)} %slice.26), channel_id=1, source_target_pairs={{0,16},{16,32},{32,48},{48,0},{1,17},{17,33},{33,49},{49,1},{2,18}... | collective-permute-start | bytes 1179656 | tf_op jit(solution)/shard_map/ppermute | solution.py:298
  139.1 6.3 %copy-start.10 = (bf16[16,192,128]{2,1,0:T(8,128)(2,1)}, bf16[16,192,128]{2,1,0:T(8,128)(2,1)S(1)}, u32[]{:S(2)}) copy-start(bf16[16,192,128]{2,1,0:T(8,128)(2,1)S(1)} %collective-permute-done.5.k2) | copy-start | bytes 2359300
  139.9 23.8 %collective-permute-start.7 = (bf16[8,192,128]{2,1,0:T(8,128)(2,1)}, bf16[8,192,128]{2,1,0:T(8,128)(2,1)S(1)}, u32[]{:S(2)}, u32[]{:S(2)}) collective-permute-start(bf16[8,192,128]{2,1,0:T(8,128)(2,1)} %slice.27), channel_id=1, source_target_pairs={{0,48},{16,0},{32,16},{48,32},{1,49},{17,1},{33,17},{49,33},{2,50}... | collective-permute-start | bytes 1179656 | tf_op jit(solution)/shard_map/ppermute | solution.py:298
  145.5 18.2 %copy-start.6 = (bf16[512,640]{1,0:T(8,128)(2,1)S(1)}, bf16[512,640]{1,0:T(8,128)(2,1)}, u32[]{:S(2)}) copy-start(bf16[512,640]{1,0:T(8,128)(2,1)} %tk_ref.3) | copy-start | bytes 1966084
  145.5 18.2 %copy-start.7 = (bf16[512,640]{1,0:T(8,128)(2,1)S(1)}, bf16[512,640]{1,0:T(8,128)(2,1)}, u32[]{:S(2)}) copy-start(bf16[512,640]{1,0:T(8,128)(2,1)} %tv_ref.3) | copy-start | bytes 1966084
  154.8 36.2 %collective-permute-start.2 = (bf16[8,192,128]{2,1,0:T(8,128)(2,1)}, bf16[8,192,128]{2,1,0:T(8,128)(2,1)}, u32[]{:S(2)}, u32[]{:S(2)}) collective-permute-start(bf16[8,192,128]{2,1,0:T(8,128)(2,1)} %slice.24), channel_id=1, source_target_pairs={{0,16},{16,32},{32,48},{48,0},{1,17},{17,33},{33,49},{49,1},{2,18}... | collective-permute-start | bytes 1179656 | tf_op jit(solution)/shard_map/ppermute | solution.py:298
  158.8 32.2 %collective-permute-start.3 = (bf16[8,192,128]{2,1,0:T(8,128)(2,1)}, bf16[8,192,128]{2,1,0:T(8,128)(2,1)}, u32[]{:S(2)}, u32[]{:S(2)}) collective-permute-start(bf16[8,192,128]{2,1,0:T(8,128)(2,1)} %slice.25), channel_id=1, source_target_pairs={{0,48},{16,0},{32,16},{48,32},{1,49},{17,1},{33,17},{49,33},{2,50}... | collective-permute-start | bytes 1179656 | tf_op jit(solution)/shard_map/ppermute | solution.py:298
  200.1 12.1 %copy-start.8 = (bf16[2560,64]{0,1:T(8,128)(2,1)S(1)}, bf16[2560,64]{0,1:T(8,128)(2,1)}, u32[]{:S(2)}) copy-start(bf16[2560,64]{0,1:T(8,128)(2,1)} %param.23) | copy-start | bytes 983044
  200.1 37.8 %all-to-all-start.3 = ((bf16[16,128,128]{2,1,0:T(8,128)(2,1)}), bf16[16,128,128]{2,1,0:T(8,128)(2,1)S(1)}, u32[]{:S(2)}, u32[]{:S(2)}) async-start(bf16[16,128,128]{2,1,0:T(8,128)(2,1)} %shard_map.138), calls=%async_computation.3 | async-start | bytes 1048576 | tf_op jit(solution)/shard_map/all_to_all | solution.py:335
  212.2 0.7 copy-start.11
  212.9 0.7 copy-start.12
  213.7 24.2 %copy-start.4 = (f32[64]{0:T(128)S(1)}, f32[64]{0:T(128)}, u32[]{:S(2)}) copy-start(f32[64]{0:T(128)} %param.24) | copy-start | bytes 772
  238.5 48.0 %copy-start.3 = (bf16[432,384]{1,0:T(8,128)(2,1)S(1)}, bf16[432,384]{1,0:T(8,128)(2,1)}, u32[]{:S(2)}) copy-start(bf16[432,384]{1,0:T(8,128)(2,1)} %weight_ref.2) | copy-start | bytes 995332
  238.5 3.2 %collective-permute-start.8 = (bf16[24,64]{1,0:T(8,128)(2,1)S(1)}, bf16[24,64]{1,0:T(8,128)(2,1)S(1)}, u32[]{:S(2)}, u32[]{:S(2)}) collective-permute-start(bf16[24,64]{1,0:T(8,128)(2,1)S(1)} %get-tuple-element.13), channel_id=1, source_target_pairs={{0,1},{1,2},{2,3},{4,5},{5,6},{6,7},{8,9},{9,10},{10,11},{12,13},{... | collective-permute-start | bytes 9224 | tf_op jit(solution)/shard_map/ppermute | solution.py:337
  240.4 7.0 %collective-permute-start.9 = (bf16[24,64]{1,0:T(8,128)(2,1)S(1)}, bf16[24,64]{1,0:T(8,128)(2,1)S(1)}, u32[]{:S(2)}, u32[]{:S(2)}) collective-permute-start(bf16[24,64]{1,0:T(8,128)(2,1)S(1)} %get-tuple-element.14), channel_id=1, source_target_pairs={{1,0},{2,1},{3,2},{5,4},{6,5},{7,6},{9,8},{10,9},{11,10},{13,12},{... | collective-permute-start | bytes 9224 | tf_op jit(solution)/shard_map/ppermute | solution.py:338
  247.4 16.3 %collective-permute-start.10 = (bf16[144,64]{1,0:T(8,128)(2,1)S(1)}, bf16[144,64]{1,0:T(8,128)(2,1)S(1)}, u32[]{:S(2)}, u32[]{:S(2)}) collective-permute-start(bf16[144,64]{1,0:T(8,128)(2,1)S(1)} %get-tuple-element.12), channel_id=1, source_target_pairs={{0,4},{4,8},{8,12},{12,0},{1,5},{5,9},{9,13},{13,1},{2,6},{6,10},{... | collective-permute-start | bytes 55304 | tf_op jit(solution)/shard_map/ppermute | solution.py:298
  252.9 14.6 %collective-permute-start.11 = (bf16[144,64]{1,0:T(8,128)(2,1)S(1)}, bf16[144,64]{1,0:T(8,128)(2,1)S(1)}, u32[]{:S(2)}, u32[]{:S(2)}) collective-permute-start(bf16[144,64]{1,0:T(8,128)(2,1)S(1)} %get-tuple-element.12), channel_id=1, source_target_pairs={{0,8},{4,12},{8,0},{12,4},{1,9},{5,13},{9,1},{13,5},{2,10},{6,14},... | collective-permute-start | bytes 55304 | tf_op jit(solution)/shard_map/ppermute | solution.py:298
  260.6 10.2 %collective-permute-start.12 = (bf16[144,64]{1,0:T(8,128)(2,1)S(1)}, bf16[144,64]{1,0:T(8,128)(2,1)S(1)}, u32[]{:S(2)}, u32[]{:S(2)}) collective-permute-start(bf16[144,64]{1,0:T(8,128)(2,1)S(1)} %get-tuple-element.12), channel_id=1, source_target_pairs={{0,12},{4,0},{8,4},{12,8},{1,13},{5,1},{9,5},{13,9},{2,14},{6,2},{... | collective-permute-start | bytes 55304 | tf_op jit(solution)/shard_map/ppermute | solution.py:298
  270.8 11.5 %copy-start.13 = (f32[384]{0:T(512)S(1)}, f32[384]{0:T(512)}, u32[]{:S(2)}) copy-start(f32[384]{0:T(512)} %param.26) | copy-start | bytes 4612
  270.8 11.4 %copy-start.14 = (f32[384]{0:T(512)S(1)}, f32[384]{0:T(512)}, u32[]{:S(2)}) copy-start(f32[384]{0:T(512)} %param.27) | copy-start | bytes 4612
  270.8 11.5 %collective-permute-start.13 = (bf16[4,144,64]{2,1,0:T(8,128)(2,1)S(1)}, bf16[4,144,64]{2,1,0:T(8,128)(2,1)S(1)}, u32[]{:S(2)}, u32[]{:S(2)}) collective-permute-start(bf16[4,144,64]{2,1,0:T(8,128)(2,1)S(1)} %pad_maximum_fusion.g0), channel_id=1, source_target_pairs={{0,16},{16,32},{32,48},{48,0},{1,17},{17,33},{33,49},{49,1},{2,18}... | collective-permute-start | bytes 221192 | tf_op jit(solution)/shard_map/ppermute | solution.py:298
  274.5 8.5 %collective-permute-start.14 = (bf16[4,144,64]{2,1,0:T(8,128)(2,1)S(1)}, bf16[4,144,64]{2,1,0:T(8,128)(2,1)S(1)}, u32[]{:S(2)}, u32[]{:S(2)}) collective-permute-start(bf16[4,144,64]{2,1,0:T(8,128)(2,1)S(1)} %pad_maximum_fusion.g0), channel_id=1, source_target_pairs={{0,32},{16,48},{32,0},{48,16},{1,33},{17,49},{33,1},{49,17},{2,34}... | collective-permute-start | bytes 221192 | tf_op jit(solution)/shard_map/ppermute | solution.py:298
  279.5 7.0 %collective-permute-start.15 = (bf16[4,144,64]{2,1,0:T(8,128)(2,1)S(1)}, bf16[4,144,64]{2,1,0:T(8,128)(2,1)S(1)}, u32[]{:S(2)}, u32[]{:S(2)}) collective-permute-start(bf16[4,144,64]{2,1,0:T(8,128)(2,1)S(1)} %pad_maximum_fusion.g0), channel_id=1, source_target_pairs={{0,48},{16,0},{32,16},{48,32},{1,49},{17,1},{33,17},{49,33},{2,50}... | collective-permute-start | bytes 221192 | tf_op jit(solution)/shard_map/ppermute | solution.py:298
  282.3 4.3 %copy-start.5 = (s32[16]{0:T(128)S(1)}, s32[16]{0:T(128)}, u32[]{:S(2)}) copy-start(s32[16]{0:T(128)} %tile_map.1) | copy-start | bytes 196

commit v2 on v1

v2 whole, which is shorter than its diff:
```python
import functools

import jax
import jax.numpy as jnp
from jax import lax
from jax.experimental import pallas as pl
from jax.experimental.pallas import tpu as pltpu
from jax.sharding import Mesh, PartitionSpec as P

PCOL = 24
HDIM = 128
TXT = 512
LAT = 16
ROWS = 96
NZ = 16
C_OUT = 384
LOG2E = 1.4426950408889634
SCALE2 = HDIM ** (-0.5) * LOG2E
Z = ("zh", "zl")
F32 = jnp.float32
BF = jnp.bfloat16
VMEM_LIMIT = 50 * 1024 * 1024


def params():
    return pltpu.CompilerParams(vmem_limit_bytes=VMEM_LIMIT)


def vmem():
    return pl.BlockSpec(memory_space=pltpu.VMEM)


def smem():
    return pl.BlockSpec(memory_space=pltpu.SMEM)


PART = 24
SLOT = 32


def pack_kernel(q_ref, k_ref, v_ref, shared_out, kv_out, q_out):
    for zl in range(4):
        last = slice((5 * zl + 4) * HDIM, (5 * zl + 5) * HDIM)
        queries_last = q_ref[:, last].astype(F32)
        for zh in range(4):
            z = zh * 4 + zl
            own = slice((5 * zl + zh) * HDIM, (5 * zl + zh + 1) * HDIM)
            shared_out[z, 0:ROWS, :] = k_ref[:, last]
            shared_out[z, ROWS : 2 * ROWS, :] = v_ref[:, last]
            part = queries_last[PART * zh : PART * (zh + 1)]
            shared_out[z, 2 * ROWS : 2 * ROWS + SLOT, :] = jnp.concatenate(
                [part, jnp.zeros((SLOT - PART, HDIM), F32)], axis=0
            ).astype(BF)
            kv_out[z, 0:ROWS, :] = k_ref[:, own]
            kv_out[z, ROWS : 2 * ROWS, :] = v_ref[:, own]
            q_out[z] = q_ref[:, own]


def pack(queries, keys, values):
    return pl.pallas_call(
        pack_kernel,
        out_shape=(
            jax.ShapeDtypeStruct((NZ, 2 * ROWS + SLOT, HDIM), BF),
            jax.ShapeDtypeStruct((NZ, 2 * ROWS, HDIM), BF),
            jax.ShapeDtypeStruct((NZ, ROWS, HDIM), BF),
        ),
        in_specs=[vmem()] * 3,
        out_specs=(vmem(),) * 3,
        compiler_params=params(),
    )(queries, keys, values)


def dot_t(a, b):
    return lax.dot_general(a, b, (((1,), (1,)), ((), ())), preferred_element_type=F32)


def attend(query, pieces, text_key, text_value, text_len):
    ones = jnp.ones((HDIM, HDIM), BF)

    def scores_of(piece):
        ref, lo, hi = piece
        return dot_t(query, ref[lo:hi, 0:ROWS, :].reshape((hi - lo) * ROWS, HDIM))

    def row_peak(scores):
        top = scores[:, :HDIM]
        for col in range(HDIM, scores.shape[1], HDIM):
            top = jnp.maximum(top, scores[:, col : col + HDIM])
        return jnp.max(top, axis=-1, keepdims=True)

    def widened(value):
        return jnp.concatenate([value, jnp.tile(ones, (value.shape[0] // HDIM, 1))], axis=1)

    peak, total = None, None
    scores = scores_of(pieces[0])
    for index, (ref, lo, hi) in enumerate(pieces):
        later = scores_of(pieces[index + 1]) if index + 1 < len(pieces) else None
        highest = row_peak(scores) * SCALE2
        value = widened(ref[lo:hi, ROWS : 2 * ROWS, :].reshape((hi - lo) * ROWS, HDIM))
        newest = highest if peak is None else jnp.maximum(peak, highest)
        weights = jnp.exp2(scores * SCALE2 - newest).astype(BF)
        part = jnp.dot(weights, value, preferred_element_type=F32)
        total = part if peak is None else total * jnp.exp2(peak - newest) + part
        peak, scores = newest, later
    self_out = total[:, :HDIM] / total[:, HDIM:]
    text_scores = dot_t(query, text_key) * SCALE2
    usable = lax.broadcasted_iota(jnp.int32, text_scores.shape, 1) < text_len
    text_scores = jnp.where(usable, text_scores, -1e30)
    text_peak = row_peak(text_scores)
    text_weights = jnp.where(usable, jnp.exp2(text_scores - text_peak), 0.0).astype(BF)
    text_total = jnp.dot(text_weights, widened(text_value), preferred_element_type=F32)
    return self_out + text_total[:, :HDIM] / text_total[:, HDIM:]


def pieces_of(refs):
    pieces = []
    for ref in refs:
        count = ref.shape[0]
        for lo in range(0, count, 8):
            pieces.append((ref, lo, min(lo + 8, count)))
    return pieces


def main_kernel(info, q_ref, k0, k1, k2, k3, k4, tk_ref, tv_ref, out_ref):
    query = q_ref[:, 0:ROWS, :].reshape(4 * ROWS, HDIM)
    column = pl.ds(pl.multiple_of(info[0] * HDIM, HDIM), HDIM)
    pieces = pieces_of((k0, k1, k2, k3, k4))
    result = attend(query, pieces, tk_ref[:, column], tv_ref[:, column], info[1])
    out_ref[...] = result.astype(BF).reshape(4, ROWS, HDIM)


def shared_kernel(info, s_ref, k1, k2, k3, k4, tk_ref, tv_ref, q_ref, out_ref):
    query = s_ref[:, 2 * ROWS : 2 * ROWS + SLOT, :].astype(F32)[:, :PART]
    query = query.reshape(NZ * PART, HDIM).astype(BF)
    column = slice(4 * HDIM, 5 * HDIM)
    pieces = pieces_of((s_ref, k1, k2, k3, k4))
    result = attend(query, pieces, tk_ref[:, column], tv_ref[:, column], info[1])
    filler = jnp.zeros((NZ, SLOT - PART, HDIM), F32)
    result = jnp.concatenate([result.reshape(NZ, PART, HDIM), filler], axis=1)
    out_ref[:, 0:ROWS, :] = q_ref[...]
    out_ref[:, ROWS : ROWS + SLOT, :] = result.astype(BF)


KEYS = 6144


def cost(rows):
    return pl.CostEstimate(
        flops=rows * (KEYS + TXT) * HDIM * 8,
        bytes_accessed=2 * KEYS * HDIM * 2,
        transcendentals=rows * (KEYS + TXT),
    )


def main_attention(info, queries, kv, text_keys, text_values):
    whole = lambda a: pl.BlockSpec(a.shape, lambda i, n=a.ndim: (0,) * n)
    return pl.pallas_call(
        main_kernel,
        grid=(NZ // 4,),
        out_shape=jax.ShapeDtypeStruct((NZ, ROWS, HDIM), BF),
        in_specs=[smem(), pl.BlockSpec((4,) + queries.shape[1:], lambda i: (i, 0, 0))]
        + [whole(a) for a in kv]
        + [whole(text_keys), whole(text_values)],
        out_specs=pl.BlockSpec((4, ROWS, HDIM), lambda i: (i, 0, 0)),
        compiler_params=params(),
        cost_estimate=cost(NZ * ROWS),
    )(info, queries, *kv, text_keys, text_values)


def shared_attention(info, kv, text_keys, text_values, queries):
    return pl.pallas_call(
        shared_kernel,
        out_shape=jax.ShapeDtypeStruct((NZ, ROWS + SLOT, HDIM), BF),
        in_specs=[smem()] + [vmem()] * 8,
        out_specs=vmem(),
        compiler_params=params(),
        cost_estimate=cost(NZ * PART),
    )(info, *kv, text_keys, text_values, queries)


def head_kernel(
    back_ref, shared_ref, gain_ref, shift_ref, weight_ref, bias_ref, out_ref
):
    blocks = []
    for head in range(20):
        zl, zh = head // 5, head % 5
        if zh < 4:
            block = back_ref[zh * 4 + zl].astype(F32)
        else:
            parts = [
                shared_ref[part * 4 + zl, ROWS : ROWS + SLOT, :].astype(F32)[:PART]
                for part in range(4)
            ]
            block = jnp.concatenate(parts, axis=0)
        blocks.append(block)
    count = 20 * HDIM
    average = jnp.sum(sum(blocks), axis=-1, keepdims=True) / count
    blocks = [block - average for block in blocks]
    variance = jnp.sum(sum(block * block for block in blocks), axis=-1, keepdims=True) / count
    scale = lax.rsqrt(variance + 1e-06)
    patches = jnp.zeros((ROWS, 64), F32)
    for head in range(20):
        span = slice(head * HDIM, (head + 1) * HDIM)
        normed = (blocks[head] * scale * gain_ref[:, span] + shift_ref[:, span]).astype(BF)
        patches = patches + jnp.dot(normed, weight_ref[span, :], preferred_element_type=F32)
    patches = patches + bias_ref[...]
    packed = jnp.concatenate([patches[: ROWS // 2], patches[ROWS // 2 :]], axis=1).astype(BF)
    for copy in range(NZ):
        out_ref[copy] = packed


def head(back, shared, mod_gain, mod_shift, head_weight, head_bias):
    return pl.pallas_call(
        head_kernel,
        out_shape=jax.ShapeDtypeStruct((NZ, ROWS // 2, HDIM), BF),
        in_specs=[vmem()] * 6,
        out_specs=vmem(),
        compiler_params=params(),
    )(back, shared, mod_gain[None], mod_shift[None], head_weight, head_bias[None])


SLAB = 72


def slab_kernel(info, line_ref, out_ref):
    zl = info[3]
    for zh in range(4):
        own = line_ref[zh * 4 + zl].astype(F32)
        above = line_ref[zh * 4 + jnp.maximum(zl - 1, 0)].astype(F32)[PCOL:, 64:]
        below = line_ref[zh * 4 + jnp.minimum(zl + 1, 3)].astype(F32)[:PCOL, :64]
        above = jnp.where(zl > 0, above, 0.0)
        below = jnp.where(zl < 3, below, 0.0)
        left = jnp.concatenate([above, own[:, :64]], axis=0)
        right = jnp.concatenate([own[:, 64:], below], axis=0)
        packed = jnp.concatenate([left, right], axis=1).astype(BF)
        for copy in range(4):
            out_ref[copy, zh] = packed


def slab_of(info, line):
    return pl.pallas_call(
        slab_kernel,
        out_shape=jax.ShapeDtypeStruct((4, 4, SLAB, HDIM), BF),
        in_specs=[smem(), vmem()],
        out_specs=vmem(),
        compiler_params=params(),
    )(info, line)


def conv_kernel(
    info, tile_map, slab_ref, weight_ref, bias_ref, gain_ref, out_ref, wide_ref, pix_ref
):
    wide_ref[...] = jnp.zeros_like(wide_ref)
    for a in range(3):
        for di in (-1, 0, 1):
            for dj in (-1, 0, 1):
                for p in range(2):
                    for q in range(2):
                        row = ((dj + 1) * 4 + p * 2 + q) * LAT
                        for pp in range(2):
                            for qq in range(2):
                                r = 2 * di + p - pp + 1
                                s = 2 * dj + q - qq + 1
                                if 0 <= r < 3 and 0 <= s < 3:
                                    tap = ((a * 3 + r) * 3 + s) * LAT
                                    col = (pp * 2 + qq) * C_OUT
                                    wide_ref[
                                        a * 3 + di + 1, row : row + LAT, col : col + C_OUT
                                    ] = weight_ref[tap : tap + LAT, :]
    x, zh = info[2], info[0]
    pre = jnp.zeros((ROWS, 4 * C_OUT), F32)
    column = lax.broadcasted_iota(jnp.int32, (6 * PCOL, 64), 0) % PCOL
    for a in range(3):
        wanted = 4 * x + zh - 2 + a
        source = jnp.int32(0)
        for b in range(16):
            source = jnp.where(tile_map[b] == wanted, b, source)
        slab = slab_ref[source].astype(F32)
        slab = jnp.concatenate([slab[:, :64], slab[:, 64:]], axis=0)
        slab = jnp.where(wanted >= 0, slab, 0.0)
        zero = jnp.zeros((8, 64), F32)
        tall = jnp.concatenate([zero, slab, zero], axis=0)
        left = jnp.where(column == 0, 0.0, tall[7 : 7 + 6 * PCOL])
        right = jnp.where(column == PCOL - 1, 0.0, tall[9 : 9 + 6 * PCOL])
        joined = jnp.concatenate([left, slab, right], axis=1)
        for di in range(3):
            part = joined[di * PCOL : di * PCOL + ROWS].astype(BF)
            pre = pre + jnp.dot(part, wide_ref[a * 3 + di], preferred_element_type=F32)
    for pp in range(2):
        for qq in range(2):
            at = (pp * 2 + qq) * C_OUT
            value = pre[:, at : at + C_OUT] + bias_ref[...]
            mean = jnp.mean(value * value, axis=-1, keepdims=True)
            value = value * lax.rsqrt(mean + 1e-06) * gain_ref[...]
            value = value / (1.0 + jnp.exp(-value))
            for i in range(4):
                for part in range(3):
                    pix_ref[part, 2 * i + pp, pl.ds(qq, PCOL, 2), :] = value[
                        i * PCOL : (i + 1) * PCOL, part * HDIM : (part + 1) * HDIM
                    ]
    for part in range(3):
        out_ref[:, :, part * HDIM : (part + 1) * HDIM] = pix_ref[part].astype(BF)


def conv(info, tile_map, gathered, conv_weight, conv_bias, norm_gain):
    return pl.pallas_call(
        conv_kernel,
        out_shape=jax.ShapeDtypeStruct((8, 48, C_OUT), BF),
        in_specs=[smem(), smem()] + [vmem()] * 4,
        out_specs=vmem(),
        scratch_shapes=[
            pltpu.VMEM((9, 192, 4 * C_OUT), BF),
            pltpu.VMEM((3, 8, 48, HDIM), F32),
        ],
        compiler_params=params(),
    )(info, tile_map, gathered, conv_weight, conv_bias[None], norm_gain[None])


def shift(block, axis, distance):
    return lax.ppermute(block, axis, [(i, (i + distance) % 4) for i in range(4)])


def around(block, axis):
    right = shift(block, axis, 1)
    left = shift(block, axis, -1)
    half = block.shape[0] // 2
    return (block, right, left, shift(right[:half], axis, 1), shift(left[half:], axis, -1))


def exchange(block, axis):
    return lax.all_to_all(block, axis, split_axis=0, concat_axis=0, tiled=True)


def per_device(
    queries,
    keys,
    values,
    text_keys,
    text_values,
    text_len,
    tile_map,
    mod_gain,
    mod_shift,
    head_weight,
    head_bias,
    conv_weight,
    conv_bias,
    norm_gain,
):
    x, zh, zl = (lax.axis_index(axis) for axis in ("x", "zh", "zl"))
    info = jnp.stack([zh, text_len[0], x, zl]).astype(jnp.int32)
    shared_send, kv_send, q_send = pack(queries, keys, values)
    shared = exchange(shared_send, Z)
    shared, kv_send = lax.optimization_barrier((shared, kv_send))
    shared_kv = (shared,) + around(shared[:, : 2 * ROWS], "x")[1:]
    kv = exchange(kv_send, Z)
    third_send = shared_attention(info, shared_kv, text_keys, text_values, q_send)
    kv, third_send = lax.optimization_barrier((kv, third_send))
    main_kv = around(kv, "x")
    third = exchange(third_send, Z)
    back = exchange(main_attention(info, third, main_kv, text_keys, text_values), Z)
    line = exchange(head(back, third, mod_gain, mod_shift, head_weight, head_bias), Z)
    plane = exchange(slab_of(info, line), "x")
    gathered = plane.reshape(16, SLAB, HDIM)
    out = conv(info, tile_map, gathered, conv_weight, conv_bias, norm_gain)
    return out[None]


def solution(mesh):
    inner = Mesh(mesh.devices.reshape(8, 4, 4, 4), ("clip", "x", "zh", "zl"))
    tokens = P(("clip", "x", "zh", "zl"), None)
    placed = (
        tokens,
        tokens,
        tokens,
        P("clip", "zl"),
        P("clip", "zl"),
        P("clip"),
        P("clip"),
    ) + (P(),) * 7
    return jax.shard_map(
        per_device,
        mesh=inner,
        in_specs=placed,
        out_specs=P(("clip", "x", "zh"), "zl", None, None),
        check_vma=False,
    )
```

time: 290 us -> 247 us (0.85)
  blocking collectives: 103 us -> 82.1 us
  starting transfers between devices: 76.6 us -> 62.2 us
  Pallas kernels: 40.7 us -> 28.5 us
  waiting for transfers between devices: 58.1 us -> 63.2 us
    ppermute x14 -> x8, starting transfers between devices: 55.8 us -> 28.8 us  [shift(): lax.ppermute(block, axis, [(i, (i + distance) % 4) for i in range(4)])]
    all_to_all x2, blocking collectives: 103 us -> 82.1 us  [exchange(): return lax.all_to_all(block, axis, split_axis=0, concat_axis=0, tiled=True)]
    all_to_all x2 -> x4, starting transfers between devices: 17.6 us -> 33.4 us  [exchange(): return lax.all_to_all(block, axis, split_axis=0, concat_axis=0, tiled=True)]
    pallas_call x3 -> x4, Pallas kernels: 37 us -> 24.7 us  [the longest x1 16.5 us: main_attention(): pl.pallas_call(main_kernel, grid=(NZ // 4,), out_shape=jax.ShapeDtypeStru...]
    ppermute x14 -> x8, waiting for transfers between devices: 28.2 us -> 40 us  [shift(): lax.ppermute(block, axis, [(i, (i + distance) % 4) for i in range(4)])]
    ppermute x2 -> x0, waiting for transfers between devices: 5.7 us -> none  [the longest x1 5.67 us: per_device(): below = lax.ppermute(patches[:PCOL], 'zl', [(i + 1, i) for i in range(3)])]
    slice x5, local copies, waits for them, and re-layouts: 5.24 us -> 1.67 us  [the longest x2 0.8 us: around(): left[half:]]
    ppermute x2 -> x0, starting transfers between devices: 3.17 us -> none  [the longest x1 1.88 us: per_device(): lax.ppermute(patches[ROWS - PCOL:], 'zl', [(i, i + 1) for i in range(3)])]
  transfers between devices with their start and end apart: 18 -> 12, of which waited for: 8 -> 8; matrix products, arithmetic and copies ran while one was open for 2% -> 1% of each run, Pallas kernels for 9% -> 2%
where the time goes in v2:
time: 247 us; the launch traced here: 246 us
  blocking collectives  82.1 us (33%)
  waiting for transfers between devices  63.2 us (26%)
  starting transfers between devices  62.2 us (25%)
  Pallas kernels  28.5 us (12%)
  local copies, waits for them, and re-layouts  9.14 us (4%)
    all_to_all x2, blocking collectives, exchange(): return lax.all_to_all(block, axis, split_axis=0, concat_axis=0, tiled=True)  82.1 us
    ppermute x8, waiting for transfers between devices, shift(): lax.ppermute(block, axis, [(i, (i + distance) % 4) for i in range(4)])  40 us
    all_to_all x4, starting transfers between devices, exchange(): return lax.all_to_all(block, axis, split_axis=0, concat_axis=0, tiled=True)  33.4 us
    ppermute x8, starting transfers between devices, shift(): lax.ppermute(block, axis, [(i, (i + distance) % 4) for i in range(4)])  28.8 us
    all_to_all x4, waiting for transfers between devices, exchange(): return lax.all_to_all(block, axis, split_axis=0, concat_axis=0, tiled=True)  23.2 us
    pallas_call x1, Pallas kernels, main_attention(): pl.pallas_call(main_kernel, grid=(NZ // 4,), out_shape=jax.ShapeDtypeStru...  16.5 us
    unnamed x39, local copies, waits for them, and re-layouts  7.44 us
    pallas_call x1, Pallas kernels, shared_attention(): pl.pallas_call(shared_kernel, out_shape=jax.ShapeDtypeStruct((NZ, ROWS +...  6.06 us
  transfers between devices with their start and end apart: 12, of which 8 were waited for; matrix products, arithmetic and copies ran while one was open for 1% of the time, Pallas kernels for 2%

profile of v2, /device:TPU:24, one launch (start us, length us, event | category | flops | bytes accessed | tf_op | source)
XLA Modules:
  0.0 246.1 jit_solution(15728273456079769867)
XLA Ops:
  0.0 1.0 copy-done
  1.0 1.0 copy-done.1
  2.1 1.0 copy-done.2
  3.1 1.2 shard_map.136
  4.3 61.6 %all_to_all.30.s_ref = bf16[16,224,128]{2,1,0:T(8,128)(2,1)S(1)} all-to-all(bf16[16,224,128]{2,1,0:T(8,128)(2,1)S(1)} %get-tuple-element.12), channel_id=1, replica_groups=mesh['clip'=8,'x'=4,'zh'=4,'zl'=4] {'zh','zl'}, dimensions={0} | all-to-all | bytes 1835008 | tf_op jit(solution)/shard_map/all_to_all | solution.py:330
  65.9 5.6 %all-to-all-start.1 = ((bf16[16,192,128]{2,1,0:T(8,128)(2,1)}), bf16[16,192,128]{2,1,0:T(8,128)(2,1)S(1)}, u32[]{:S(2)}, u32[]{:S(2)}) async-start(bf16[16,192,128]{2,1,0:T(8,128)(2,1)} %get-tuple-element.14), calls=%async_computation.1 | async-start | bytes 1572864 | tf_op jit(solution)/shard_map/all_to_all | solution.py:330
  71.5 0.1 slice.15
  71.6 0.0 copy-start.6
  71.6 0.0 copy-start.7
  71.6 3.5 %collective-permute-start = (bf16[16,192,128]{2,1,0:T(8,128)(2,1)S(1)}, bf16[16,192,128]{2,1,0:T(8,128)(2,1)S(1)}, u32[]{:S(2)}, u32[]{:S(2)}) collective-permute-start(bf16[16,192,128]{2,1,0:T(8,128)(2,1)S(1)} %slice.15), channel_id=1, source_target_pairs={{0,16},{16,32},{32,48},{48,0},{1,17},{17,33},{33,49},{49,1},{2,18}... | collective-permute-start | bytes 2359304 | tf_op jit(solution)/shard_map/ppermute | solution.py:319
  75.2 3.7 %collective-permute-start.1 = (bf16[16,192,128]{2,1,0:T(8,128)(2,1)S(1)}, bf16[16,192,128]{2,1,0:T(8,128)(2,1)S(1)}, u32[]{:S(2)}, u32[]{:S(2)}) collective-permute-start(bf16[16,192,128]{2,1,0:T(8,128)(2,1)S(1)} %slice.15), channel_id=1, source_target_pairs={{0,48},{16,0},{32,16},{48,32},{1,49},{17,1},{33,17},{49,33},{2,50}... | collective-permute-start | bytes 2359304 | tf_op jit(solution)/shard_map/ppermute | solution.py:319
  78.8 15.2 %collective-permute-done.k1 = bf16[16,192,128]{2,1,0:T(8,128)(2,1)S(1)} collective-permute-done((bf16[16,192,128]{2,1,0:T(8,128)(2,1)S(1)}, bf16[16,192,128]{2,1,0:T(8,128)(2,1)S(1)}, u32[]{:S(2)}, u32[]{:S(2)}) %collective-permute-start) | collective-permute-done | bytes 786464 | tf_op jit(solution)/shard_map/ppermute | solution.py:319
  94.0 0.8 slice.20
  94.8 2.2 collective-permute-start.2
  97.0 0.0 collective-permute-done.1.k2
  97.0 0.9 copy-done.12
  97.9 0.8 slice.21
  98.7 4.9 %collective-permute-start.3 = (bf16[8,192,128]{2,1,0:T(8,128)(2,1)}, bf16[8,192,128]{2,1,0:T(8,128)(2,1)}, u32[]{:S(2)}, u32[]{:S(2)}) collective-permute-start(bf16[8,192,128]{2,1,0:T(8,128)(2,1)} %slice.21), channel_id=1, source_target_pairs={{0,48},{16,0},{32,16},{48,32},{1,49},{17,1},{33,17},{49,33},{2,50}... | collective-permute-start | bytes 1179656 | tf_op jit(solution)/shard_map/ppermute | solution.py:319
  104.2 0.1 pad_add_fusion.info
  104.3 3.8 %collective-permute-done.2.k3 = bf16[8,192,128]{2,1,0:T(8,128)(2,1)} collective-permute-done((bf16[8,192,128]{2,1,0:T(8,128)(2,1)}, bf16[8,192,128]{2,1,0:T(8,128)(2,1)}, u32[]{:S(2)}, u32[]{:S(2)}) %collective-permute-start.2) | collective-permute-done | bytes 393248 | tf_op jit(solution)/shard_map/ppermute | solution.py:319
  108.1 2.8 %collective-permute-done.3.k4 = bf16[8,192,128]{2,1,0:T(8,128)(2,1)} collective-permute-done((bf16[8,192,128]{2,1,0:T(8,128)(2,1)}, bf16[8,192,128]{2,1,0:T(8,128)(2,1)}, u32[]{:S(2)}, u32[]{:S(2)}) %collective-permute-start.3) | collective-permute-done | bytes 393248 | tf_op jit(solution)/shard_map/ppermute | solution.py:319
  110.9 6.1 %shard_map.137 = bf16[16,128,128]{2,1,0:T(8,128)(2,1)} custom-call(s32[4]{0:T(128)S(1)} %pad_add_fusion.info, bf16[16,224,128]{2,1,0:T(8,128)(2,1)} %copy-done.10, bf16[16,192,128]{2,1,0:T(8,128)(2,1)S(1)} %collective-permute-done.k1, bf16[16,192,128]{2,1,0:T(8,128)(2,1)} %copy-done.12, bf16[8,192,128]{2,1,0:T(8,128)(2,1)} %collective-permute-done.2.k3, ...), custom_call_target="tpu_custom_call" | custom-call | flops 2617245696 | bytes 3145728 | tf_op jit(solution)/shard_map/pallas_call | solution.py:170
  117.0 0.0 all-to-all-done.1.k0
  117.0 11.4 %all-to-all-start.2 = ((bf16[16,128,128]{2,1,0:T(8,128)(2,1)}), bf16[16,128,128]{2,1,0:T(8,128)(2,1)S(1)}, u32[]{:S(2)}, u32[]{:S(2)}) async-start(bf16[16,128,128]{2,1,0:T(8,128)(2,1)} %shard_map.137), calls=%async_computation.2 | async-start | bytes 1048576 | tf_op jit(solution)/shard_map/all_to_all | solution.py:330
  128.4 2.9 %collective-permute-start.4 = (bf16[16,192,128]{2,1,0:T(8,128)(2,1)S(1)}, bf16[16,192,128]{2,1,0:T(8,128)(2,1)S(1)}, u32[]{:S(2)}, u32[]{:S(2)}) collective-permute-start(bf16[16,192,128]{2,1,0:T(8,128)(2,1)S(1)} %all-to-all-done.1.k0), channel_id=1, source_target_pairs={{0,16},{16,32},{32,48},{48,0},{1,17},{17,33},{33,49},{49,1},{2,18}... | collective-permute-start | bytes 2359304 | tf_op jit(solution)/shard_map/ppermute | solution.py:319
  131.4 4.6 %collective-permute-start.5 = (bf16[16,192,128]{2,1,0:T(8,128)(2,1)S(1)}, bf16[16,192,128]{2,1,0:T(8,128)(2,1)S(1)}, u32[]{:S(2)}, u32[]{:S(2)}) collective-permute-start(bf16[16,192,128]{2,1,0:T(8,128)(2,1)S(1)} %all-to-all-done.1.k0), channel_id=1, source_target_pairs={{0,48},{16,0},{32,16},{48,32},{1,49},{17,1},{33,17},{49,33},{2,50}... | collective-permute-start | bytes 2359304 | tf_op jit(solution)/shard_map/ppermute | solution.py:319
  136.0 12.8 %collective-permute-done.4.k1 = bf16[16,192,128]{2,1,0:T(8,128)(2,1)S(1)} collective-permute-done((bf16[16,192,128]{2,1,0:T(8,128)(2,1)S(1)}, bf16[16,192,128]{2,1,0:T(8,128)(2,1)S(1)}, u32[]{:S(2)}, u32[]{:S(2)}) %collective-permute-start.4) | collective-permute-done | bytes 786464 | tf_op jit(solution)/shard_map/ppermute | solution.py:319
  148.8 1.9 collective-permute-start.6
  150.8 5.1 %collective-permute-start.7 = (bf16[8,192,128]{2,1,0:T(8,128)(2,1)S(1)}, bf16[8,192,128]{2,1,0:T(8,128)(2,1)S(1)}, u32[]{:S(2)}, u32[]{:S(2)}) collective-permute-start(bf16[8,192,128]{2,1,0:T(8,128)(2,1)S(1)} %slice.23), channel_id=1, source_target_pairs={{0,48},{16,0},{32,16},{48,32},{1,49},{17,1},{33,17},{49,33},{2,50}... | collective-permute-start | bytes 1179656 | tf_op jit(solution)/shard_map/ppermute | solution.py:319
  156.0 3.7 %collective-permute-done.6.k3 = bf16[8,192,128]{2,1,0:T(8,128)(2,1)S(1)} collective-permute-done((bf16[8,192,128]{2,1,0:T(8,128)(2,1)S(1)}, bf16[8,192,128]{2,1,0:T(8,128)(2,1)S(1)}, u32[]{:S(2)}, u32[]{:S(2)}) %collective-permute-start.6) | collective-permute-done | bytes 393248 | tf_op jit(solution)/shard_map/ppermute | solution.py:319
  159.7 1.5 collective-permute-done.7.k4
  161.2 0.7 copy-done.8
  162.0 0.0 all-to-all-done.2.q_ref.shared_ref
  162.0 1.0 copy-done.9
  163.0 16.5 %shard_map.138 = bf16[16,96,128]{2,1,0:T(8,128)(2,1)} custom-call(s32[4]{0:T(128)S(1)} %pad_add_fusion.info, bf16[16,128,128]{2,1,0:T(8,128)(2,1)S(1)} %all-to-all-done.2.q_ref.shared_ref, bf16[16,192,128]{2,1,0:T(8,128)(2,1)S(1)} %all-to-all-done.1.k0, bf16[16,192,128]{2,1,0:T(8,128)(2,1)} %copy-done.13, bf16[16,192,128]{2,1,0:T(8,128)(2,1)} %copy-done.14, ...), custom_call_target="tpu_custom_call" | custom-call | flops 10468982784 | bytes 3145728 | tf_op jit(solution)/shard_map/pallas_call | solution.py:156
  179.5 11.8 %all-to-all-start.3 = ((bf16[16,96,128]{2,1,0:T(8,128)(2,1)}), bf16[16,96,128]{2,1,0:T(8,128)(2,1)S(1)}, u32[]{:S(2)}, u32[]{:S(2)}) async-start(bf16[16,96,128]{2,1,0:T(8,128)(2,1)} %shard_map.138), calls=%async_computation.3 | async-start | bytes 786432 | tf_op jit(solution)/shard_map/all_to_all | solution.py:330
  191.3 0.0 copy-start.16
  191.4 0.7 copy-done.16
  192.1 0.3 copy.15.weight_ref
  192.4 0.0 copy-start.5
  192.4 17.0 %all-to-all-done.3.back_ref = bf16[16,96,128]{2,1,0:T(8,128)(2,1)S(1)} async-done(((bf16[16,96,128]{2,1,0:T(8,128)(2,1)}), bf16[16,96,128]{2,1,0:T(8,128)(2,1)S(1)}, u32[]{:S(2)}, u32[]{:S(2)}) %all-to-all-start.3) | async-done | bytes 393248 | tf_op jit(solution)/shard_map/all_to_all | solution.py:330
  209.5 0.7 shard_map.139
  210.2 20.5 %all_to_all.31.line_ref = bf16[16,48,128]{2,1,0:T(8,128)(2,1)S(1)} all-to-all(bf16[16,48,128]{2,1,0:T(8,128)(2,1)S(1)} %shard_map.139), channel_id=1, replica_groups=mesh['clip'=8,'x'=4,'zh'=4,'zl'=4] {'zh','zl'}, dimensions={0} | all-to-all | bytes 393216 | tf_op jit(solution)/shard_map/all_to_all | solution.py:330
  230.7 1.4 shard_map.140
  232.1 4.6 %all-to-all-start.5 = ((bf16[4,4,72,128]{3,2,1,0:T(8,128)(2,1)}), bf16[4,4,72,128]{3,2,1,0:T(8,128)(2,1)S(1)}, u32[]{:S(2)}, u32[]{:S(2)}) async-start(bf16[4,4,72,128]{3,2,1,0:T(8,128)(2,1)} %shard_map.140), calls=%async_computation.5 | async-start | bytes 589824 | tf_op jit(solution)/shard_map/all_to_all | solution.py:330
  236.7 0.7 copy-done.18
  237.4 6.2 %all-to-all-done.5 = bf16[4,4,72,128]{3,2,1,0:T(8,128)(2,1)S(1)} async-done(((bf16[4,4,72,128]{3,2,1,0:T(8,128)(2,1)}), bf16[4,4,72,128]{3,2,1,0:T(8,128)(2,1)S(1)}, u32[]{:S(2)}, u32[]{:S(2)}) %all-to-all-start.5) | async-done | bytes 294944 | tf_op jit(solution)/shard_map/all_to_all | solution.py:330
  243.5 2.6 %shard_map.141 = bf16[8,48,384]{2,1,0:T(8,128)(2,1)} custom-call(s32[4]{0:T(128)S(1)} %pad_add_fusion.info, s32[16]{0:T(128)S(1)} %copy-done.4, bf16[16,72,128]{2,1,0:T(8,128)(2,1)S(1)} %bitcast.6, bf16[432,384]{1,0:T(8,128)(2,1)S(1)} %copy-done.3, f32[1,384]{1,0:T(1,128)S(1)} %broadcast_in_dim.21.bias_ref, f32[1,384]{1,0:T(1,128)S(1)} %broadcast_in_dim.22.gain_ref), custom_call_target="tpu_custom_call" | custom-call | tf_op jit(solution)/shard_map/pallas_call | solution.py:305
  (33 shorter events, 0.1 us)
Async XLA Ops:
  0.0 1.0 copy-start
  1.0 1.0 copy-start.1
  2.1 1.0 copy-start.2
  65.9 5.6 %copy-start.10 = (bf16[16,224,128]{2,1,0:T(8,128)(2,1)}, bf16[16,224,128]{2,1,0:T(8,128)(2,1)S(1)}, u32[]{:S(2)}) copy-start(bf16[16,224,128]{2,1,0:T(8,128)(2,1)S(1)} %all_to_all.30.s_ref) | copy-start | bytes 2752516
  65.9 51.1 %all-to-all-start.1 = ((bf16[16,192,128]{2,1,0:T(8,128)(2,1)}), bf16[16,192,128]{2,1,0:T(8,128)(2,1)S(1)}, u32[]{:S(2)}, u32[]{:S(2)}) async-start(bf16[16,192,128]{2,1,0:T(8,128)(2,1)} %get-tuple-element.14), calls=%async_computation.1 | async-start | bytes 1572864 | tf_op jit(solution)/shard_map/all_to_all | solution.py:330
  71.6 39.3 %copy-start.6 = (bf16[512,640]{1,0:T(8,128)(2,1)S(1)}, bf16[512,640]{1,0:T(8,128)(2,1)}, u32[]{:S(2)}) copy-start(bf16[512,640]{1,0:T(8,128)(2,1)} %tk_ref.3) | copy-start | bytes 1966084
  71.6 39.3 %copy-start.7 = (bf16[512,640]{1,0:T(8,128)(2,1)S(1)}, bf16[512,640]{1,0:T(8,128)(2,1)}, u32[]{:S(2)}) copy-start(bf16[512,640]{1,0:T(8,128)(2,1)} %tv_ref.3) | copy-start | bytes 1966084
  71.6 22.4 %collective-permute-start = (bf16[16,192,128]{2,1,0:T(8,128)(2,1)S(1)}, bf16[16,192,128]{2,1,0:T(8,128)(2,1)S(1)}, u32[]{:S(2)}, u32[]{:S(2)}) collective-permute-start(bf16[16,192,128]{2,1,0:T(8,128)(2,1)S(1)} %slice.15), channel_id=1, source_target_pairs={{0,16},{16,32},{32,48},{48,0},{1,17},{17,33},{33,49},{49,1},{2,18}... | collective-permute-start | bytes 2359304 | tf_op jit(solution)/shard_map/ppermute | solution.py:319
  75.2 21.8 %collective-permute-start.1 = (bf16[16,192,128]{2,1,0:T(8,128)(2,1)S(1)}, bf16[16,192,128]{2,1,0:T(8,128)(2,1)S(1)}, u32[]{:S(2)}, u32[]{:S(2)}) collective-permute-start(bf16[16,192,128]{2,1,0:T(8,128)(2,1)S(1)} %slice.15), channel_id=1, source_target_pairs={{0,48},{16,0},{32,16},{48,32},{1,49},{17,1},{33,17},{49,33},{2,50}... | collective-permute-start | bytes 2359304 | tf_op jit(solution)/shard_map/ppermute | solution.py:319
  94.8 13.3 %collective-permute-start.2 = (bf16[8,192,128]{2,1,0:T(8,128)(2,1)}, bf16[8,192,128]{2,1,0:T(8,128)(2,1)}, u32[]{:S(2)}, u32[]{:S(2)}) collective-permute-start(bf16[8,192,128]{2,1,0:T(8,128)(2,1)} %slice.20), channel_id=1, source_target_pairs={{0,16},{16,32},{32,48},{48,0},{1,17},{17,33},{33,49},{49,1},{2,18}... | collective-permute-start | bytes 1179656 | tf_op jit(solution)/shard_map/ppermute | solution.py:319
  97.0 0.9 copy-start.12
  98.7 12.3 %collective-permute-start.3 = (bf16[8,192,128]{2,1,0:T(8,128)(2,1)}, bf16[8,192,128]{2,1,0:T(8,128)(2,1)}, u32[]{:S(2)}, u32[]{:S(2)}) collective-permute-start(bf16[8,192,128]{2,1,0:T(8,128)(2,1)} %slice.21), channel_id=1, source_target_pairs={{0,48},{16,0},{32,16},{48,32},{1,49},{17,1},{33,17},{49,33},{2,50}... | collective-permute-start | bytes 1179656 | tf_op jit(solution)/shard_map/ppermute | solution.py:319
  117.0 45.0 %all-to-all-start.2 = ((bf16[16,128,128]{2,1,0:T(8,128)(2,1)}), bf16[16,128,128]{2,1,0:T(8,128)(2,1)S(1)}, u32[]{:S(2)}, u32[]{:S(2)}) async-start(bf16[16,128,128]{2,1,0:T(8,128)(2,1)} %shard_map.137), calls=%async_computation.2 | async-start | bytes 1048576 | tf_op jit(solution)/shard_map/all_to_all | solution.py:330
  128.4 20.3 %collective-permute-start.4 = (bf16[16,192,128]{2,1,0:T(8,128)(2,1)S(1)}, bf16[16,192,128]{2,1,0:T(8,128)(2,1)S(1)}, u32[]{:S(2)}, u32[]{:S(2)}) collective-permute-start(bf16[16,192,128]{2,1,0:T(8,128)(2,1)S(1)} %all-to-all-done.1.k0), channel_id=1, source_target_pairs={{0,16},{16,32},{32,48},{48,0},{1,17},{17,33},{33,49},{49,1},{2,18}... | collective-permute-start | bytes 2359304 | tf_op jit(solution)/shard_map/ppermute | solution.py:319
  131.4 19.4 %collective-permute-start.5 = (bf16[16,192,128]{2,1,0:T(8,128)(2,1)S(1)}, bf16[16,192,128]{2,1,0:T(8,128)(2,1)S(1)}, u32[]{:S(2)}, u32[]{:S(2)}) collective-permute-start(bf16[16,192,128]{2,1,0:T(8,128)(2,1)S(1)} %all-to-all-done.1.k0), channel_id=1, source_target_pairs={{0,48},{16,0},{32,16},{48,32},{1,49},{17,1},{33,17},{49,33},{2,50}... | collective-permute-start | bytes 2359304 | tf_op jit(solution)/shard_map/ppermute | solution.py:319
  148.8 2.0 copy-start.13
  148.8 10.9 %collective-permute-start.6 = (bf16[8,192,128]{2,1,0:T(8,128)(2,1)S(1)}, bf16[8,192,128]{2,1,0:T(8,128)(2,1)S(1)}, u32[]{:S(2)}, u32[]{:S(2)}) collective-permute-start(bf16[8,192,128]{2,1,0:T(8,128)(2,1)S(1)} %slice.22), channel_id=1, source_target_pairs={{0,16},{16,32},{32,48},{48,0},{1,17},{17,33},{33,49},{49,1},{2,18}... | collective-permute-start | bytes 1179656 | tf_op jit(solution)/shard_map/ppermute | solution.py:319
  150.8 8.9 %copy-start.14 = (bf16[16,192,128]{2,1,0:T(8,128)(2,1)}, bf16[16,192,128]{2,1,0:T(8,128)(2,1)S(1)}, u32[]{:S(2)}) copy-start(bf16[16,192,128]{2,1,0:T(8,128)(2,1)S(1)} %collective-permute-done.5.k2) | copy-start | bytes 2359300
  150.8 10.4 %collective-permute-start.7 = (bf16[8,192,128]{2,1,0:T(8,128)(2,1)S(1)}, bf16[8,192,128]{2,1,0:T(8,128)(2,1)S(1)}, u32[]{:S(2)}, u32[]{:S(2)}) collective-permute-start(bf16[8,192,128]{2,1,0:T(8,128)(2,1)S(1)} %slice.23), channel_id=1, source_target_pairs={{0,48},{16,0},{32,16},{48,32},{1,49},{17,1},{33,17},{49,33},{2,50}... | collective-permute-start | bytes 1179656 | tf_op jit(solution)/shard_map/ppermute | solution.py:319
  161.2 0.7 copy-start.8
  162.0 1.0 copy-start.9
  179.5 11.8 %copy-start.15 = (f32[2560]{0:T(1024)S(1)}, f32[2560]{0:T(1024)}, u32[]{:S(2)}) copy-start(f32[2560]{0:T(1024)} %param.21) | copy-start | bytes 30724
  179.5 12.6 %copy-start.11 = (bf16[2560,64]{0,1:T(8,128)(2,1)S(1)}, bf16[2560,64]{0,1:T(8,128)(2,1)}, u32[]{:S(2)}) copy-start(bf16[2560,64]{0,1:T(8,128)(2,1)} %param.23) | copy-start | bytes 983044
  179.5 29.9 %all-to-all-start.3 = ((bf16[16,96,128]{2,1,0:T(8,128)(2,1)}), bf16[16,96,128]{2,1,0:T(8,128)(2,1)S(1)}, u32[]{:S(2)}, u32[]{:S(2)}) async-start(bf16[16,96,128]{2,1,0:T(8,128)(2,1)} %shard_map.138), calls=%async_computation.3 | async-start | bytes 786432 | tf_op jit(solution)/shard_map/all_to_all | solution.py:330
  191.3 0.7 copy-start.16
  192.4 17.0 %copy-start.5 = (f32[64]{0:T(128)S(1)}, f32[64]{0:T(128)}, u32[]{:S(2)}) copy-start(f32[64]{0:T(128)} %param.24) | copy-start | bytes 772
  232.1 4.6 %copy-start.17 = (f32[384]{0:T(512)S(1)}, f32[384]{0:T(512)}, u32[]{:S(2)}) copy-start(f32[384]{0:T(512)} %param.26) | copy-start | bytes 4612
  232.1 11.5 %copy-start.3 = (bf16[432,384]{1,0:T(8,128)(2,1)S(1)}, bf16[432,384]{1,0:T(8,128)(2,1)}, u32[]{:S(2)}) copy-start(bf16[432,384]{1,0:T(8,128)(2,1)} %weight_ref.2) | copy-start | bytes 995332
  232.1 11.5 %all-to-all-start.5 = ((bf16[4,4,72,128]{3,2,1,0:T(8,128)(2,1)}), bf16[4,4,72,128]{3,2,1,0:T(8,128)(2,1)S(1)}, u32[]{:S(2)}, u32[]{:S(2)}) async-start(bf16[4,4,72,128]{3,2,1,0:T(8,128)(2,1)} %shard_map.140), calls=%async_computation.5 | async-start | bytes 589824 | tf_op jit(solution)/shard_map/all_to_all | solution.py:330
  236.7 0.7 copy-start.18
  237.4 6.2 %copy-start.4 = (s32[16]{0:T(128)S(1)}, s32[16]{0:T(128)}, u32[]{:S(2)}) copy-start(s32[16]{0:T(128)} %tile_map.1) | copy-start | bytes 196

commit v3 on v2

--- a/solution.py
+++ b/solution.py
@@ -38,143 +38,258 @@
 SLOT = 32
 
 
-def pack_kernel(q_ref, k_ref, v_ref, shared_out, kv_out, q_out):
+def load_kernel(q_hbm, k_hbm, v_hbm, main_out, kv_out, q_out, q_ref, k_ref, v_ref, sems):
+    width = 5 * HDIM
+    copies = []
     for zl in range(4):
+        span = slice(zl * width, (zl + 1) * width)
+        for index, (source, target) in enumerate(((k_hbm, k_ref), (v_hbm, v_ref), (q_hbm, q_ref))):
+            copy = pltpu.make_async_copy(
+                source.at[:, span], target.at[:, span], sems.at[3 * zl + index]
+            )
+            copy.start()
+            copies.append(copy)
+    for zl in range(4):
+        for copy in copies[3 * zl : 3 * zl + 3]:
+            copy.wait()
         last = slice((5 * zl + 4) * HDIM, (5 * zl + 5) * HDIM)
-        queries_last = q_ref[:, last].astype(F32)
+        q_out[zl] = q_ref[:, last]
+        kv_out[zl, 0:ROWS, :] = k_ref[:, last]
+        kv_out[zl, ROWS : 2 * ROWS, :] = v_ref[:, last]
+        for index, ref in enumerate((k_ref, v_ref, q_ref)):
+            rows = slice(index * ROWS, (index + 1) * ROWS)
+            for zh in range(4):
+                own = slice((5 * zl + zh) * HDIM, (5 * zl + zh + 1) * HDIM)
+                main_out[zh * 4 + zl, rows, :] = ref[:, own]
+
+
+def load(queries, keys, values):
+    return pl.pallas_call(
+        load_kernel,
+        out_shape=(
+            jax.ShapeDtypeStruct((NZ, 3 * ROWS, HDIM), BF),
+            jax.ShapeDtypeStruct((4, 2 * ROWS, HDIM), BF),
+            jax.ShapeDtypeStruct((4, ROWS, HDIM), BF),
+        ),
+        in_specs=[pl.BlockSpec(memory_space=pl.ANY)] * 3,
+        out_specs=(vmem(),) * 3,
+        scratch_shapes=[pltpu.VMEM((ROWS, 20 * HDIM), BF)] * 3
+        + [pltpu.SemaphoreType.DMA((12,))],
+        compiler_params=pltpu.CompilerParams(vmem_limit_bytes=60 * 1024 * 1024),
+    )(queries, keys, values)
+
+
+def pack_kernel(kv_ref, q0, q1, q2, q3, out_ref):
+    for zl in range(4):
+        columns = [ref[zl].astype(F32) for ref in (q0, q1, q2, q3)]
         for zh in range(4):
-            z = zh * 4 + zl
-            own = slice((5 * zl + zh) * HDIM, (5 * zl + zh + 1) * HDIM)
-            shared_out[z, 0:ROWS, :] = k_ref[:, last]
-            shared_out[z, ROWS : 2 * ROWS, :] = v_ref[:, last]
-            part = queries_last[PART * zh : PART * (zh + 1)]
-            shared_out[z, 2 * ROWS : 2 * ROWS + SLOT, :] = jnp.concatenate(
-                [part, jnp.zeros((SLOT - PART, HDIM), F32)], axis=0
+            out_ref[zh * 4 + zl, 0 : 2 * ROWS, :] = kv_ref[zl]
+            span = slice(PART * zh, PART * (zh + 1))
+            out_ref[zh * 4 + zl, 2 * ROWS : 3 * ROWS, :] = jnp.concatenate(
+                [column[span] for column in columns], axis=0
             ).astype(BF)
-            kv_out[z, 0:ROWS, :] = k_ref[:, own]
-            kv_out[z, ROWS : 2 * ROWS, :] = v_ref[:, own]
-            q_out[z] = q_ref[:, own]
-
-
-def pack(queries, keys, values):
+
+
+def pack(kv, columns):
     return pl.pallas_call(
         pack_kernel,
-        out_shape=(
-            jax.ShapeDtypeStruct((NZ, 2 * ROWS + SLOT, HDIM), BF),
-            jax.ShapeDtypeStruct((NZ, 2 * ROWS, HDIM), BF),
-            jax.ShapeDtypeStruct((NZ, ROWS, HDIM), BF),
-        ),
-        in_specs=[vmem()] * 3,
-        out_specs=(vmem(),) * 3,
-        compiler_params=params(),
-    )(queries, keys, values)
+        out_shape=jax.ShapeDtypeStruct((NZ, 3 * ROWS, HDIM), BF),
+        in_specs=[vmem()] * 5,
+        out_specs=vmem(),
+        compiler_params=params(),
+    )(kv, *columns)
 
 
 def dot_t(a, b):
     return lax.dot_general(a, b, (((1,), (1,)), ((), ())), preferred_element_type=F32)
 
 
-def attend(query, pieces, text_key, text_value, text_len):
-    ones = jnp.ones((HDIM, HDIM), BF)
-
-    def scores_of(piece):
-        ref, lo, hi = piece
-        return dot_t(query, ref[lo:hi, 0:ROWS, :].reshape((hi - lo) * ROWS, HDIM))
-
-    def row_peak(scores):
-        top = scores[:, :HDIM]
-        for col in range(HDIM, scores.shape[1], HDIM):
-            top = jnp.maximum(top, scores[:, col : col + HDIM])
-        return jnp.max(top, axis=-1, keepdims=True)
-
-    def widened(value):
-        return jnp.concatenate([value, jnp.tile(ones, (value.shape[0] // HDIM, 1))], axis=1)
-
-    peak, total = None, None
-    scores = scores_of(pieces[0])
-    for index, (ref, lo, hi) in enumerate(pieces):
-        later = scores_of(pieces[index + 1]) if index + 1 < len(pieces) else None
+def row_peak(scores):
+    top = scores[:, :HDIM]
+    for col in range(HDIM, scores.shape[1], HDIM):
+        top = jnp.maximum(top, scores[:, col : col + HDIM])
+    return jnp.max(top, axis=-1, keepdims=True)
+
+
+def widened(value):
+    return jnp.concatenate([value, jnp.ones(value.shape, BF)], axis=1)
+
+
+def absorb(query, pieces, peak, total):
+    def rows_of(piece, first):
+        parts = [
+            ref[lo:hi, first : first + ROWS, :].reshape((hi - lo) * ROWS, HDIM)
+            for ref, lo, hi in piece
+        ]
+        return parts[0] if len(parts) == 1 else jnp.concatenate(parts, axis=0)
+
+    scores = dot_t(query, rows_of(pieces[0], 0))
+    for index, piece in enumerate(pieces):
+        more = index + 1 < len(pieces)
+        later = dot_t(query, rows_of(pieces[index + 1], 0)) if more else None
         highest = row_peak(scores) * SCALE2
-        value = widened(ref[lo:hi, ROWS : 2 * ROWS, :].reshape((hi - lo) * ROWS, HDIM))
+        value = widened(rows_of(piece, ROWS))
         newest = highest if peak is None else jnp.maximum(peak, highest)
         weights = jnp.exp2(scores * SCALE2 - newest).astype(BF)
         part = jnp.dot(weights, value, preferred_element_type=F32)
         total = part if peak is None else total * jnp.exp2(peak - newest) + part
         peak, scores = newest, later
-    self_out = total[:, :HDIM] / total[:, HDIM:]
+    return peak, total
+
+
+def text_part(query, text_key, text_value, text_len):
     text_scores = dot_t(query, text_key) * SCALE2
     usable = lax.broadcasted_iota(jnp.int32, text_scores.shape, 1) < text_len
     text_scores = jnp.where(usable, text_scores, -1e30)
     text_peak = row_peak(text_scores)
     text_weights = jnp.where(usable, jnp.exp2(text_scores - text_peak), 0.0).astype(BF)
     text_total = jnp.dot(text_weights, widened(text_value), preferred_element_type=F32)
-    return self_out + text_total[:, :HDIM] / text_total[:, HDIM:]
+    return text_total[:, :HDIM] / text_total[:, HDIM:]
 
 
 def pieces_of(refs):
     pieces = []
     for ref in refs:
-        count = ref.shape[0]
-        for lo in range(0, count, 8):
-            pieces.append((ref, lo, min(lo + 8, count)))
+        for lo in range(0, ref.shape[0], 8):
+            part = (ref, lo, min(lo + 8, ref.shape[0]))
+            if pieces and sum(hi - lo for _, lo, hi in pieces[-1]) < 8:
+                pieces[-1].append(part)
+            else:
+                pieces.append([part])
     return pieces
 
 
-def main_kernel(info, q_ref, k0, k1, k2, k3, k4, tk_ref, tv_ref, out_ref):
-    query = q_ref[:, 0:ROWS, :].reshape(4 * ROWS, HDIM)
+def first_kernel(q_ref, k0, k1, k2, total_ref, state_ref):
+    query = q_ref[...].reshape(4 * ROWS, HDIM)
+    peak, total = absorb(query, pieces_of((k0, k1, k2)), None, None)
+    total_ref[...] = total[:, :HDIM]
+    lane = lax.broadcasted_iota(jnp.int32, (4 * ROWS, HDIM), 1)
+    state_ref[...] = jnp.where(lane < 64, peak, total[:, HDIM:])
+
+
+def second_kernel(info, q_ref, total_ref, state_ref, k3, k4, tk_ref, tv_ref, out_ref):
+    query = q_ref[...].reshape(4 * ROWS, HDIM)
     column = pl.ds(pl.multiple_of(info[0] * HDIM, HDIM), HDIM)
-    pieces = pieces_of((k0, k1, k2, k3, k4))
-    result = attend(query, pieces, tk_ref[:, column], tv_ref[:, column], info[1])
+    state = state_ref[...]
+    peak = state[:, 0:1]
+    weight = jnp.broadcast_to(state[:, HDIM - 1 : HDIM], (4 * ROWS, HDIM))
+    total = jnp.concatenate([total_ref[...], weight], axis=1)
+    peak, total = absorb(query, pieces_of((k3, k4)), peak, total)
+    result = total[:, :HDIM] / total[:, HDIM:]
+    result = result + text_part(query, tk_ref[:, column], tv_ref[:, column], info[1])
     out_ref[...] = result.astype(BF).reshape(4, ROWS, HDIM)
 
 
-def shared_kernel(info, s_ref, k1, k2, k3, k4, tk_ref, tv_ref, q_ref, out_ref):
-    query = s_ref[:, 2 * ROWS : 2 * ROWS + SLOT, :].astype(F32)[:, :PART]
-    query = query.reshape(NZ * PART, HDIM).astype(BF)
+def shared_kernel(s_ref, p0, p1, p2, p3):
+    rows = NZ * PART
+    lane = lax.broadcasted_iota(jnp.int32, (rows, HDIM), 1)
+    queries = s_ref[:, 2 * ROWS : 3 * ROWS, :].astype(F32)
+    for column, out_ref in enumerate((p0, p1, p2, p3)):
+        query = queries[:, PART * column : PART * (column + 1)].reshape(rows, HDIM).astype(BF)
+        peak, total = absorb(query, pieces_of((s_ref,)), None, None)
+        out_ref[:, 0:HDIM] = (total[:, :HDIM] / total[:, HDIM:]).astype(BF)
+        level = peak + jnp.log2(total[:, HDIM:])
+        high = level.astype(BF).astype(F32)
+        middle = (level - high).astype(BF).astype(F32)
+        low = level - high - middle
+        terms = jnp.where(lane == 0, high, jnp.where(lane == 1, middle, low))
+        out_ref[:, HDIM:] = terms.astype(BF)
+
+
+def merge_kernel(info, s_ref, p0, p1, p2, p3, tk_ref, tv_ref, out_ref):
+    rows = NZ * PART
+    query = s_ref[:, 2 * ROWS : 3 * ROWS, :].astype(F32)[:, :PART]
+    query = query.reshape(rows, HDIM).astype(BF)
+    levels = []
+    for ref in (p0, p1, p2, p3):
+        terms = ref[:, HDIM:].astype(F32)
+        levels.append(terms[:, 0:1] + terms[:, 1:2] + terms[:, 2:3])
+    top = functools.reduce(jnp.maximum, levels)
+    weights = [jnp.exp2(level - top) for level in levels]
+    result = sum(
+        weight * ref[:, 0:HDIM].astype(F32) for weight, ref in zip(weights, (p0, p1, p2, p3))
+    ) / sum(weights)
     column = slice(4 * HDIM, 5 * HDIM)
-    pieces = pieces_of((s_ref, k1, k2, k3, k4))
-    result = attend(query, pieces, tk_ref[:, column], tv_ref[:, column], info[1])
+    result = result + text_part(query, tk_ref[:, column], tv_ref[:, column], info[1])
     filler = jnp.zeros((NZ, SLOT - PART, HDIM), F32)
-    result = jnp.concatenate([result.reshape(NZ, PART, HDIM), filler], axis=1)
-    out_ref[:, 0:ROWS, :] = q_ref[...]
-    out_ref[:, ROWS : ROWS + SLOT, :] = result.astype(BF)
+    out_ref[...] = jnp.concatenate([result.reshape(NZ, PART, HDIM), filler], axis=1).astype(BF)
 
 
 KEYS = 6144
 
 
-def cost(rows):
+def cost(rows, keys):
     return pl.CostEstimate(
-        flops=rows * (KEYS + TXT) * HDIM * 8,
-        bytes_accessed=2 * KEYS * HDIM * 2,
-        transcendentals=rows * (KEYS + TXT),
+        flops=rows * keys * HDIM * 8,
+        bytes_accessed=2 * keys * HDIM * 2,
+        transcendentals=rows * keys,
     )
 
 
-def main_attention(info, queries, kv, text_keys, text_values):
-    whole = lambda a: pl.BlockSpec(a.shape, lambda i, n=a.ndim: (0,) * n)
-    return pl.pallas_call(
-        main_kernel,
+def whole(array):
+    return pl.BlockSpec(array.shape, lambda i: (0,) * array.ndim)
+
+
+def main_first(queries, kv):
+    rows = 4 * ROWS
+    return pl.pallas_call(
+        first_kernel,
+        grid=(NZ // 4,),
+        out_shape=(
+            jax.ShapeDtypeStruct((NZ * ROWS, HDIM), F32),
+            jax.ShapeDtypeStruct((NZ * ROWS, HDIM), F32),
+        ),
+        in_specs=[pl.BlockSpec((4, ROWS, HDIM), lambda i: (i, 2, 0))] + [whole(a) for a in kv],
+        out_specs=(
+            pl.BlockSpec((rows, HDIM), lambda i: (i, 0)),
+            pl.BlockSpec((rows, HDIM), lambda i: (i, 0)),
+        ),
+        compiler_params=params(),
+        cost_estimate=cost(NZ * ROWS, 4608),
+    )(queries, *kv)
+
+
+def main_second(info, queries, total, state, kv, text_keys, text_values):
+    rows = 4 * ROWS
+    return pl.pallas_call(
+        second_kernel,
         grid=(NZ // 4,),
         out_shape=jax.ShapeDtypeStruct((NZ, ROWS, HDIM), BF),
-        in_specs=[smem(), pl.BlockSpec((4,) + queries.shape[1:], lambda i: (i, 0, 0))]
+        in_specs=[
+            smem(),
+            pl.BlockSpec((4, ROWS, HDIM), lambda i: (i, 2, 0)),
+            pl.BlockSpec((rows, HDIM), lambda i: (i, 0)),
+            pl.BlockSpec((rows, HDIM), lambda i: (i, 0)),
+        ]
         + [whole(a) for a in kv]
         + [whole(text_keys), whole(text_values)],
         out_specs=pl.BlockSpec((4, ROWS, HDIM), lambda i: (i, 0, 0)),
         compiler_params=params(),
-        cost_estimate=cost(NZ * ROWS),
-    )(info, queries, *kv, text_keys, text_values)
-
-
-def shared_attention(info, kv, text_keys, text_values, queries):
+        cost_estimate=cost(NZ * ROWS, 2048),
+    )(info, queries, total, state, *kv, text_keys, text_values)
+
+
+def shared_attention(shared):
+    part = jax.ShapeDtypeStruct((NZ * PART, 2 * HDIM), BF)
     return pl.pallas_call(
         shared_kernel,
-        out_shape=jax.ShapeDtypeStruct((NZ, ROWS + SLOT, HDIM), BF),
-        in_specs=[smem()] + [vmem()] * 8,
+        out_shape=(part,) * 4,
+        in_specs=[vmem()],
+        out_specs=(vmem(),) * 4,
+        compiler_params=params(),
+        cost_estimate=cost(NZ * ROWS, NZ * ROWS),
+    )(shared)
+
+
+def shared_merge(info, shared, parts, text_keys, text_values):
+    return pl.pallas_call(
+        merge_kernel,
+        out_shape=jax.ShapeDtypeStruct((NZ, SLOT, HDIM), BF),
+        in_specs=[smem()] + [vmem()] * 7,
         out_specs=vmem(),
         compiler_params=params(),
-        cost_estimate=cost(NZ * PART),
-    )(info, *kv, text_keys, text_values, queries)
+        cost_estimate=cost(NZ * PART, TXT),
+    )(info, shared, *parts, text_keys, text_values)
 
 
 def head_kernel(
@@ -186,10 +301,7 @@
         if zh < 4:
             block = back_ref[zh * 4 + zl].astype(F32)
         else:
-            parts = [
-                shared_ref[part * 4 + zl, ROWS : ROWS + SLOT, :].astype(F32)[:PART]
-                for part in range(4)
-            ]
+            parts = [shared_ref[part * 4 + zl].astype(F32)[:PART] for part in range(4)]
             block = jnp.concatenate(parts, axis=0)
         blocks.append(block)
     count = 20 * HDIM
@@ -348,17 +460,22 @@
 ):
     x, zh, zl = (lax.axis_index(axis) for axis in ("x", "zh", "zl"))
     info = jnp.stack([zh, text_len[0], x, zl]).astype(jnp.int32)
-    shared_send, kv_send, q_send = pack(queries, keys, values)
+    main_send, last_kv, last_q = load(queries, keys, values)
+    columns = [last_q] + [shift(last_q, "x", distance) for distance in (1, 2, 3)]
+    main = exchange(main_send, Z)
+    main, shared_send = lax.optimization_barrier((main, pack(last_kv, columns)))
     shared = exchange(shared_send, Z)
-    shared, kv_send = lax.optimization_barrier((shared, kv_send))
-    shared_kv = (shared,) + around(shared[:, : 2 * ROWS], "x")[1:]
-    kv = exchange(kv_send, Z)
-    third_send = shared_attention(info, shared_kv, text_keys, text_values, q_send)
-    kv, third_send = lax.optimization_barrier((kv, third_send))
-    main_kv = around(kv, "x")
-    third = exchange(third_send, Z)
-    back = exchange(main_attention(info, third, main_kv, text_keys, text_values), Z)
-    line = exchange(head(back, third, mod_gain, mod_shift, head_weight, head_bias), Z)
+    main_kv = (main,) + around(main[:, : 2 * ROWS], "x")[1:]
+    total, state = main_first(main, main_kv[:3])
+    out = main_second(info, main, total, state, main_kv[3:], text_keys, text_values)
+    out, shared = lax.optimization_barrier((out, shared))
+    back = exchange(out, Z)
+    parts = shared_attention(shared)
+    parts = [parts[0]] + [shift(parts[distance], "x", -distance) for distance in (1, 2, 3)]
+    merged = shared_merge(info, shared, parts, text_keys, text_values)
+    back, merged = lax.optimization_barrier((back, merged))
+    shared_back = exchange(merged, Z)
+    line = exchange(head(back, shared_back, mod_gain, mod_shift, head_weight, head_bias), Z)
     plane = exchange(slab_of(info, line), "x")
     gathered = plane.reshape(16, SLAB, HDIM)
     out = conv(info, tile_map, gathered, conv_weight, conv_bias, norm_gain)

time: 247 us -> 231 us (0.935)
  blocking collectives: 82.1 us -> 19.5 us
  waiting for transfers between devices: 63.2 us -> 88.3 us
  starting transfers between devices: 62.2 us -> 83.4 us
  local copies, waits for them, and re-layouts: 9.14 us -> 3.66 us
  Pallas kernels: 28.5 us -> 33.6 us
    all_to_all x2 -> x1, blocking collectives: 82.1 us -> 19.5 us  [exchange(): return lax.all_to_all(block, axis, split_axis=0, concat_axis=0, tiled=True)]
    all_to_all x4 -> x5, waiting for transfers between devices: 23.2 us -> 62.3 us  [exchange(): return lax.all_to_all(block, axis, split_axis=0, concat_axis=0, tiled=True)]
    all_to_all x4 -> x5, starting transfers between devices: 33.4 us -> 48.1 us  [exchange(): return lax.all_to_all(block, axis, split_axis=0, concat_axis=0, tiled=True)]
    ppermute x8 -> x10, waiting for transfers between devices: 40 us -> 26 us  [shift(): lax.ppermute(block, axis, [(i, (i + distance) % 4) for i in range(4)])]
    ppermute x8 -> x10, starting transfers between devices: 28.8 us -> 35.4 us  [shift(): lax.ppermute(block, axis, [(i, (i + distance) % 4) for i in range(4)])]
    pallas_call x3 -> x6, Pallas kernels: 23.8 us -> 28.9 us  [the longest x1 11.1 us: main_first(): pl.pallas_call(first_kernel, grid=(NZ // 4,), out_shape=(jax.ShapeDtypeSt...]
    unnamed x39 -> x35, local copies, waits for them, and re-layouts: 7.44 us -> 3.52 us
  transfers between devices with their start and end apart: 12 -> 15, of which waited for: 8 -> 9; matrix products, arithmetic and copies ran while one was open for 1% -> 0% of each run, Pallas kernels for 2% -> 11%
where the time goes in v3:
time: 231 us; the launch traced here: 230 us
  waiting for transfers between devices  88.3 us (38%)
  starting transfers between devices  83.4 us (36%)
  Pallas kernels  33.6 us (15%)
  blocking collectives  19.5 us (8%)
  local copies, waits for them, and re-layouts  3.66 us (2%)
    all_to_all x5, waiting for transfers between devices, exchange(): return lax.all_to_all(block, axis, split_axis=0, concat_axis=0, tiled=True)  62.3 us
    all_to_all x5, starting transfers between devices, exchange(): return lax.all_to_all(block, axis, split_axis=0, concat_axis=0, tiled=True)  48.1 us
    ppermute x10, starting transfers between devices, shift(): lax.ppermute(block, axis, [(i, (i + distance) % 4) for i in range(4)])  35.4 us
    ppermute x10, waiting for transfers between devices, shift(): lax.ppermute(block, axis, [(i, (i + distance) % 4) for i in range(4)])  26 us
    all_to_all x1, blocking collectives, exchange(): return lax.all_to_all(block, axis, split_axis=0, concat_axis=0, tiled=True)  19.5 us
    pallas_call x1, Pallas kernels, main_first(): pl.pallas_call(first_kernel, grid=(NZ // 4,), out_shape=(jax.ShapeDtypeSt...  11.1 us
    pallas_call x1, Pallas kernels, main_second(): pl.pallas_call(second_kernel, grid=(NZ // 4,), out_shape=jax.ShapeDtypeSt...  8.43 us
  transfers between devices with their start and end apart: 15, of which 9 were waited for; matrix products, arithmetic and copies ran while one was open for 0% of the time, Pallas kernels for 11%

profile of v3, /device:TPU:24, one launch (start us, length us, event | category | flops | bytes accessed | tf_op | source)
XLA Modules:
  0.0 229.6 jit_solution(17193883760639288282)
XLA Ops:
  0.0 2.7 %shard_map.136 = (bf16[16,288,128]{2,1,0:T(8,128)(2,1)}, bf16[4,192,128]{2,1,0:T(8,128)(2,1)}, bf16[4,96,128]{2,1,0:T(8,128)(2,1)}) custom-call(bf16[96,2560]{1,0:T(8,128)(2,1)} %q_hbm.1, bf16[96,2560]{1,0:T(8,128)(2,1)} %k_hbm.1, bf16[96,2560]{1,0:T(8,128)(2,1)} %v_hbm.1), custom_call_target="tpu_custom_call" | custom-call | tf_op jit(solution)/shard_map/pallas_call | solution.py:67
  2.7 0.0 copy-start.3
  2.7 15.3 %all-to-all-start = ((bf16[16,288,128]{2,1,0:T(8,128)(2,1)}), bf16[16,288,128]{2,1,0:T(8,128)(2,1)S(1)}, u32[]{:S(2)}, u32[]{:S(2)}) async-start(bf16[16,288,128]{2,1,0:T(8,128)(2,1)} %get-tuple-element.20), calls=%async_computation | async-start | bytes 2359296 | tf_op jit(solution)/shard_map/all_to_all | solution.py:442
  18.1 3.4 %collective-permute-start = (bf16[4,96,128]{2,1,0:T(8,128)(2,1)S(1)}, bf16[4,96,128]{2,1,0:T(8,128)(2,1)S(1)}, u32[]{:S(2)}, u32[]{:S(2)}) collective-permute-start(bf16[4,96,128]{2,1,0:T(8,128)(2,1)S(1)} %copy-done.8), channel_id=1, source_target_pairs={{0,16},{16,32},{32,48},{48,0},{1,17},{17,33},{33,49},{49,1},{2,18}... | collective-permute-start | bytes 294920 | tf_op jit(solution)/shard_map/ppermute | solution.py:431
  21.5 4.6 %collective-permute-start.1 = (bf16[4,96,128]{2,1,0:T(8,128)(2,1)S(1)}, bf16[4,96,128]{2,1,0:T(8,128)(2,1)S(1)}, u32[]{:S(2)}, u32[]{:S(2)}) collective-permute-start(bf16[4,96,128]{2,1,0:T(8,128)(2,1)S(1)} %copy-done.8), channel_id=1, source_target_pairs={{0,32},{16,48},{32,0},{48,16},{1,33},{17,49},{33,1},{49,17},{2,34}... | collective-permute-start | bytes 294920 | tf_op jit(solution)/shard_map/ppermute | solution.py:431
  26.1 3.3 %collective-permute-start.2 = (bf16[4,96,128]{2,1,0:T(8,128)(2,1)S(1)}, bf16[4,96,128]{2,1,0:T(8,128)(2,1)S(1)}, u32[]{:S(2)}, u32[]{:S(2)}) collective-permute-start(bf16[4,96,128]{2,1,0:T(8,128)(2,1)S(1)} %copy-done.8), channel_id=1, source_target_pairs={{0,48},{16,0},{32,16},{48,32},{1,49},{17,1},{33,17},{49,33},{2,50}... | collective-permute-start | bytes 294920 | tf_op jit(solution)/shard_map/ppermute | solution.py:431
  29.5 0.0 collective-permute-done.q1
  29.5 0.0 collective-permute-done.1.q2
  29.5 3.1 %collective-permute-done.2.q3 = bf16[4,96,128]{2,1,0:T(8,128)(2,1)S(1)} collective-permute-done((bf16[4,96,128]{2,1,0:T(8,128)(2,1)S(1)}, bf16[4,96,128]{2,1,0:T(8,128)(2,1)S(1)}, u32[]{:S(2)}, u32[]{:S(2)}) %collective-permute-start.2) | collective-permute-done | bytes 98336 | tf_op jit(solution)/shard_map/ppermute | solution.py:431
  32.6 1.2 shard_map.137
  33.8 39.2 %all-to-all-done.q_ref.k0 = bf16[16,288,128]{2,1,0:T(8,128)(2,1)S(1)} async-done(((bf16[16,288,128]{2,1,0:T(8,128)(2,1)}), bf16[16,288,128]{2,1,0:T(8,128)(2,1)S(1)}, u32[]{:S(2)}, u32[]{:S(2)}) %all-to-all-start) | async-done | bytes 1179680 | tf_op jit(solution)/shard_map/all_to_all | solution.py:442
  73.1 8.5 %all-to-all-start.1 = ((bf16[16,288,128]{2,1,0:T(8,128)(2,1)}), bf16[16,288,128]{2,1,0:T(8,128)(2,1)S(1)}, u32[]{:S(2)}, u32[]{:S(2)}) async-start(bf16[16,288,128]{2,1,0:T(8,128)(2,1)} %shard_map.137), calls=%async_computation.1 | async-start | bytes 2359296 | tf_op jit(solution)/shard_map/all_to_all | solution.py:442
  81.6 0.1 slice.9
  81.6 3.4 %collective-permute-start.3 = (bf16[16,192,128]{2,1,0:T(8,128)(2,1)S(1)}, bf16[16,192,128]{2,1,0:T(8,128)(2,1)S(1)}, u32[]{:S(2)}, u32[]{:S(2)}) collective-permute-start(bf16[16,192,128]{2,1,0:T(8,128)(2,1)S(1)} %slice.9), channel_id=1, source_target_pairs={{0,16},{16,32},{32,48},{48,0},{1,17},{17,33},{33,49},{49,1},{2,18}... | collective-permute-start | bytes 2359304 | tf_op jit(solution)/shard_map/ppermute | solution.py:431
  85.0 3.7 %collective-permute-start.4 = (bf16[16,192,128]{2,1,0:T(8,128)(2,1)S(1)}, bf16[16,192,128]{2,1,0:T(8,128)(2,1)S(1)}, u32[]{:S(2)}, u32[]{:S(2)}) collective-permute-start(bf16[16,192,128]{2,1,0:T(8,128)(2,1)S(1)} %slice.9), channel_id=1, source_target_pairs={{0,48},{16,0},{32,16},{48,32},{1,49},{17,1},{33,17},{49,33},{2,50}... | collective-permute-start | bytes 2359304 | tf_op jit(solution)/shard_map/ppermute | solution.py:431
  89.4 0.1 pad_add_fusion.info
  89.4 14.5 %collective-permute-done.3.k1 = bf16[16,192,128]{2,1,0:T(8,128)(2,1)S(1)} collective-permute-done((bf16[16,192,128]{2,1,0:T(8,128)(2,1)S(1)}, bf16[16,192,128]{2,1,0:T(8,128)(2,1)S(1)}, u32[]{:S(2)}, u32[]{:S(2)}) %collective-permute-start.3) | collective-permute-done | bytes 786464 | tf_op jit(solution)/shard_map/ppermute | solution.py:431
  104.0 2.2 collective-permute-start.5
  106.2 0.0 collective-permute-done.4.k2
  106.2 0.9 copy-done.6
  107.1 5.0 %collective-permute-start.6 = (bf16[8,192,128]{2,1,0:T(8,128)(2,1)S(1)}, bf16[8,192,128]{2,1,0:T(8,128)(2,1)S(1)}, u32[]{:S(2)}, u32[]{:S(2)}) collective-permute-start(bf16[8,192,128]{2,1,0:T(8,128)(2,1)S(1)} %slice.13), channel_id=1, source_target_pairs={{0,48},{16,0},{32,16},{48,32},{1,49},{17,1},{33,17},{49,33},{2,50}... | collective-permute-start | bytes 1179656 | tf_op jit(solution)/shard_map/ppermute | solution.py:431
  112.1 1.1 copy-done.5
  113.2 1.1 copy-done.7
  114.4 11.1 %shard_map.138 = (f32[1536,128]{1,0:T(8,128)S(1)}, f32[1536,128]{1,0:T(8,128)S(1)}) custom-call(bf16[16,288,128]{2,1,0:T(8,128)(2,1)} %copy-done.11, bf16[16,288,128]{2,1,0:T(8,128)(2,1)} %copy-done.11, bf16[16,192,128]{2,1,0:T(8,128)(2,1)S(1)} %copy-done.5, bf16[16,192,128]{2,1,0:T(8,128)(2,1)S(1)} %copy-done.7), custom_call_target="tpu_custom_call" | custom-call | flops 7247757312 | bytes 2359296 | tf_op jit(solution)/shard_map/pallas_call | solution.py:235
  125.4 0.0 collective-permute-done.5.k3
  125.5 0.0 collective-permute-done.6.k4
  125.5 8.4 %shard_map.139 = bf16[16,96,128]{2,1,0:T(8,128)(2,1)} custom-call(s32[4]{0:T(128)S(1)} %pad_add_fusion.info, bf16[16,288,128]{2,1,0:T(8,128)(2,1)} %copy-done.11, f32[1536,128]{1,0:T(8,128)S(1)} %get-tuple-element.24.total_ref, f32[1536,128]{1,0:T(8,128)S(1)} %get-tuple-element.25.state_ref, bf16[8,192,128]{2,1,0:T(8,128)(2,1)S(1)} %collective-permute-done.5.k3, ...), custom_call_target="tpu_custom_call" | custom-call | flops 3221225472 | bytes 1048576 | tf_op jit(solution)/shard_map/pallas_call | solution.py:254
  133.9 2.8 %all-to-all-done.1.s_ref = bf16[16,288,128]{2,1,0:T(8,128)(2,1)S(1)} async-done(((bf16[16,288,128]{2,1,0:T(8,128)(2,1)}), bf16[16,288,128]{2,1,0:T(8,128)(2,1)S(1)}, u32[]{:S(2)}, u32[]{:S(2)}) %all-to-all-start.1) | async-done | bytes 1179680 | tf_op jit(solution)/shard_map/all_to_all | solution.py:442
  136.7 8.9 %all-to-all-start.2 = ((bf16[16,96,128]{2,1,0:T(8,128)(2,1)}), bf16[16,96,128]{2,1,0:T(8,128)(2,1)S(1)}, u32[]{:S(2)}, u32[]{:S(2)}) async-start(bf16[16,96,128]{2,1,0:T(8,128)(2,1)} %shard_map.139), calls=%async_computation.2 | async-start | bytes 786432 | tf_op jit(solution)/shard_map/all_to_all | solution.py:442
  145.6 3.5 %shard_map.140 = (bf16[384,256]{1,0:T(8,128)(2,1)S(1)}, bf16[384,256]{1,0:T(8,128)(2,1)S(1)}, bf16[384,256]{1,0:T(8,128)(2,1)S(1)}, bf16[384,256]{1,0:T(8,128)(2,1)S(1)}) custom-call(bf16[16,288,128]{2,1,0:T(8,128)(2,1)S(1)} %all-to-all-done.1.s_ref), custom_call_target="tpu_custom_call" | custom-call | flops 2415919104 | bytes 786432 | tf_op jit(solution)/shard_map/pallas_call | solution.py:274
  149.1 4.3 %collective-permute-start.7 = (bf16[384,256]{1,0:T(8,128)(2,1)S(1)}, bf16[384,256]{1,0:T(8,128)(2,1)S(1)}, u32[]{:S(2)}, u32[]{:S(2)}) collective-permute-start(bf16[384,256]{1,0:T(8,128)(2,1)S(1)} %get-tuple-element.30), channel_id=1, source_target_pairs={{0,48},{16,0},{32,16},{48,32},{1,49},{17,1},{33,17},{49,33},{2,50}... | collective-permute-start | bytes 589832 | tf_op jit(solution)/shard_map/ppermute | solution.py:431
  153.4 2.7 %collective-permute-start.8 = (bf16[384,256]{1,0:T(8,128)(2,1)S(1)}, bf16[384,256]{1,0:T(8,128)(2,1)S(1)}, u32[]{:S(2)}, u32[]{:S(2)}) collective-permute-start(bf16[384,256]{1,0:T(8,128)(2,1)S(1)} %get-tuple-element.31), channel_id=1, source_target_pairs={{0,32},{16,48},{32,0},{48,16},{1,33},{17,49},{33,1},{49,17},{2,34}... | collective-permute-start | bytes 589832 | tf_op jit(solution)/shard_map/ppermute | solution.py:431
  156.1 2.8 %collective-permute-start.9 = (bf16[384,256]{1,0:T(8,128)(2,1)S(1)}, bf16[384,256]{1,0:T(8,128)(2,1)S(1)}, u32[]{:S(2)}, u32[]{:S(2)}) collective-permute-start(bf16[384,256]{1,0:T(8,128)(2,1)S(1)} %get-tuple-element.32), channel_id=1, source_target_pairs={{0,16},{16,32},{32,48},{48,0},{1,17},{17,33},{33,49},{49,1},{2,18}... | collective-permute-start | bytes 589832 | tf_op jit(solution)/shard_map/ppermute | solution.py:431
  158.9 2.8 %collective-permute-done.7.p1 = bf16[384,256]{1,0:T(8,128)(2,1)S(1)} collective-permute-done((bf16[384,256]{1,0:T(8,128)(2,1)S(1)}, bf16[384,256]{1,0:T(8,128)(2,1)S(1)}, u32[]{:S(2)}, u32[]{:S(2)}) %collective-permute-start.7) | collective-permute-done | bytes 196640 | tf_op jit(solution)/shard_map/ppermute | solution.py:431
  161.7 3.0 %collective-permute-done.8.p2 = bf16[384,256]{1,0:T(8,128)(2,1)S(1)} collective-permute-done((bf16[384,256]{1,0:T(8,128)(2,1)S(1)}, bf16[384,256]{1,0:T(8,128)(2,1)S(1)}, u32[]{:S(2)}, u32[]{:S(2)}) %collective-permute-start.8) | collective-permute-done | bytes 196640 | tf_op jit(solution)/shard_map/ppermute | solution.py:431
  164.6 2.6 %collective-permute-done.9.p3 = bf16[384,256]{1,0:T(8,128)(2,1)S(1)} collective-permute-done((bf16[384,256]{1,0:T(8,128)(2,1)S(1)}, bf16[384,256]{1,0:T(8,128)(2,1)S(1)}, u32[]{:S(2)}, u32[]{:S(2)}) %collective-permute-start.9) | collective-permute-done | bytes 196640 | tf_op jit(solution)/shard_map/ppermute | solution.py:431
  167.3 2.0 shard_map.141
  169.3 0.0 all-to-all-done.2.back_ref
  169.3 11.9 %all-to-all-start.3 = ((bf16[16,32,128]{2,1,0:T(8,128)(2,1)}), bf16[16,32,128]{2,1,0:T(8,128)(2,1)S(1)}, u32[]{:S(2)}, u32[]{:S(2)}) async-start(bf16[16,32,128]{2,1,0:T(8,128)(2,1)} %shard_map.141), calls=%async_computation.3 | async-start | bytes 262144 | tf_op jit(solution)/shard_map/all_to_all | solution.py:442
  181.2 0.3 copy.15.weight_ref
  181.6 13.5 %all-to-all-done.3.shared_ref = bf16[16,32,128]{2,1,0:T(8,128)(2,1)S(1)} async-done(((bf16[16,32,128]{2,1,0:T(8,128)(2,1)}), bf16[16,32,128]{2,1,0:T(8,128)(2,1)S(1)}, u32[]{:S(2)}, u32[]{:S(2)}) %all-to-all-start.3) | async-done | bytes 131104 | tf_op jit(solution)/shard_map/all_to_all | solution.py:442
  195.1 0.0 copy-start.10
  195.1 0.7 shard_map.142
  195.9 19.5 %all_to_all.30.line_ref = bf16[16,48,128]{2,1,0:T(8,128)(2,1)S(1)} all-to-all(bf16[16,48,128]{2,1,0:T(8,128)(2,1)S(1)} %shard_map.142), channel_id=1, replica_groups=mesh['clip'=8,'x'=4,'zh'=4,'zl'=4] {'zh','zl'}, dimensions={0} | all-to-all | bytes 393216 | tf_op jit(solution)/shard_map/all_to_all | solution.py:442
  215.4 1.4 shard_map.143
  216.8 3.5 %all-to-all-start.5 = ((bf16[4,4,72,128]{3,2,1,0:T(8,128)(2,1)}), bf16[4,4,72,128]{3,2,1,0:T(8,128)(2,1)S(1)}, u32[]{:S(2)}, u32[]{:S(2)}) async-start(bf16[4,4,72,128]{3,2,1,0:T(8,128)(2,1)} %shard_map.143), calls=%async_computation.5 | async-start | bytes 589824 | tf_op jit(solution)/shard_map/all_to_all | solution.py:442
  220.3 6.8 %all-to-all-done.5 = bf16[4,4,72,128]{3,2,1,0:T(8,128)(2,1)S(1)} async-done(((bf16[4,4,72,128]{3,2,1,0:T(8,128)(2,1)}), bf16[4,4,72,128]{3,2,1,0:T(8,128)(2,1)S(1)}, u32[]{:S(2)}, u32[]{:S(2)}) %all-to-all-start.5) | async-done | bytes 294944 | tf_op jit(solution)/shard_map/all_to_all | solution.py:442
  227.1 2.6 %shard_map.144 = bf16[8,48,384]{2,1,0:T(8,128)(2,1)} custom-call(s32[4]{0:T(128)S(1)} %pad_add_fusion.info, s32[16]{0:T(128)S(1)} %copy-done.10, bf16[16,72,128]{2,1,0:T(8,128)(2,1)S(1)} %bitcast.6, bf16[432,384]{1,0:T(8,128)(2,1)S(1)} %copy-done.2, f32[1,384]{1,0:T(1,128)S(1)} %broadcast_in_dim.21.bias_ref, f32[1,384]{1,0:T(1,128)S(1)} %broadcast_in_dim.22.gain_ref), custom_call_target="tpu_custom_call" | custom-call | tf_op jit(solution)/shard_map/pallas_call | solution.py:417
  (35 shorter events, 0.1 us)
Async XLA Ops:
  2.7 15.4 %copy-start.8 = (bf16[4,96,128]{2,1,0:T(8,128)(2,1)S(1)}, bf16[4,96,128]{2,1,0:T(8,128)(2,1)}, u32[]{:S(2)}) copy-start(bf16[4,96,128]{2,1,0:T(8,128)(2,1)} %get-tuple-element.22.q0) | copy-start | bytes 294916
  2.7 29.9 %copy-start.3 = (bf16[4,192,128]{2,1,0:T(8,128)(2,1)S(1)}, bf16[4,192,128]{2,1,0:T(8,128)(2,1)}, u32[]{:S(2)}) copy-start(bf16[4,192,128]{2,1,0:T(8,128)(2,1)} %get-tuple-element.21.kv_ref) | copy-start | bytes 589828
  2.7 70.4 %all-to-all-start = ((bf16[16,288,128]{2,1,0:T(8,128)(2,1)}), bf16[16,288,128]{2,1,0:T(8,128)(2,1)S(1)}, u32[]{:S(2)}, u32[]{:S(2)}) async-start(bf16[16,288,128]{2,1,0:T(8,128)(2,1)} %get-tuple-element.20), calls=%async_computation | async-start | bytes 2359296 | tf_op jit(solution)/shard_map/all_to_all | solution.py:442
  18.1 11.4 %collective-permute-start = (bf16[4,96,128]{2,1,0:T(8,128)(2,1)S(1)}, bf16[4,96,128]{2,1,0:T(8,128)(2,1)S(1)}, u32[]{:S(2)}, u32[]{:S(2)}) collective-permute-start(bf16[4,96,128]{2,1,0:T(8,128)(2,1)S(1)} %copy-done.8), channel_id=1, source_target_pairs={{0,16},{16,32},{32,48},{48,0},{1,17},{17,33},{33,49},{49,1},{2,18}... | collective-permute-start | bytes 294920 | tf_op jit(solution)/shard_map/ppermute | solution.py:431
  21.5 8.0 %collective-permute-start.1 = (bf16[4,96,128]{2,1,0:T(8,128)(2,1)S(1)}, bf16[4,96,128]{2,1,0:T(8,128)(2,1)S(1)}, u32[]{:S(2)}, u32[]{:S(2)}) collective-permute-start(bf16[4,96,128]{2,1,0:T(8,128)(2,1)S(1)} %copy-done.8), channel_id=1, source_target_pairs={{0,32},{16,48},{32,0},{48,16},{1,33},{17,49},{33,1},{49,17},{2,34}... | collective-permute-start | bytes 294920 | tf_op jit(solution)/shard_map/ppermute | solution.py:431
  26.1 6.5 %collective-permute-start.2 = (bf16[4,96,128]{2,1,0:T(8,128)(2,1)S(1)}, bf16[4,96,128]{2,1,0:T(8,128)(2,1)S(1)}, u32[]{:S(2)}, u32[]{:S(2)}) collective-permute-start(bf16[4,96,128]{2,1,0:T(8,128)(2,1)S(1)} %copy-done.8), channel_id=1, source_target_pairs={{0,48},{16,0},{32,16},{48,32},{1,49},{17,1},{33,17},{49,33},{2,50}... | collective-permute-start | bytes 294920 | tf_op jit(solution)/shard_map/ppermute | solution.py:431
  73.1 8.5 %copy-start.11 = (bf16[16,288,128]{2,1,0:T(8,128)(2,1)}, bf16[16,288,128]{2,1,0:T(8,128)(2,1)S(1)}, u32[]{:S(2)}) copy-start(bf16[16,288,128]{2,1,0:T(8,128)(2,1)S(1)} %all-to-all-done.q_ref.k0) | copy-start | bytes 3538948
  73.1 63.6 %all-to-all-start.1 = ((bf16[16,288,128]{2,1,0:T(8,128)(2,1)}), bf16[16,288,128]{2,1,0:T(8,128)(2,1)S(1)}, u32[]{:S(2)}, u32[]{:S(2)}) async-start(bf16[16,288,128]{2,1,0:T(8,128)(2,1)} %shard_map.137), calls=%async_computation.1 | async-start | bytes 2359296 | tf_op jit(solution)/shard_map/all_to_all | solution.py:442
  81.6 22.3 %collective-permute-start.3 = (bf16[16,192,128]{2,1,0:T(8,128)(2,1)S(1)}, bf16[16,192,128]{2,1,0:T(8,128)(2,1)S(1)}, u32[]{:S(2)}, u32[]{:S(2)}) collective-permute-start(bf16[16,192,128]{2,1,0:T(8,128)(2,1)S(1)} %slice.9), channel_id=1, source_target_pairs={{0,16},{16,32},{32,48},{48,0},{1,17},{17,33},{33,49},{49,1},{2,18}... | collective-permute-start | bytes 2359304 | tf_op jit(solution)/shard_map/ppermute | solution.py:431
  85.0 21.1 %collective-permute-start.4 = (bf16[16,192,128]{2,1,0:T(8,128)(2,1)S(1)}, bf16[16,192,128]{2,1,0:T(8,128)(2,1)S(1)}, u32[]{:S(2)}, u32[]{:S(2)}) collective-permute-start(bf16[16,192,128]{2,1,0:T(8,128)(2,1)S(1)} %slice.9), channel_id=1, source_target_pairs={{0,48},{16,0},{32,16},{48,32},{1,49},{17,1},{33,17},{49,33},{2,50}... | collective-permute-start | bytes 2359304 | tf_op jit(solution)/shard_map/ppermute | solution.py:431
  103.9 2.2 copy-start.4
  104.0 21.5 %collective-permute-start.5 = (bf16[8,192,128]{2,1,0:T(8,128)(2,1)S(1)}, bf16[8,192,128]{2,1,0:T(8,128)(2,1)S(1)}, u32[]{:S(2)}, u32[]{:S(2)}) collective-permute-start(bf16[8,192,128]{2,1,0:T(8,128)(2,1)S(1)} %slice.12), channel_id=1, source_target_pairs={{0,16},{16,32},{32,48},{48,0},{1,17},{17,33},{33,49},{49,1},{2,18}... | collective-permute-start | bytes 1179656 | tf_op jit(solution)/shard_map/ppermute | solution.py:431
  106.2 0.9 copy-start.6
  107.1 18.4 %copy-start = (bf16[512,640]{1,0:T(8,128)(2,1)S(1)}, bf16[512,640]{1,0:T(8,128)(2,1)}, u32[]{:S(2)}) copy-start(bf16[512,640]{1,0:T(8,128)(2,1)} %tk_ref.3) | copy-start | bytes 1966084
  107.1 18.4 %copy-start.1 = (bf16[512,640]{1,0:T(8,128)(2,1)S(1)}, bf16[512,640]{1,0:T(8,128)(2,1)}, u32[]{:S(2)}) copy-start(bf16[512,640]{1,0:T(8,128)(2,1)} %tv_ref.3) | copy-start | bytes 1966084
  107.1 18.4 %collective-permute-start.6 = (bf16[8,192,128]{2,1,0:T(8,128)(2,1)S(1)}, bf16[8,192,128]{2,1,0:T(8,128)(2,1)S(1)}, u32[]{:S(2)}, u32[]{:S(2)}) collective-permute-start(bf16[8,192,128]{2,1,0:T(8,128)(2,1)S(1)} %slice.13), channel_id=1, source_target_pairs={{0,48},{16,0},{32,16},{48,32},{1,49},{17,1},{33,17},{49,33},{2,50}... | collective-permute-start | bytes 1179656 | tf_op jit(solution)/shard_map/ppermute | solution.py:431
  112.1 1.1 copy-start.5
  113.2 1.1 copy-start.7
  136.7 32.6 %all-to-all-start.2 = ((bf16[16,96,128]{2,1,0:T(8,128)(2,1)}), bf16[16,96,128]{2,1,0:T(8,128)(2,1)S(1)}, u32[]{:S(2)}, u32[]{:S(2)}) async-start(bf16[16,96,128]{2,1,0:T(8,128)(2,1)} %shard_map.139), calls=%async_computation.2 | async-start | bytes 786432 | tf_op jit(solution)/shard_map/all_to_all | solution.py:442
  149.1 12.6 %collective-permute-start.7 = (bf16[384,256]{1,0:T(8,128)(2,1)S(1)}, bf16[384,256]{1,0:T(8,128)(2,1)S(1)}, u32[]{:S(2)}, u32[]{:S(2)}) collective-permute-start(bf16[384,256]{1,0:T(8,128)(2,1)S(1)} %get-tuple-element.30), channel_id=1, source_target_pairs={{0,48},{16,0},{32,16},{48,32},{1,49},{17,1},{33,17},{49,33},{2,50}... | collective-permute-start | bytes 589832 | tf_op jit(solution)/shard_map/ppermute | solution.py:431
  153.4 11.2 %collective-permute-start.8 = (bf16[384,256]{1,0:T(8,128)(2,1)S(1)}, bf16[384,256]{1,0:T(8,128)(2,1)S(1)}, u32[]{:S(2)}, u32[]{:S(2)}) collective-permute-start(bf16[384,256]{1,0:T(8,128)(2,1)S(1)} %get-tuple-element.31), channel_id=1, source_target_pairs={{0,32},{16,48},{32,0},{48,16},{1,33},{17,49},{33,1},{49,17},{2,34}... | collective-permute-start | bytes 589832 | tf_op jit(solution)/shard_map/ppermute | solution.py:431
  156.1 11.2 %collective-permute-start.9 = (bf16[384,256]{1,0:T(8,128)(2,1)S(1)}, bf16[384,256]{1,0:T(8,128)(2,1)S(1)}, u32[]{:S(2)}, u32[]{:S(2)}) collective-permute-start(bf16[384,256]{1,0:T(8,128)(2,1)S(1)} %get-tuple-element.32), channel_id=1, source_target_pairs={{0,16},{16,32},{32,48},{48,0},{1,17},{17,33},{33,49},{49,1},{2,18}... | collective-permute-start | bytes 589832 | tf_op jit(solution)/shard_map/ppermute | solution.py:431
  167.3 13.9 %copy-start.12 = (bf16[2560,64]{0,1:T(8,128)(2,1)S(1)}, bf16[2560,64]{0,1:T(8,128)(2,1)}, u32[]{:S(2)}) copy-start(bf16[2560,64]{0,1:T(8,128)(2,1)} %param.23) | copy-start | bytes 983044
  169.3 12.2 %copy-start.13 = (f32[2560]{0:T(1024)S(1)}, f32[2560]{0:T(1024)}, u32[]{:S(2)}) copy-start(f32[2560]{0:T(1024)} %param.21) | copy-start | bytes 30724
  169.3 12.3 %copy-start.14 = (f32[2560]{0:T(1024)S(1)}, f32[2560]{0:T(1024)}, u32[]{:S(2)}) copy-start(f32[2560]{0:T(1024)} %param.22) | copy-start | bytes 30724
  169.3 25.8 %copy-start.9 = (f32[64]{0:T(128)S(1)}, f32[64]{0:T(128)}, u32[]{:S(2)}) copy-start(f32[64]{0:T(128)} %param.24) | copy-start | bytes 772
  169.3 25.8 %all-to-all-start.3 = ((bf16[16,32,128]{2,1,0:T(8,128)(2,1)}), bf16[16,32,128]{2,1,0:T(8,128)(2,1)S(1)}, u32[]{:S(2)}, u32[]{:S(2)}) async-start(bf16[16,32,128]{2,1,0:T(8,128)(2,1)} %shard_map.141), calls=%async_computation.3 | async-start | bytes 262144 | tf_op jit(solution)/shard_map/all_to_all | solution.py:442
  195.1 25.1 %copy-start.15 = (f32[384]{0:T(512)S(1)}, f32[384]{0:T(512)}, u32[]{:S(2)}) copy-start(f32[384]{0:T(512)} %param.26) | copy-start | bytes 4612
  195.1 25.1 %copy-start.16 = (f32[384]{0:T(512)S(1)}, f32[384]{0:T(512)}, u32[]{:S(2)}) copy-start(f32[384]{0:T(512)} %param.27) | copy-start | bytes 4612
  195.1 31.9 %copy-start.2 = (bf16[432,384]{1,0:T(8,128)(2,1)S(1)}, bf16[432,384]{1,0:T(8,128)(2,1)}, u32[]{:S(2)}) copy-start(bf16[432,384]{1,0:T(8,128)(2,1)} %weight_ref.2) | copy-start | bytes 995332
  195.1 31.9 %copy-start.10 = (s32[16]{0:T(128)S(1)}, s32[16]{0:T(128)}, u32[]{:S(2)}) copy-start(s32[16]{0:T(128)} %tile_map.1) | copy-start | bytes 196
  216.8 10.3 %all-to-all-start.5 = ((bf16[4,4,72,128]{3,2,1,0:T(8,128)(2,1)}), bf16[4,4,72,128]{3,2,1,0:T(8,128)(2,1)S(1)}, u32[]{:S(2)}, u32[]{:S(2)}) async-start(bf16[4,4,72,128]{3,2,1,0:T(8,128)(2,1)} %shard_map.143), calls=%async_computation.5 | async-start | bytes 589824 | tf_op jit(solution)/shard_map/all_to_all | solution.py:442

commit v4 on v3

--- a/solution.py
+++ b/solution.py
@@ -34,11 +34,9 @@
     return pl.BlockSpec(memory_space=pltpu.SMEM)
 
 
-PART = 24
-SLOT = 32
-
-
-def load_kernel(q_hbm, k_hbm, v_hbm, main_out, kv_out, q_out, q_ref, k_ref, v_ref, sems):
+def load_kernel(
+    q_hbm, k_hbm, v_hbm, main_out, kv_out, last_out, q_ref, k_ref, v_ref, sems
+):
     width = 5 * HDIM
     copies = []
     for zl in range(4):
@@ -53,14 +51,17 @@
         for copy in copies[3 * zl : 3 * zl + 3]:
             copy.wait()
         last = slice((5 * zl + 4) * HDIM, (5 * zl + 5) * HDIM)
-        q_out[zl] = q_ref[:, last]
-        kv_out[zl, 0:ROWS, :] = k_ref[:, last]
-        kv_out[zl, ROWS : 2 * ROWS, :] = v_ref[:, last]
         for index, ref in enumerate((k_ref, v_ref, q_ref)):
             rows = slice(index * ROWS, (index + 1) * ROWS)
             for zh in range(4):
                 own = slice((5 * zl + zh) * HDIM, (5 * zl + zh + 1) * HDIM)
                 main_out[zh * 4 + zl, rows, :] = ref[:, own]
+                if index < 2:
+                    kv_out[zh * 4 + zl, rows, :] = ref[:, last]
+    for distance in range(4):
+        group = lax.rem(lax.axis_index("zl") + distance, 4)
+        span = pl.ds(pl.multiple_of((5 * group + 4) * HDIM, HDIM), HDIM)
+        last_out[distance] = q_ref[:, span]
 
 
 def load(queries, keys, values):
@@ -68,7 +69,7 @@
         load_kernel,
         out_shape=(
             jax.ShapeDtypeStruct((NZ, 3 * ROWS, HDIM), BF),
-            jax.ShapeDtypeStruct((4, 2 * ROWS, HDIM), BF),
+            jax.ShapeDtypeStruct((NZ, 2 * ROWS, HDIM), BF),
             jax.ShapeDtypeStruct((4, ROWS, HDIM), BF),
         ),
         in_specs=[pl.BlockSpec(memory_space=pl.ANY)] * 3,
@@ -77,27 +78,6 @@
         + [pltpu.SemaphoreType.DMA((12,))],
         compiler_params=pltpu.CompilerParams(vmem_limit_bytes=60 * 1024 * 1024),
     )(queries, keys, values)
-
-
-def pack_kernel(kv_ref, q0, q1, q2, q3, out_ref):
-    for zl in range(4):
-        columns = [ref[zl].astype(F32) for ref in (q0, q1, q2, q3)]
-        for zh in range(4):
-            out_ref[zh * 4 + zl, 0 : 2 * ROWS, :] = kv_ref[zl]
-            span = slice(PART * zh, PART * (zh + 1))
-            out_ref[zh * 4 + zl, 2 * ROWS : 3 * ROWS, :] = jnp.concatenate(
-                [column[span] for column in columns], axis=0
-            ).astype(BF)
-
-
-def pack(kv, columns):
-    return pl.pallas_call(
-        pack_kernel,
-        out_shape=jax.ShapeDtypeStruct((NZ, 3 * ROWS, HDIM), BF),
-        in_specs=[vmem()] * 5,
-        out_specs=vmem(),
-        compiler_params=params(),
-    )(kv, *columns)
 
 
 def dot_t(a, b):
@@ -159,34 +139,45 @@
     return pieces
 
 
-def first_kernel(q_ref, k0, k1, k2, total_ref, state_ref):
-    query = q_ref[...].reshape(4 * ROWS, HDIM)
-    peak, total = absorb(query, pieces_of((k0, k1, k2)), None, None)
+def put_state(peak, total, total_ref, state_ref):
     total_ref[...] = total[:, :HDIM]
-    lane = lax.broadcasted_iota(jnp.int32, (4 * ROWS, HDIM), 1)
+    lane = lax.broadcasted_iota(jnp.int32, total_ref.shape, 1)
     state_ref[...] = jnp.where(lane < 64, peak, total[:, HDIM:])
 
 
-def second_kernel(info, q_ref, total_ref, state_ref, k3, k4, tk_ref, tv_ref, out_ref):
-    query = q_ref[...].reshape(4 * ROWS, HDIM)
+def get_state(total_ref, state_ref):
+    state = state_ref[...]
+    weight = jnp.broadcast_to(state[:, HDIM - 1 : HDIM], state.shape)
+    return state[:, 0:1], jnp.concatenate([total_ref[...], weight], axis=1)
+
+
+def own_kernel(info, q_ref, k0, tk_ref, tv_ref, total_ref, state_ref, text_ref):
+    query = q_ref[...].reshape(GROUP * ROWS, HDIM)
     column = pl.ds(pl.multiple_of(info[0] * HDIM, HDIM), HDIM)
-    state = state_ref[...]
-    peak = state[:, 0:1]
-    weight = jnp.broadcast_to(state[:, HDIM - 1 : HDIM], (4 * ROWS, HDIM))
-    total = jnp.concatenate([total_ref[...], weight], axis=1)
-    peak, total = absorb(query, pieces_of((k3, k4)), peak, total)
-    result = total[:, :HDIM] / total[:, HDIM:]
-    result = result + text_part(query, tk_ref[:, column], tv_ref[:, column], info[1])
-    out_ref[...] = result.astype(BF).reshape(4, ROWS, HDIM)
-
-
-def shared_kernel(s_ref, p0, p1, p2, p3):
-    rows = NZ * PART
+    text_ref[...] = text_part(query, tk_ref[:, column], tv_ref[:, column], info[1])
+    put_state(*absorb(query, pieces_of((k0,)), None, None), total_ref, state_ref)
+
+
+def near_kernel(q_ref, total_in, state_in, k1, k2, total_ref, state_ref):
+    query = q_ref[...].reshape(GROUP * ROWS, HDIM)
+    state = get_state(total_in, state_in)
+    put_state(*absorb(query, pieces_of((k1, k2)), *state), total_ref, state_ref)
+
+
+def far_kernel(q_ref, total_in, state_in, text_in, k3, k4, out_ref):
+    query = q_ref[...].reshape(GROUP * ROWS, HDIM)
+    state = get_state(total_in, state_in)
+    peak, total = absorb(query, pieces_of((k3, k4)), *state)
+    result = total[:, :HDIM] / total[:, HDIM:] + text_in[...]
+    out_ref[...] = result.astype(BF).reshape(GROUP, ROWS, HDIM)
+
+
+def shared_kernel(kv_ref, q0, q1, q2, q3, p0, p1, p2, p3):
+    rows = 4 * ROWS
     lane = lax.broadcasted_iota(jnp.int32, (rows, HDIM), 1)
-    queries = s_ref[:, 2 * ROWS : 3 * ROWS, :].astype(F32)
     for column, out_ref in enumerate((p0, p1, p2, p3)):
-        query = queries[:, PART * column : PART * (column + 1)].reshape(rows, HDIM).astype(BF)
-        peak, total = absorb(query, pieces_of((s_ref,)), None, None)
+        query = jnp.concatenate([ref[column] for ref in (q0, q1, q2, q3)], axis=0)
+        peak, total = absorb(query, pieces_of((kv_ref,)), None, None)
         out_ref[:, 0:HDIM] = (total[:, :HDIM] / total[:, HDIM:]).astype(BF)
         level = peak + jnp.log2(total[:, HDIM:])
         high = level.astype(BF).astype(F32)
@@ -196,10 +187,8 @@
         out_ref[:, HDIM:] = terms.astype(BF)
 
 
-def merge_kernel(info, s_ref, p0, p1, p2, p3, tk_ref, tv_ref, out_ref):
-    rows = NZ * PART
-    query = s_ref[:, 2 * ROWS : 3 * ROWS, :].astype(F32)[:, :PART]
-    query = query.reshape(rows, HDIM).astype(BF)
+def merge_kernel(info, q0, q1, q2, q3, p0, p1, p2, p3, tk_ref, tv_ref, out_ref):
+    query = jnp.concatenate([ref[0] for ref in (q0, q1, q2, q3)], axis=0)
     levels = []
     for ref in (p0, p1, p2, p3):
         terms = ref[:, HDIM:].astype(F32)
@@ -211,8 +200,9 @@
     ) / sum(weights)
     column = slice(4 * HDIM, 5 * HDIM)
     result = result + text_part(query, tk_ref[:, column], tv_ref[:, column], info[1])
-    filler = jnp.zeros((NZ, SLOT - PART, HDIM), F32)
-    out_ref[...] = jnp.concatenate([result.reshape(NZ, PART, HDIM), filler], axis=1).astype(BF)
+    for distance in range(4):
+        rows = slice(distance * ROWS, (distance + 1) * ROWS)
+        out_ref[lax.rem(info[3] + 4 - distance, 4)] = result[rows].astype(BF)
 
 
 KEYS = 6144
@@ -226,93 +216,89 @@
     )
 
 
-def whole(array):
-    return pl.BlockSpec(array.shape, lambda i: (0,) * array.ndim)
-
-
-def main_first(queries, kv):
-    rows = 4 * ROWS
-    return pl.pallas_call(
-        first_kernel,
-        grid=(NZ // 4,),
-        out_shape=(
-            jax.ShapeDtypeStruct((NZ * ROWS, HDIM), F32),
-            jax.ShapeDtypeStruct((NZ * ROWS, HDIM), F32),
-        ),
-        in_specs=[pl.BlockSpec((4, ROWS, HDIM), lambda i: (i, 2, 0))] + [whole(a) for a in kv],
-        out_specs=(
-            pl.BlockSpec((rows, HDIM), lambda i: (i, 0)),
-            pl.BlockSpec((rows, HDIM), lambda i: (i, 0)),
-        ),
-        compiler_params=params(),
-        cost_estimate=cost(NZ * ROWS, 4608),
-    )(queries, *kv)
-
-
-def main_second(info, queries, total, state, kv, text_keys, text_values):
-    rows = 4 * ROWS
-    return pl.pallas_call(
-        second_kernel,
-        grid=(NZ // 4,),
+GROUP = 4
+QUERY_BLOCK = pl.BlockSpec((GROUP, ROWS, HDIM), lambda i: (i, 2, 0))
+STATE_BLOCK = pl.BlockSpec((GROUP * ROWS, HDIM), lambda i: (i, 0))
+STATE = jax.ShapeDtypeStruct((NZ * ROWS, HDIM), F32)
+
+
+def main_own(info, main, text_keys, text_values):
+    return pl.pallas_call(
+        own_kernel,
+        grid=(NZ // GROUP,),
+        out_shape=(STATE,) * 3,
+        in_specs=[smem(), QUERY_BLOCK, vmem(), vmem(), vmem()],
+        out_specs=(STATE_BLOCK,) * 3,
+        compiler_params=params(),
+        cost_estimate=cost(NZ * ROWS, NZ * ROWS + TXT),
+    )(info, main, main, text_keys, text_values)
+
+
+def main_near(main, total, state, kv):
+    return pl.pallas_call(
+        near_kernel,
+        grid=(NZ // GROUP,),
+        out_shape=(STATE,) * 2,
+        in_specs=[QUERY_BLOCK, STATE_BLOCK, STATE_BLOCK] + [vmem()] * len(kv),
+        out_specs=(STATE_BLOCK,) * 2,
+        compiler_params=params(),
+        cost_estimate=cost(NZ * ROWS, 2 * NZ * ROWS),
+    )(main, total, state, *kv)
+
+
+def main_far(main, total, state, text, kv):
+    return pl.pallas_call(
+        far_kernel,
+        grid=(NZ // GROUP,),
         out_shape=jax.ShapeDtypeStruct((NZ, ROWS, HDIM), BF),
-        in_specs=[
-            smem(),
-            pl.BlockSpec((4, ROWS, HDIM), lambda i: (i, 2, 0)),
-            pl.BlockSpec((rows, HDIM), lambda i: (i, 0)),
-            pl.BlockSpec((rows, HDIM), lambda i: (i, 0)),
-        ]
-        + [whole(a) for a in kv]
-        + [whole(text_keys), whole(text_values)],
-        out_specs=pl.BlockSpec((4, ROWS, HDIM), lambda i: (i, 0, 0)),
-        compiler_params=params(),
-        cost_estimate=cost(NZ * ROWS, 2048),
-    )(info, queries, total, state, *kv, text_keys, text_values)
-
-
-def shared_attention(shared):
-    part = jax.ShapeDtypeStruct((NZ * PART, 2 * HDIM), BF)
+        in_specs=[QUERY_BLOCK] + [STATE_BLOCK] * 3 + [vmem()] * len(kv),
+        out_specs=pl.BlockSpec((GROUP, ROWS, HDIM), lambda i: (i, 0, 0)),
+        compiler_params=params(),
+        cost_estimate=cost(NZ * ROWS, NZ * ROWS),
+    )(main, total, state, text, *kv)
+
+
+def shared_attention(kv, columns):
+    part = jax.ShapeDtypeStruct((4 * ROWS, 2 * HDIM), BF)
     return pl.pallas_call(
         shared_kernel,
         out_shape=(part,) * 4,
-        in_specs=[vmem()],
+        in_specs=[vmem()] * 5,
         out_specs=(vmem(),) * 4,
         compiler_params=params(),
         cost_estimate=cost(NZ * ROWS, NZ * ROWS),
-    )(shared)
-
-
-def shared_merge(info, shared, parts, text_keys, text_values):
+    )(kv, *columns)
+
+
+def shared_merge(info, queries, parts, text_keys, text_values):
     return pl.pallas_call(
         merge_kernel,
-        out_shape=jax.ShapeDtypeStruct((NZ, SLOT, HDIM), BF),
-        in_specs=[smem()] + [vmem()] * 7,
+        out_shape=jax.ShapeDtypeStruct((4, ROWS, HDIM), BF),
+        in_specs=[smem()] + [vmem()] * 10,
         out_specs=vmem(),
         compiler_params=params(),
-        cost_estimate=cost(NZ * PART, TXT),
-    )(info, shared, *parts, text_keys, text_values)
+        cost_estimate=cost(4 * ROWS, TXT),
+    )(info, *queries, *parts, text_keys, text_values)
 
 
 def head_kernel(
     back_ref, shared_ref, gain_ref, shift_ref, weight_ref, bias_ref, out_ref
 ):
     blocks = []
-    for head in range(20):
-        zl, zh = head // 5, head % 5
-        if zh < 4:
-            block = back_ref[zh * 4 + zl].astype(F32)
-        else:
-            parts = [shared_ref[part * 4 + zl].astype(F32)[:PART] for part in range(4)]
-            block = jnp.concatenate(parts, axis=0)
-        blocks.append(block)
+    for zl in range(4):
+        for zh in range(5):
+            start = (5 * zl + zh) * HDIM
+            block = back_ref[zh * 4 + zl] if zh < 4 else shared_ref[zl]
+            blocks.append((block.astype(F32), slice(start, start + HDIM)))
     count = 20 * HDIM
-    average = jnp.sum(sum(blocks), axis=-1, keepdims=True) / count
-    blocks = [block - average for block in blocks]
-    variance = jnp.sum(sum(block * block for block in blocks), axis=-1, keepdims=True) / count
+    average = jnp.sum(sum(block for block, _ in blocks), axis=-1, keepdims=True) / count
+    blocks = [(block - average, span) for block, span in blocks]
+    variance = sum(block * block for block, _ in blocks)
+    variance = jnp.sum(variance, axis=-1, keepdims=True) / count
     scale = lax.rsqrt(variance + 1e-06)
     patches = jnp.zeros((ROWS, 64), F32)
-    for head in range(20):
-        span = slice(head * HDIM, (head + 1) * HDIM)
-        normed = (blocks[head] * scale * gain_ref[:, span] + shift_ref[:, span]).astype(BF)
+    for block, span in blocks:
+        normed = (block * scale * gain_ref[:, span] + shift_ref[:, span]).astype(BF)
         patches = patches + jnp.dot(normed, weight_ref[span, :], preferred_element_type=F32)
     patches = patches + bias_ref[...]
     packed = jnp.concatenate([patches[: ROWS // 2], patches[ROWS // 2 :]], axis=1).astype(BF)
@@ -435,7 +421,7 @@
     right = shift(block, axis, 1)
     left = shift(block, axis, -1)
     half = block.shape[0] // 2
-    return (block, right, left, shift(right[:half], axis, 1), shift(left[half:], axis, -1))
+    return (right, left), (shift(right[:half], axis, 1), shift(left[half:], axis, -1))
 
 
 def exchange(block, axis):
@@ -460,22 +446,25 @@
 ):
     x, zh, zl = (lax.axis_index(axis) for axis in ("x", "zh", "zl"))
     info = jnp.stack([zh, text_len[0], x, zl]).astype(jnp.int32)
-    main_send, last_kv, last_q = load(queries, keys, values)
-    columns = [last_q] + [shift(last_q, "x", distance) for distance in (1, 2, 3)]
+    main_send, shared_send, last = load(queries, keys, values)
+    last = jnp.stack([last] + [shift(last, "x", d) for d in (1, 2, 3)], axis=1)
+    last = [last[0]] + [shift(last[d], "zl", d) for d in (1, 2, 3)]
     main = exchange(main_send, Z)
-    main, shared_send = lax.optimization_barrier((main, pack(last_kv, columns)))
+    main, last, shared_send = lax.optimization_barrier((main, last, shared_send))
     shared = exchange(shared_send, Z)
-    main_kv = (main,) + around(main[:, : 2 * ROWS], "x")[1:]
-    total, state = main_first(main, main_kv[:3])
-    out = main_second(info, main, total, state, main_kv[3:], text_keys, text_values)
+    near, far = around(main[:, : 2 * ROWS], "x")
+    total, state, text = main_own(info, main, text_keys, text_values)
+    total, state = main_near(main, total, state, near)
+    out = main_far(main, total, state, text, far)
     out, shared = lax.optimization_barrier((out, shared))
     back = exchange(out, Z)
-    parts = shared_attention(shared)
-    parts = [parts[0]] + [shift(parts[distance], "x", -distance) for distance in (1, 2, 3)]
-    merged = shared_merge(info, shared, parts, text_keys, text_values)
+    parts = shared_attention(shared, last)
+    parts = [parts[0]] + [shift(parts[d], "x", -d) for d in (1, 2, 3)]
+    merged = shared_merge(info, last, parts, text_keys, text_values)
     back, merged = lax.optimization_barrier((back, merged))
-    shared_back = exchange(merged, Z)
-    line = exchange(head(back, shared_back, mod_gain, mod_shift, head_weight, head_bias), Z)
+    shared_back = exchange(merged, "zl")
+    line = head(back, shared_back, mod_gain, mod_shift, head_weight, head_bias)
+    line = exchange(line, Z)
     plane = exchange(slab_of(info, line), "x")
     gathered = plane.reshape(16, SLAB, HDIM)
     out = conv(info, tile_map, gathered, conv_weight, conv_bias, norm_gain)

time: 231 us -> 222 us (0.961)
  waiting for transfers between devices: 88.3 us -> 65.6 us
  starting transfers between devices: 83.4 us -> 90.2 us
  blocking collectives: 19.5 us -> 23.6 us
    all_to_all x5, waiting for transfers between devices: 62.3 us -> 12.5 us  [exchange(): return lax.all_to_all(block, axis, split_axis=0, concat_axis=0, tiled=True)]
    ppermute x10 -> x13, waiting for transfers between devices: 26 us -> 53.1 us  [shift(): lax.ppermute(block, axis, [(i, (i + distance) % 4) for i in range(4)])]
    ppermute x10 -> x13, starting transfers between devices: 35.4 us -> 44.7 us  [shift(): lax.ppermute(block, axis, [(i, (i + distance) % 4) for i in range(4)])]
    all_to_all x1, blocking collectives: 19.5 us -> 23.6 us  [exchange(): return lax.all_to_all(block, axis, split_axis=0, concat_axis=0, tiled=True)]
    all_to_all x5, starting transfers between devices: 48.1 us -> 45.4 us  [exchange(): return lax.all_to_all(block, axis, split_axis=0, concat_axis=0, tiled=True)]
  transfers between devices with their start and end apart: 15 -> 18, of which waited for: 9 -> 10; matrix products, arithmetic and copies ran while one was open for 0% -> 2% of each run, Pallas kernels for 11% -> 13%
where the time goes in v4:
time: 222 us; the launch traced here: 221 us
  starting transfers between devices  90.2 us (41%)
  waiting for transfers between devices  65.6 us (30%)
  Pallas kernels  35.3 us (16%)
  blocking collectives  23.6 us (11%)
  local copies, waits for them, and re-layouts  4.75 us (2%)
    ppermute x13, waiting for transfers between devices, shift(): lax.ppermute(block, axis, [(i, (i + distance) % 4) for i in range(4)])  53.1 us
    all_to_all x5, starting transfers between devices, exchange(): return lax.all_to_all(block, axis, split_axis=0, concat_axis=0, tiled=True)  45.4 us
    ppermute x13, starting transfers between devices, shift(): lax.ppermute(block, axis, [(i, (i + distance) % 4) for i in range(4)])  44.7 us
    all_to_all x1, blocking collectives, exchange(): return lax.all_to_all(block, axis, split_axis=0, concat_axis=0, tiled=True)  23.6 us
    all_to_all x5, waiting for transfers between devices, exchange(): return lax.all_to_all(block, axis, split_axis=0, concat_axis=0, tiled=True)  12.5 us
    pallas_call x1, Pallas kernels, main_near(): pl.pallas_call(near_kernel, grid=(NZ // GROUP,), out_shape=(STATE,) * 2,...  8.97 us
    pallas_call x1, Pallas kernels, main_own(): pl.pallas_call(own_kernel, grid=(NZ // GROUP,), out_shape=(STATE,) * 3, i...  6.68 us
    pallas_call x1, Pallas kernels, main_far(): pl.pallas_call(far_kernel, grid=(NZ // GROUP,), out_shape=jax.ShapeDtypeS...  6.51 us
  transfers between devices with their start and end apart: 18, of which 10 were waited for; matrix products, arithmetic and copies ran while one was open for 2% of the time, Pallas kernels for 13%

profile of v4, /device:TPU:24, one launch (start us, length us, event | category | flops | bytes accessed | tf_op | source)
XLA Modules:
  0.0 220.6 jit_solution(17376854869799515572)
XLA Ops:
  0.0 2.9 %shard_map.136 = (bf16[16,288,128]{2,1,0:T(8,128)(2,1)}, bf16[16,192,128]{2,1,0:T(8,128)(2,1)}, bf16[4,96,128]{2,1,0:T(8,128)(2,1)}) custom-call(bf16[96,2560]{1,0:T(8,128)(2,1)} %q_hbm.1, bf16[96,2560]{1,0:T(8,128)(2,1)} %k_hbm.1, bf16[96,2560]{1,0:T(8,128)(2,1)} %v_hbm.1), custom_call_target="tpu_custom_call" | custom-call | tf_op jit(solution)/shard_map/pallas_call | solution.py:68
  2.9 0.0 copy-start.11
  2.9 15.3 %all-to-all-start = ((bf16[16,288,128]{2,1,0:T(8,128)(2,1)}), bf16[16,288,128]{2,1,0:T(8,128)(2,1)S(1)}, u32[]{:S(2)}, u32[]{:S(2)}) async-start(bf16[16,288,128]{2,1,0:T(8,128)(2,1)} %get-tuple-element.27), calls=%async_computation | async-start | bytes 2359296 | tf_op jit(solution)/shard_map/all_to_all | solution.py:428
  18.3 3.4 %collective-permute-start = (bf16[4,96,128]{2,1,0:T(8,128)(2,1)S(1)}, bf16[4,96,128]{2,1,0:T(8,128)(2,1)S(1)}, u32[]{:S(2)}, u32[]{:S(2)}) collective-permute-start(bf16[4,96,128]{2,1,0:T(8,128)(2,1)S(1)} %copy-done.11), channel_id=1, source_target_pairs={{0,16},{16,32},{32,48},{48,0},{1,17},{17,33},{33,49},{49,1},{2,18}... | collective-permute-start | bytes 294920 | tf_op jit(solution)/shard_map/ppermute | solution.py:417
  21.7 4.6 %collective-permute-start.1 = (bf16[4,96,128]{2,1,0:T(8,128)(2,1)S(1)}, bf16[4,96,128]{2,1,0:T(8,128)(2,1)S(1)}, u32[]{:S(2)}, u32[]{:S(2)}) collective-permute-start(bf16[4,96,128]{2,1,0:T(8,128)(2,1)S(1)} %copy-done.11), channel_id=1, source_target_pairs={{0,32},{16,48},{32,0},{48,16},{1,33},{17,49},{33,1},{49,17},{2,34}... | collective-permute-start | bytes 294920 | tf_op jit(solution)/shard_map/ppermute | solution.py:417
  26.4 3.3 %collective-permute-start.2 = (bf16[4,96,128]{2,1,0:T(8,128)(2,1)S(1)}, bf16[4,96,128]{2,1,0:T(8,128)(2,1)S(1)}, u32[]{:S(2)}, u32[]{:S(2)}) collective-permute-start(bf16[4,96,128]{2,1,0:T(8,128)(2,1)S(1)} %copy-done.11), channel_id=1, source_target_pairs={{0,48},{16,0},{32,16},{48,32},{1,49},{17,1},{33,17},{49,33},{2,50}... | collective-permute-start | bytes 294920 | tf_op jit(solution)/shard_map/ppermute | solution.py:417
  29.7 0.0 collective-permute-done.1
  29.7 3.1 %collective-permute-done.2 = bf16[4,96,128]{2,1,0:T(8,128)(2,1)S(1)} collective-permute-done((bf16[4,96,128]{2,1,0:T(8,128)(2,1)S(1)}, bf16[4,96,128]{2,1,0:T(8,128)(2,1)S(1)}, u32[]{:S(2)}, u32[]{:S(2)}) %collective-permute-start.2) | collective-permute-done | bytes 98336 | tf_op jit(solution)/shard_map/ppermute | solution.py:417
  32.9 0.1 pad_maximum_fusion
  33.0 3.8 %collective-permute-start.3 = (bf16[4,96,128]{2,1,0:T(8,128)(2,1)S(1)}, bf16[4,96,128]{2,1,0:T(8,128)(2,1)S(1)}, u32[]{:S(2)}, u32[]{:S(2)}) collective-permute-start(bf16[4,96,128]{2,1,0:T(8,128)(2,1)S(1)} %get-tuple-element.51), channel_id=1, source_target_pairs={{0,1},{1,2},{2,3},{3,0},{4,5},{5,6},{6,7},{7,4},{8,9},{9,10},{10,1... | collective-permute-start | bytes 294920 | tf_op jit(solution)/shard_map/ppermute | solution.py:417
  36.8 4.3 %collective-permute-start.4 = (bf16[4,96,128]{2,1,0:T(8,128)(2,1)S(1)}, bf16[4,96,128]{2,1,0:T(8,128)(2,1)S(1)}, u32[]{:S(2)}, u32[]{:S(2)}) collective-permute-start(bf16[4,96,128]{2,1,0:T(8,128)(2,1)S(1)} %get-tuple-element.50), channel_id=1, source_target_pairs={{0,2},{1,3},{2,0},{3,1},{4,6},{5,7},{6,4},{7,5},{8,10},{9,11},{10,... | collective-permute-start | bytes 294920 | tf_op jit(solution)/shard_map/ppermute | solution.py:417
  41.1 3.4 %collective-permute-start.5 = (bf16[4,96,128]{2,1,0:T(8,128)(2,1)S(1)}, bf16[4,96,128]{2,1,0:T(8,128)(2,1)S(1)}, u32[]{:S(2)}, u32[]{:S(2)}) collective-permute-start(bf16[4,96,128]{2,1,0:T(8,128)(2,1)S(1)} %get-tuple-element.49), channel_id=1, source_target_pairs={{0,3},{1,0},{2,1},{3,2},{4,7},{5,4},{6,5},{7,6},{8,11},{9,8},{10,9... | collective-permute-start | bytes 294920 | tf_op jit(solution)/shard_map/ppermute | solution.py:417
  44.4 32.2 %collective-permute-done.3.q1 = bf16[4,96,128]{2,1,0:T(8,128)(2,1)S(1)} collective-permute-done((bf16[4,96,128]{2,1,0:T(8,128)(2,1)S(1)}, bf16[4,96,128]{2,1,0:T(8,128)(2,1)S(1)}, u32[]{:S(2)}, u32[]{:S(2)}) %collective-permute-start.3) | collective-permute-done | bytes 98336 | tf_op jit(solution)/shard_map/ppermute | solution.py:417
  76.6 3.0 %collective-permute-done.4.q2 = bf16[4,96,128]{2,1,0:T(8,128)(2,1)S(1)} collective-permute-done((bf16[4,96,128]{2,1,0:T(8,128)(2,1)S(1)}, bf16[4,96,128]{2,1,0:T(8,128)(2,1)S(1)}, u32[]{:S(2)}, u32[]{:S(2)}) %collective-permute-start.4) | collective-permute-done | bytes 98336 | tf_op jit(solution)/shard_map/ppermute | solution.py:417
  79.6 1.1 copy-done.9
  80.7 9.8 %all-to-all-start.1 = ((bf16[16,192,128]{2,1,0:T(8,128)(2,1)}), bf16[16,192,128]{2,1,0:T(8,128)(2,1)S(1)}, u32[]{:S(2)}, u32[]{:S(2)}) async-start(bf16[16,192,128]{2,1,0:T(8,128)(2,1)} %get-tuple-element.36), calls=%async_computation.1 | async-start | bytes 1572864 | tf_op jit(solution)/shard_map/all_to_all | solution.py:428
  90.5 0.0 copy-start.1
  90.5 2.2 slice.25
  92.7 3.4 %collective-permute-start.6 = (bf16[16,192,128]{2,1,0:T(8,128)(2,1)}, bf16[16,192,128]{2,1,0:T(8,128)(2,1)S(1)}, u32[]{:S(2)}, u32[]{:S(2)}) collective-permute-start(bf16[16,192,128]{2,1,0:T(8,128)(2,1)} %slice.25), channel_id=1, source_target_pairs={{0,16},{16,32},{32,48},{48,0},{1,17},{17,33},{33,49},{49,1},{2,18}... | collective-permute-start | bytes 2359304 | tf_op jit(solution)/shard_map/ppermute | solution.py:417
  96.1 3.7 %collective-permute-start.7 = (bf16[16,192,128]{2,1,0:T(8,128)(2,1)}, bf16[16,192,128]{2,1,0:T(8,128)(2,1)}, u32[]{:S(2)}, u32[]{:S(2)}) collective-permute-start(bf16[16,192,128]{2,1,0:T(8,128)(2,1)} %slice.25), channel_id=1, source_target_pairs={{0,48},{16,0},{32,16},{48,32},{1,49},{17,1},{33,17},{49,33},{2,50}... | collective-permute-start | bytes 2359304 | tf_op jit(solution)/shard_map/ppermute | solution.py:417
  100.4 0.1 pad_add_fusion.info
  100.5 6.7 %shard_map.137 = (f32[1536,128]{1,0:T(8,128)S(1)}, f32[1536,128]{1,0:T(8,128)S(1)}, f32[1536,128]{1,0:T(8,128)S(1)}) custom-call(s32[4]{0:T(128)S(1)} %pad_add_fusion.info, bf16[16,288,128]{2,1,0:T(8,128)(2,1)} %copy-done.9, bf16[16,288,128]{2,1,0:T(8,128)(2,1)} %copy-done.9, bf16[512,640]{1,0:T(8,128)(2,1)S(1)} %copy-done, bf16[512,640]{1,0:T(8,128)(2,1)S(1)} %copy-done.1), custom_call_target="tpu_custom_call" | custom-call | flops 3221225472 | bytes 1048576 | tf_op jit(solution)/shard_map/pallas_call | solution.py:226
  107.2 7.5 %collective-permute-done.6.k1 = bf16[16,192,128]{2,1,0:T(8,128)(2,1)S(1)} collective-permute-done((bf16[16,192,128]{2,1,0:T(8,128)(2,1)}, bf16[16,192,128]{2,1,0:T(8,128)(2,1)S(1)}, u32[]{:S(2)}, u32[]{:S(2)}) %collective-permute-start.6) | collective-permute-done | bytes 786464 | tf_op jit(solution)/shard_map/ppermute | solution.py:417
  114.7 2.2 collective-permute-start.8
  116.9 1.0 slice.33
  117.9 4.9 %collective-permute-start.9 = (bf16[8,192,128]{2,1,0:T(8,128)(2,1)S(1)}, bf16[8,192,128]{2,1,0:T(8,128)(2,1)S(1)}, u32[]{:S(2)}, u32[]{:S(2)}) collective-permute-start(bf16[8,192,128]{2,1,0:T(8,128)(2,1)S(1)} %slice.33), channel_id=1, source_target_pairs={{0,48},{16,0},{32,16},{48,32},{1,49},{17,1},{33,17},{49,33},{2,50}... | collective-permute-start | bytes 1179656 | tf_op jit(solution)/shard_map/ppermute | solution.py:417
  122.8 9.0 %shard_map.138 = (f32[1536,128]{1,0:T(8,128)S(1)}, f32[1536,128]{1,0:T(8,128)S(1)}) custom-call(bf16[16,288,128]{2,1,0:T(8,128)(2,1)} %copy-done.9, f32[1536,128]{1,0:T(8,128)S(1)} %get-tuple-element.31.total_in, f32[1536,128]{1,0:T(8,128)S(1)} %get-tuple-element.32.state_in, bf16[16,192,128]{2,1,0:T(8,128)(2,1)S(1)} %collective-permute-done.6.k1, ...), custom_call_target="tpu_custom_call" | custom-call | flops 4831838208 | bytes 1572864 | tf_op jit(solution)/shard_map/pallas_call | solution.py:238
  131.8 0.0 copy-start.4
  131.8 6.5 %shard_map.139 = bf16[16,96,128]{2,1,0:T(8,128)(2,1)} custom-call(bf16[16,288,128]{2,1,0:T(8,128)(2,1)} %copy-done.9, f32[1536,128]{1,0:T(8,128)S(1)} %get-tuple-element.33.total_in, f32[1536,128]{1,0:T(8,128)S(1)} %get-tuple-element.34.state_in, f32[1536,128]{1,0:T(8,128)S(1)} %get-tuple-element.35.text_in, ...), custom_call_target="tpu_custom_call" | custom-call | flops 2415919104 | bytes 786432 | tf_op jit(solution)/shard_map/pallas_call | solution.py:250
  138.4 11.7 %all-to-all-start.2 = ((bf16[16,96,128]{2,1,0:T(8,128)(2,1)}), bf16[16,96,128]{2,1,0:T(8,128)(2,1)S(1)}, u32[]{:S(2)}, u32[]{:S(2)}) async-start(bf16[16,96,128]{2,1,0:T(8,128)(2,1)} %shard_map.139), calls=%async_computation.2 | async-start | bytes 786432 | tf_op jit(solution)/shard_map/all_to_all | solution.py:428
  150.1 3.5 %shard_map.140 = (bf16[384,256]{1,0:T(8,128)(2,1)S(1)}, bf16[384,256]{1,0:T(8,128)(2,1)S(1)}, bf16[384,256]{1,0:T(8,128)(2,1)S(1)}, bf16[384,256]{1,0:T(8,128)(2,1)S(1)}) custom-call(bf16[16,192,128]{2,1,0:T(8,128)(2,1)S(1)} %all-to-all-done.1.kv_ref, bf16[4,96,128]{2,1,0:T(8,128)(2,1)S(1)} %get-tuple-element.38.q0, ...), custom_call_target="tpu_custom_call" | custom-call | flops 2415919104 | bytes 786432 | tf_op jit(solution)/shard_map/pallas_call | solution.py:263
  153.7 2.8 %collective-permute-start.10 = (bf16[384,256]{1,0:T(8,128)(2,1)S(1)}, bf16[384,256]{1,0:T(8,128)(2,1)S(1)}, u32[]{:S(2)}, u32[]{:S(2)}) collective-permute-start(bf16[384,256]{1,0:T(8,128)(2,1)S(1)} %get-tuple-element.44), channel_id=1, source_target_pairs={{0,48},{16,0},{32,16},{48,32},{1,49},{17,1},{33,17},{49,33},{2,50}... | collective-permute-start | bytes 589832 | tf_op jit(solution)/shard_map/ppermute | solution.py:417
  156.5 2.1 collective-permute-start.11
  158.6 2.8 %collective-permute-start.12 = (bf16[384,256]{1,0:T(8,128)(2,1)S(1)}, bf16[384,256]{1,0:T(8,128)(2,1)S(1)}, u32[]{:S(2)}, u32[]{:S(2)}) collective-permute-start(bf16[384,256]{1,0:T(8,128)(2,1)S(1)} %get-tuple-element.46), channel_id=1, source_target_pairs={{0,16},{16,32},{32,48},{48,0},{1,17},{17,33},{33,49},{49,1},{2,18}... | collective-permute-start | bytes 589832 | tf_op jit(solution)/shard_map/ppermute | solution.py:417
  161.5 0.2 collective-permute-done.10.p1
  161.7 5.4 %collective-permute-done.11.p2 = bf16[384,256]{1,0:T(8,128)(2,1)S(1)} collective-permute-done((bf16[384,256]{1,0:T(8,128)(2,1)S(1)}, bf16[384,256]{1,0:T(8,128)(2,1)S(1)}, u32[]{:S(2)}, u32[]{:S(2)}) %collective-permute-start.11) | collective-permute-done | bytes 196640 | tf_op jit(solution)/shard_map/ppermute | solution.py:417
  167.0 1.7 collective-permute-done.12.p3
  168.7 2.0 shard_map.141
  170.7 0.3 all-to-all-done.2.back_ref
  171.0 5.1 %all-to-all-start.3 = ((bf16[4,96,128]{2,1,0:T(8,128)(2,1)}), bf16[4,96,128]{2,1,0:T(8,128)(2,1)S(1)}, u32[]{:S(2)}, u32[]{:S(2)}) async-start(bf16[4,96,128]{2,1,0:T(8,128)(2,1)} %shard_map.141), calls=%async_computation.3 | async-start | bytes 196608 | tf_op jit(solution)/shard_map/all_to_all | solution.py:428
  176.2 0.3 copy.15.weight_ref
  176.5 5.4 %all-to-all-done.3.shared_ref = bf16[4,96,128]{2,1,0:T(8,128)(2,1)S(1)} async-done(((bf16[4,96,128]{2,1,0:T(8,128)(2,1)}), bf16[4,96,128]{2,1,0:T(8,128)(2,1)S(1)}, u32[]{:S(2)}, u32[]{:S(2)}) %all-to-all-start.3) | async-done | bytes 98336 | tf_op jit(solution)/shard_map/all_to_all | solution.py:428
  182.0 0.7 shard_map.142
  182.8 23.6 %all_to_all.30.line_ref = bf16[16,48,128]{2,1,0:T(8,128)(2,1)S(1)} all-to-all(bf16[16,48,128]{2,1,0:T(8,128)(2,1)S(1)} %shard_map.142), channel_id=1, replica_groups=mesh['clip'=8,'x'=4,'zh'=4,'zl'=4] {'zh','zl'}, dimensions={0} | all-to-all | bytes 393216 | tf_op jit(solution)/shard_map/all_to_all | solution.py:428
  206.3 1.4 shard_map.143
  207.7 3.5 %all-to-all-start.5 = ((bf16[4,4,72,128]{3,2,1,0:T(8,128)(2,1)}), bf16[4,4,72,128]{3,2,1,0:T(8,128)(2,1)S(1)}, u32[]{:S(2)}, u32[]{:S(2)}) async-start(bf16[4,4,72,128]{3,2,1,0:T(8,128)(2,1)} %shard_map.143), calls=%async_computation.5 | async-start | bytes 589824 | tf_op jit(solution)/shard_map/all_to_all | solution.py:428
  211.2 6.8 %all-to-all-done.5 = bf16[4,4,72,128]{3,2,1,0:T(8,128)(2,1)S(1)} async-done(((bf16[4,4,72,128]{3,2,1,0:T(8,128)(2,1)}), bf16[4,4,72,128]{3,2,1,0:T(8,128)(2,1)S(1)}, u32[]{:S(2)}, u32[]{:S(2)}) %all-to-all-start.5) | async-done | bytes 294944 | tf_op jit(solution)/shard_map/all_to_all | solution.py:428
  218.0 2.6 %shard_map.144 = bf16[8,48,384]{2,1,0:T(8,128)(2,1)} custom-call(s32[4]{0:T(128)S(1)} %pad_add_fusion.info, s32[16]{0:T(128)S(1)} %copy-done.8, bf16[16,72,128]{2,1,0:T(8,128)(2,1)S(1)} %bitcast.18, bf16[432,384]{1,0:T(8,128)(2,1)S(1)} %copy-done.2, f32[1,384]{1,0:T(1,128)S(1)} %broadcast_in_dim.21.bias_ref, f32[1,384]{1,0:T(1,128)S(1)} %broadcast_in_dim.22.gain_ref), custom_call_target="tpu_custom_call" | custom-call | tf_op jit(solution)/shard_map/pallas_call | solution.py:403
  (41 shorter events, 0.2 us)
Async XLA Ops:
  2.9 15.4 %copy-start.11 = (bf16[4,96,128]{2,1,0:T(8,128)(2,1)S(1)}, bf16[4,96,128]{2,1,0:T(8,128)(2,1)}, u32[]{:S(2)}) copy-start(bf16[4,96,128]{2,1,0:T(8,128)(2,1)} %get-tuple-element.28) | copy-start | bytes 294916
  2.9 76.7 %all-to-all-start = ((bf16[16,288,128]{2,1,0:T(8,128)(2,1)}), bf16[16,288,128]{2,1,0:T(8,128)(2,1)S(1)}, u32[]{:S(2)}, u32[]{:S(2)}) async-start(bf16[16,288,128]{2,1,0:T(8,128)(2,1)} %get-tuple-element.27), calls=%async_computation | async-start | bytes 2359296 | tf_op jit(solution)/shard_map/all_to_all | solution.py:428
  18.3 11.4 %collective-permute-start = (bf16[4,96,128]{2,1,0:T(8,128)(2,1)S(1)}, bf16[4,96,128]{2,1,0:T(8,128)(2,1)S(1)}, u32[]{:S(2)}, u32[]{:S(2)}) collective-permute-start(bf16[4,96,128]{2,1,0:T(8,128)(2,1)S(1)} %copy-done.11), channel_id=1, source_target_pairs={{0,16},{16,32},{32,48},{48,0},{1,17},{17,33},{33,49},{49,1},{2,18}... | collective-permute-start | bytes 294920 | tf_op jit(solution)/shard_map/ppermute | solution.py:417
  21.7 8.0 %collective-permute-start.1 = (bf16[4,96,128]{2,1,0:T(8,128)(2,1)S(1)}, bf16[4,96,128]{2,1,0:T(8,128)(2,1)S(1)}, u32[]{:S(2)}, u32[]{:S(2)}) collective-permute-start(bf16[4,96,128]{2,1,0:T(8,128)(2,1)S(1)} %copy-done.11), channel_id=1, source_target_pairs={{0,32},{16,48},{32,0},{48,16},{1,33},{17,49},{33,1},{49,17},{2,34}... | collective-permute-start | bytes 294920 | tf_op jit(solution)/shard_map/ppermute | solution.py:417
  26.4 6.5 %collective-permute-start.2 = (bf16[4,96,128]{2,1,0:T(8,128)(2,1)S(1)}, bf16[4,96,128]{2,1,0:T(8,128)(2,1)S(1)}, u32[]{:S(2)}, u32[]{:S(2)}) collective-permute-start(bf16[4,96,128]{2,1,0:T(8,128)(2,1)S(1)} %copy-done.11), channel_id=1, source_target_pairs={{0,48},{16,0},{32,16},{48,32},{1,49},{17,1},{33,17},{49,33},{2,50}... | collective-permute-start | bytes 294920 | tf_op jit(solution)/shard_map/ppermute | solution.py:417
  33.0 43.7 %collective-permute-start.3 = (bf16[4,96,128]{2,1,0:T(8,128)(2,1)S(1)}, bf16[4,96,128]{2,1,0:T(8,128)(2,1)S(1)}, u32[]{:S(2)}, u32[]{:S(2)}) collective-permute-start(bf16[4,96,128]{2,1,0:T(8,128)(2,1)S(1)} %get-tuple-element.51), channel_id=1, source_target_pairs={{0,1},{1,2},{2,3},{3,0},{4,5},{5,6},{6,7},{7,4},{8,9},{9,10},{10,1... | collective-permute-start | bytes 294920 | tf_op jit(solution)/shard_map/ppermute | solution.py:417
  36.8 42.8 %collective-permute-start.4 = (bf16[4,96,128]{2,1,0:T(8,128)(2,1)S(1)}, bf16[4,96,128]{2,1,0:T(8,128)(2,1)S(1)}, u32[]{:S(2)}, u32[]{:S(2)}) collective-permute-start(bf16[4,96,128]{2,1,0:T(8,128)(2,1)S(1)} %get-tuple-element.50), channel_id=1, source_target_pairs={{0,2},{1,3},{2,0},{3,1},{4,6},{5,7},{6,4},{7,5},{8,10},{9,11},{10,... | collective-permute-start | bytes 294920 | tf_op jit(solution)/shard_map/ppermute | solution.py:417
  41.1 38.5 %collective-permute-start.5 = (bf16[4,96,128]{2,1,0:T(8,128)(2,1)S(1)}, bf16[4,96,128]{2,1,0:T(8,128)(2,1)S(1)}, u32[]{:S(2)}, u32[]{:S(2)}) collective-permute-start(bf16[4,96,128]{2,1,0:T(8,128)(2,1)S(1)} %get-tuple-element.49), channel_id=1, source_target_pairs={{0,3},{1,0},{2,1},{3,2},{4,7},{5,4},{6,5},{7,6},{8,11},{9,8},{10,9... | collective-permute-start | bytes 294920 | tf_op jit(solution)/shard_map/ppermute | solution.py:417
  79.6 10.9 %copy-start.3 = (bf16[4,96,128]{2,1,0:T(8,128)(2,1)}, bf16[4,96,128]{2,1,0:T(8,128)(2,1)S(1)}, u32[]{:S(2)}) copy-start(bf16[4,96,128]{2,1,0:T(8,128)(2,1)S(1)} %collective-permute-done.4.q2) | copy-start | bytes 294916
  79.6 10.9 %copy-start.5 = (bf16[4,96,128]{2,1,0:T(8,128)(2,1)}, bf16[4,96,128]{2,1,0:T(8,128)(2,1)S(1)}, u32[]{:S(2)}) copy-start(bf16[4,96,128]{2,1,0:T(8,128)(2,1)S(1)} %collective-permute-done.5.q3) | copy-start | bytes 294916
  79.6 1.1 copy-start.9
  80.7 57.7 %all-to-all-start.1 = ((bf16[16,192,128]{2,1,0:T(8,128)(2,1)}), bf16[16,192,128]{2,1,0:T(8,128)(2,1)S(1)}, u32[]{:S(2)}, u32[]{:S(2)}) async-start(bf16[16,192,128]{2,1,0:T(8,128)(2,1)} %get-tuple-element.36), calls=%async_computation.1 | async-start | bytes 1572864 | tf_op jit(solution)/shard_map/all_to_all | solution.py:428
  90.5 10.0 %copy-start = (bf16[512,640]{1,0:T(8,128)(2,1)S(1)}, bf16[512,640]{1,0:T(8,128)(2,1)}, u32[]{:S(2)}) copy-start(bf16[512,640]{1,0:T(8,128)(2,1)} %tk_ref.3) | copy-start | bytes 1966084
  90.5 10.0 %copy-start.1 = (bf16[512,640]{1,0:T(8,128)(2,1)S(1)}, bf16[512,640]{1,0:T(8,128)(2,1)}, u32[]{:S(2)}) copy-start(bf16[512,640]{1,0:T(8,128)(2,1)} %tv_ref.3) | copy-start | bytes 1966084
  92.7 22.0 %collective-permute-start.6 = (bf16[16,192,128]{2,1,0:T(8,128)(2,1)}, bf16[16,192,128]{2,1,0:T(8,128)(2,1)S(1)}, u32[]{:S(2)}, u32[]{:S(2)}) collective-permute-start(bf16[16,192,128]{2,1,0:T(8,128)(2,1)} %slice.25), channel_id=1, source_target_pairs={{0,16},{16,32},{32,48},{48,0},{1,17},{17,33},{33,49},{49,1},{2,18}... | collective-permute-start | bytes 2359304 | tf_op jit(solution)/shard_map/ppermute | solution.py:417
  96.1 20.8 %collective-permute-start.7 = (bf16[16,192,128]{2,1,0:T(8,128)(2,1)}, bf16[16,192,128]{2,1,0:T(8,128)(2,1)}, u32[]{:S(2)}, u32[]{:S(2)}) collective-permute-start(bf16[16,192,128]{2,1,0:T(8,128)(2,1)} %slice.25), channel_id=1, source_target_pairs={{0,48},{16,0},{32,16},{48,32},{1,49},{17,1},{33,17},{49,33},{2,50}... | collective-permute-start | bytes 2359304 | tf_op jit(solution)/shard_map/ppermute | solution.py:417
  114.7 17.1 %collective-permute-start.8 = (bf16[8,192,128]{2,1,0:T(8,128)(2,1)S(1)}, bf16[8,192,128]{2,1,0:T(8,128)(2,1)S(1)}, u32[]{:S(2)}, u32[]{:S(2)}) collective-permute-start(bf16[8,192,128]{2,1,0:T(8,128)(2,1)S(1)} %slice.32), channel_id=1, source_target_pairs={{0,16},{16,32},{32,48},{48,0},{1,17},{17,33},{33,49},{49,1},{2,18}... | collective-permute-start | bytes 1179656 | tf_op jit(solution)/shard_map/ppermute | solution.py:417
  117.9 13.9 %collective-permute-start.9 = (bf16[8,192,128]{2,1,0:T(8,128)(2,1)S(1)}, bf16[8,192,128]{2,1,0:T(8,128)(2,1)S(1)}, u32[]{:S(2)}, u32[]{:S(2)}) collective-permute-start(bf16[8,192,128]{2,1,0:T(8,128)(2,1)S(1)} %slice.33), channel_id=1, source_target_pairs={{0,48},{16,0},{32,16},{48,32},{1,49},{17,1},{33,17},{49,33},{2,50}... | collective-permute-start | bytes 1179656 | tf_op jit(solution)/shard_map/ppermute | solution.py:417
  131.8 18.3 %copy-start.4 = (bf16[4,96,128]{2,1,0:T(8,128)(2,1)S(1)}, bf16[4,96,128]{2,1,0:T(8,128)(2,1)}, u32[]{:S(2)}) copy-start(bf16[4,96,128]{2,1,0:T(8,128)(2,1)} %copy-done.3) | copy-start | bytes 294916
  131.8 18.3 %copy-start.6 = (bf16[4,96,128]{2,1,0:T(8,128)(2,1)S(1)}, bf16[4,96,128]{2,1,0:T(8,128)(2,1)}, u32[]{:S(2)}) copy-start(bf16[4,96,128]{2,1,0:T(8,128)(2,1)} %copy-done.5) | copy-start | bytes 294916
  138.4 32.7 %all-to-all-start.2 = ((bf16[16,96,128]{2,1,0:T(8,128)(2,1)}), bf16[16,96,128]{2,1,0:T(8,128)(2,1)S(1)}, u32[]{:S(2)}, u32[]{:S(2)}) async-start(bf16[16,96,128]{2,1,0:T(8,128)(2,1)} %shard_map.139), calls=%async_computation.2 | async-start | bytes 786432 | tf_op jit(solution)/shard_map/all_to_all | solution.py:428
  153.7 8.0 %collective-permute-start.10 = (bf16[384,256]{1,0:T(8,128)(2,1)S(1)}, bf16[384,256]{1,0:T(8,128)(2,1)S(1)}, u32[]{:S(2)}, u32[]{:S(2)}) collective-permute-start(bf16[384,256]{1,0:T(8,128)(2,1)S(1)} %get-tuple-element.44), channel_id=1, source_target_pairs={{0,48},{16,0},{32,16},{48,32},{1,49},{17,1},{33,17},{49,33},{2,50}... | collective-permute-start | bytes 589832 | tf_op jit(solution)/shard_map/ppermute | solution.py:417
  156.5 10.6 %collective-permute-start.11 = (bf16[384,256]{1,0:T(8,128)(2,1)S(1)}, bf16[384,256]{1,0:T(8,128)(2,1)S(1)}, u32[]{:S(2)}, u32[]{:S(2)}) collective-permute-start(bf16[384,256]{1,0:T(8,128)(2,1)S(1)} %get-tuple-element.45), channel_id=1, source_target_pairs={{0,32},{16,48},{32,0},{48,16},{1,33},{17,49},{33,1},{49,17},{2,34}... | collective-permute-start | bytes 589832 | tf_op jit(solution)/shard_map/ppermute | solution.py:417
  158.6 10.1 %collective-permute-start.12 = (bf16[384,256]{1,0:T(8,128)(2,1)S(1)}, bf16[384,256]{1,0:T(8,128)(2,1)S(1)}, u32[]{:S(2)}, u32[]{:S(2)}) collective-permute-start(bf16[384,256]{1,0:T(8,128)(2,1)S(1)} %get-tuple-element.46), channel_id=1, source_target_pairs={{0,16},{16,32},{32,48},{48,0},{1,17},{17,33},{33,49},{49,1},{2,18}... | collective-permute-start | bytes 589832 | tf_op jit(solution)/shard_map/ppermute | solution.py:417
  168.7 7.4 %copy-start.10 = (bf16[2560,64]{0,1:T(8,128)(2,1)S(1)}, bf16[2560,64]{0,1:T(8,128)(2,1)}, u32[]{:S(2)}) copy-start(bf16[2560,64]{0,1:T(8,128)(2,1)} %param.23) | copy-start | bytes 983044
  170.7 5.8 %copy-start.12 = (f32[2560]{0:T(1024)S(1)}, f32[2560]{0:T(1024)}, u32[]{:S(2)}) copy-start(f32[2560]{0:T(1024)} %param.21) | copy-start | bytes 30724
  170.7 5.8 %copy-start.13 = (f32[2560]{0:T(1024)S(1)}, f32[2560]{0:T(1024)}, u32[]{:S(2)}) copy-start(f32[2560]{0:T(1024)} %param.22) | copy-start | bytes 30724
  170.7 11.2 %copy-start.7 = (f32[64]{0:T(128)S(1)}, f32[64]{0:T(128)}, u32[]{:S(2)}) copy-start(f32[64]{0:T(128)} %param.24) | copy-start | bytes 772
  171.0 11.0 %all-to-all-start.3 = ((bf16[4,96,128]{2,1,0:T(8,128)(2,1)}), bf16[4,96,128]{2,1,0:T(8,128)(2,1)S(1)}, u32[]{:S(2)}, u32[]{:S(2)}) async-start(bf16[4,96,128]{2,1,0:T(8,128)(2,1)} %shard_map.141), calls=%async_computation.3 | async-start | bytes 196608 | tf_op jit(solution)/shard_map/all_to_all | solution.py:428
  182.0 29.2 %copy-start.14 = (f32[384]{0:T(512)S(1)}, f32[384]{0:T(512)}, u32[]{:S(2)}) copy-start(f32[384]{0:T(512)} %param.26) | copy-start | bytes 4612
  182.0 29.2 %copy-start.15 = (f32[384]{0:T(512)S(1)}, f32[384]{0:T(512)}, u32[]{:S(2)}) copy-start(f32[384]{0:T(512)} %param.27) | copy-start | bytes 4612
  182.0 36.0 %copy-start.2 = (bf16[432,384]{1,0:T(8,128)(2,1)S(1)}, bf16[432,384]{1,0:T(8,128)(2,1)}, u32[]{:S(2)}) copy-start(bf16[432,384]{1,0:T(8,128)(2,1)} %weight_ref.2) | copy-start | bytes 995332
  182.0 36.0 %copy-start.8 = (s32[16]{0:T(128)S(1)}, s32[16]{0:T(128)}, u32[]{:S(2)}) copy-start(s32[16]{0:T(128)} %tile_map.1) | copy-start | bytes 196
  207.7 10.3 %all-to-all-start.5 = ((bf16[4,4,72,128]{3,2,1,0:T(8,128)(2,1)}), bf16[4,4,72,128]{3,2,1,0:T(8,128)(2,1)S(1)}, u32[]{:S(2)}, u32[]{:S(2)}) async-start(bf16[4,4,72,128]{3,2,1,0:T(8,128)(2,1)} %shard_map.143), calls=%async_computation.5 | async-start | bytes 589824 | tf_op jit(solution)/shard_map/all_to_all | solution.py:428

commit v5 on v4

--- a/solution.py
+++ b/solution.py
@@ -95,26 +95,38 @@
     return jnp.concatenate([value, jnp.ones(value.shape, BF)], axis=1)
 
 
-def absorb(query, pieces, peak, total):
-    def rows_of(piece, first):
-        parts = [
-            ref[lo:hi, first : first + ROWS, :].reshape((hi - lo) * ROWS, HDIM)
-            for ref, lo, hi in piece
-        ]
-        return parts[0] if len(parts) == 1 else jnp.concatenate(parts, axis=0)
-
-    scores = dot_t(query, rows_of(pieces[0], 0))
-    for index, piece in enumerate(pieces):
-        more = index + 1 < len(pieces)
-        later = dot_t(query, rows_of(pieces[index + 1], 0)) if more else None
+def rows_of(piece, first):
+    parts = [
+        ref[lo:hi, first : first + ROWS, :].reshape((hi - lo) * ROWS, HDIM)
+        for ref, lo, hi in piece
+    ]
+    return parts[0] if len(parts) == 1 else jnp.concatenate(parts, axis=0)
+
+
+def absorb(groups, pieces, begin, finish):
+    steps = [(group, piece) for group in range(len(groups)) for piece in range(len(pieces))]
+
+    def scores_of(step):
+        return dot_t(groups[step[0]](), rows_of(pieces[step[1]], 0))
+
+    scores = scores_of(steps[0])
+    for index, (group, piece) in enumerate(steps):
+        if piece == 0:
+            peak, total = begin(group)
+        later = scores_of(steps[index + 1]) if index + 1 < len(steps) else None
         highest = row_peak(scores) * SCALE2
-        value = widened(rows_of(piece, ROWS))
+        value = widened(rows_of(pieces[piece], ROWS))
         newest = highest if peak is None else jnp.maximum(peak, highest)
         weights = jnp.exp2(scores * SCALE2 - newest).astype(BF)
         part = jnp.dot(weights, value, preferred_element_type=F32)
         total = part if peak is None else total * jnp.exp2(peak - newest) + part
         peak, scores = newest, later
-    return peak, total
+        if piece + 1 == len(pieces):
+            finish(group, peak, total)
+
+
+def fresh(group):
+    return None, None
 
 
 def text_part(query, text_key, text_value, text_len):
@@ -139,64 +151,110 @@
     return pieces
 
 
-def put_state(peak, total, total_ref, state_ref):
-    total_ref[...] = total[:, :HDIM]
-    lane = lax.broadcasted_iota(jnp.int32, total_ref.shape, 1)
-    state_ref[...] = jnp.where(lane < 64, peak, total[:, HDIM:])
-
-
-def get_state(total_ref, state_ref):
-    state = state_ref[...]
-    weight = jnp.broadcast_to(state[:, HDIM - 1 : HDIM], state.shape)
-    return state[:, 0:1], jnp.concatenate([total_ref[...], weight], axis=1)
-
-
-def own_kernel(info, q_ref, k0, tk_ref, tv_ref, total_ref, state_ref, text_ref):
-    query = q_ref[...].reshape(GROUP * ROWS, HDIM)
+GROUP = 4
+
+
+def rows_in(group):
+    return slice(group * GROUP * ROWS, (group + 1) * GROUP * ROWS)
+
+
+def sources_in(group):
+    return slice(group * GROUP, (group + 1) * GROUP)
+
+
+def queries_of(main_ref):
+    def query(group):
+        part = main_ref[sources_in(group), 2 * ROWS : 3 * ROWS, :]
+        return part.reshape(GROUP * ROWS, HDIM)
+
+    return [functools.partial(query, group) for group in range(NZ // GROUP)]
+
+
+def state_to(total_ref, state_ref):
+    def finish(group, peak, total):
+        total_ref[rows_in(group), :] = total[:, :HDIM]
+        lane = lax.broadcasted_iota(jnp.int32, (GROUP * ROWS, HDIM), 1)
+        state_ref[rows_in(group), :] = jnp.where(lane < 64, peak, total[:, HDIM:])
+
+    return finish
+
+
+def state_from(total_ref, state_ref):
+    def begin(group):
+        state = state_ref[rows_in(group), :]
+        weight = jnp.broadcast_to(state[:, HDIM - 1 : HDIM], state.shape)
+        return state[:, 0:1], jnp.concatenate([total_ref[rows_in(group), :], weight], axis=1)
+
+    return begin
+
+
+def own_kernel(info, main_ref, tk_ref, tv_ref, total_ref, state_ref, text_ref):
     column = pl.ds(pl.multiple_of(info[0] * HDIM, HDIM), HDIM)
-    text_ref[...] = text_part(query, tk_ref[:, column], tv_ref[:, column], info[1])
-    put_state(*absorb(query, pieces_of((k0,)), None, None), total_ref, state_ref)
-
-
-def near_kernel(q_ref, total_in, state_in, k1, k2, total_ref, state_ref):
-    query = q_ref[...].reshape(GROUP * ROWS, HDIM)
-    state = get_state(total_in, state_in)
-    put_state(*absorb(query, pieces_of((k1, k2)), *state), total_ref, state_ref)
-
-
-def far_kernel(q_ref, total_in, state_in, text_in, k3, k4, out_ref):
-    query = q_ref[...].reshape(GROUP * ROWS, HDIM)
-    state = get_state(total_in, state_in)
-    peak, total = absorb(query, pieces_of((k3, k4)), *state)
-    result = total[:, :HDIM] / total[:, HDIM:] + text_in[...]
-    out_ref[...] = result.astype(BF).reshape(GROUP, ROWS, HDIM)
+    queries = queries_of(main_ref)
+    absorb(queries, pieces_of((main_ref,)), fresh, state_to(total_ref, state_ref))
+    for group, query in enumerate(queries):
+        text = text_part(query(), tk_ref[:, column], tv_ref[:, column], info[1])
+        text_ref[rows_in(group), :] = text
+
+
+def near_kernel(main_ref, total_in, state_in, k1, k2, total_ref, state_ref):
+    begin, finish = state_from(total_in, state_in), state_to(total_ref, state_ref)
+    absorb(queries_of(main_ref), pieces_of((k1, k2)), begin, finish)
+
+
+def far_kernel(main_ref, total_in, state_in, text_in, k3, k4, out_ref):
+    def finish(group, peak, total):
+        result = total[:, :HDIM] / total[:, HDIM:] + text_in[rows_in(group), :]
+        out_ref[sources_in(group)] = result.astype(BF).reshape(GROUP, ROWS, HDIM)
+
+    begin = state_from(total_in, state_in)
+    absorb(queries_of(main_ref), pieces_of((k3, k4)), begin, finish)
+
+
+PART_ROWS = 4 * ROWS + 3 * 16
 
 
 def shared_kernel(kv_ref, q0, q1, q2, q3, p0, p1, p2, p3):
     rows = 4 * ROWS
-    lane = lax.broadcasted_iota(jnp.int32, (rows, HDIM), 1)
-    for column, out_ref in enumerate((p0, p1, p2, p3)):
-        query = jnp.concatenate([ref[column] for ref in (q0, q1, q2, q3)], axis=0)
-        peak, total = absorb(query, pieces_of((kv_ref,)), None, None)
-        out_ref[:, 0:HDIM] = (total[:, :HDIM] / total[:, HDIM:]).astype(BF)
-        level = peak + jnp.log2(total[:, HDIM:])
+    line = lax.broadcasted_iota(jnp.int32, (16, rows), 0)
+    outs = (p0, p1, p2, p3)
+
+    def query(column):
+        return jnp.concatenate([ref[column] for ref in (q0, q1, q2, q3)], axis=0)
+
+    def finish(column, peak, total):
+        outs[column][0:rows] = (total[:, :HDIM] / total[:, HDIM:]).astype(BF)
+        level = jnp.transpose(peak + jnp.log2(total[:, HDIM:]))[0:16]
         high = level.astype(BF).astype(F32)
         middle = (level - high).astype(BF).astype(F32)
         low = level - high - middle
-        terms = jnp.where(lane == 0, high, jnp.where(lane == 1, middle, low))
-        out_ref[:, HDIM:] = terms.astype(BF)
+        terms = jnp.where(line == 0, high, jnp.where(line == 1, middle, low)).astype(BF)
+        for part in range(3):
+            start = rows + 16 * part
+            outs[column][start : start + 16] = terms[:, part * HDIM : (part + 1) * HDIM]
+
+    queries = [functools.partial(query, column) for column in range(4)]
+    absorb(queries, pieces_of((kv_ref,)), fresh, finish)
+
+
+def level_of(ref):
+    columns = []
+    for part in range(3):
+        start = 4 * ROWS + 16 * part
+        terms = ref[start : start + 16].astype(F32)
+        level = terms[0:1] + terms[1:2] + terms[2:3]
+        columns.append(jnp.transpose(jnp.broadcast_to(level, (HDIM, HDIM))))
+    return jnp.concatenate(columns, axis=0)
 
 
 def merge_kernel(info, q0, q1, q2, q3, p0, p1, p2, p3, tk_ref, tv_ref, out_ref):
     query = jnp.concatenate([ref[0] for ref in (q0, q1, q2, q3)], axis=0)
-    levels = []
-    for ref in (p0, p1, p2, p3):
-        terms = ref[:, HDIM:].astype(F32)
-        levels.append(terms[:, 0:1] + terms[:, 1:2] + terms[:, 2:3])
+    parts = (p0, p1, p2, p3)
+    levels = [level_of(ref) for ref in parts]
     top = functools.reduce(jnp.maximum, levels)
     weights = [jnp.exp2(level - top) for level in levels]
     result = sum(
-        weight * ref[:, 0:HDIM].astype(F32) for weight, ref in zip(weights, (p0, p1, p2, p3))
+        weight * ref[0 : 4 * ROWS].astype(F32) for weight, ref in zip(weights, parts)
     ) / sum(weights)
     column = slice(4 * HDIM, 5 * HDIM)
     result = result + text_part(query, tk_ref[:, column], tv_ref[:, column], info[1])
@@ -205,6 +263,20 @@
         out_ref[lax.rem(info[3] + 4 - distance, 4)] = result[rows].astype(BF)
 
 
+def rows_kernel(main_ref, out_ref):
+    out_ref[...] = main_ref[:, 0 : 2 * ROWS, :]
+
+
+def key_rows(main):
+    return pl.pallas_call(
+        rows_kernel,
+        out_shape=jax.ShapeDtypeStruct((NZ, 2 * ROWS, HDIM), BF),
+        in_specs=[vmem()],
+        out_specs=vmem(),
+        compiler_params=params(),
+    )(main)
+
+
 KEYS = 6144
 
 
@@ -216,31 +288,26 @@
     )
 
 
-GROUP = 4
-QUERY_BLOCK = pl.BlockSpec((GROUP, ROWS, HDIM), lambda i: (i, 2, 0))
-STATE_BLOCK = pl.BlockSpec((GROUP * ROWS, HDIM), lambda i: (i, 0))
 STATE = jax.ShapeDtypeStruct((NZ * ROWS, HDIM), F32)
 
 
 def main_own(info, main, text_keys, text_values):
     return pl.pallas_call(
         own_kernel,
-        grid=(NZ // GROUP,),
         out_shape=(STATE,) * 3,
-        in_specs=[smem(), QUERY_BLOCK, vmem(), vmem(), vmem()],
-        out_specs=(STATE_BLOCK,) * 3,
+        in_specs=[smem()] + [vmem()] * 3,
+        out_specs=(vmem(),) * 3,
         compiler_params=params(),
         cost_estimate=cost(NZ * ROWS, NZ * ROWS + TXT),
-    )(info, main, main, text_keys, text_values)
+    )(info, main, text_keys, text_values)
 
 
 def main_near(main, total, state, kv):
     return pl.pallas_call(
         near_kernel,
-        grid=(NZ // GROUP,),
         out_shape=(STATE,) * 2,
-        in_specs=[QUERY_BLOCK, STATE_BLOCK, STATE_BLOCK] + [vmem()] * len(kv),
-        out_specs=(STATE_BLOCK,) * 2,
+        in_specs=[vmem()] * 5,
+        out_specs=(vmem(),) * 2,
         compiler_params=params(),
         cost_estimate=cost(NZ * ROWS, 2 * NZ * ROWS),
     )(main, total, state, *kv)
@@ -249,17 +316,16 @@
 def main_far(main, total, state, text, kv):
     return pl.pallas_call(
         far_kernel,
-        grid=(NZ // GROUP,),
         out_shape=jax.ShapeDtypeStruct((NZ, ROWS, HDIM), BF),
-        in_specs=[QUERY_BLOCK] + [STATE_BLOCK] * 3 + [vmem()] * len(kv),
-        out_specs=pl.BlockSpec((GROUP, ROWS, HDIM), lambda i: (i, 0, 0)),
+        in_specs=[vmem()] * 6,
+        out_specs=vmem(),
         compiler_params=params(),
         cost_estimate=cost(NZ * ROWS, NZ * ROWS),
     )(main, total, state, text, *kv)
 
 
 def shared_attention(kv, columns):
-    part = jax.ShapeDtypeStruct((4 * ROWS, 2 * HDIM), BF)
+    part = jax.ShapeDtypeStruct((PART_ROWS, HDIM), BF)
     return pl.pallas_call(
         shared_kernel,
         out_shape=(part,) * 4,
@@ -452,7 +518,7 @@
     main = exchange(main_send, Z)
     main, last, shared_send = lax.optimization_barrier((main, last, shared_send))
     shared = exchange(shared_send, Z)
-    near, far = around(main[:, : 2 * ROWS], "x")
+    near, far = around(key_rows(main), "x")
     total, state, text = main_own(info, main, text_keys, text_values)
     total, state = main_near(main, total, state, near)
     out = main_far(main, total, state, text, far)

time: 222 us -> 218 us (0.982)
    ppermute x13, waiting for transfers between devices: 53.1 us -> 49.7 us  [shift(): lax.ppermute(block, axis, [(i, (i + distance) % 4) for i in range(4)])]
    pallas_call x3 -> x4, Pallas kernels: 22.2 us -> 20.7 us  [the longest x1 8.82 us: main_near(): pl.pallas_call(near_kernel, out_shape=(STATE,) * 2, in_specs=[vmem()] * 5...]
  transfers between devices with their start and end apart: 18 -> 18, of which waited for: 10 -> 9; matrix products, arithmetic and copies ran while one was open for 2% -> 1% of each run, Pallas kernels for 13% -> 12%
where the time goes in v5:
time: 218 us; the launch traced here: 217 us
  starting transfers between devices  90.5 us (42%)
  waiting for transfers between devices  63.7 us (29%)
  Pallas kernels  33.7 us (15%)
  blocking collectives  22 us (10%)
  local copies, waits for them, and re-layouts  5.48 us (3%)
    ppermute x13, waiting for transfers between devices, shift(): lax.ppermute(block, axis, [(i, (i + distance) % 4) for i in range(4)])  49.7 us
    all_to_all x5, starting transfers between devices, exchange(): return lax.all_to_all(block, axis, split_axis=0, concat_axis=0, tiled=True)  45.4 us
    ppermute x13, starting transfers between devices, shift(): lax.ppermute(block, axis, [(i, (i + distance) % 4) for i in range(4)])  45 us
    all_to_all x1, blocking collectives, exchange(): return lax.all_to_all(block, axis, split_axis=0, concat_axis=0, tiled=True)  22 us
    all_to_all x5, waiting for transfers between devices, exchange(): return lax.all_to_all(block, axis, split_axis=0, concat_axis=0, tiled=True)  13.9 us
    pallas_call x1, Pallas kernels, main_near(): pl.pallas_call(near_kernel, out_shape=(STATE,) * 2, in_specs=[vmem()] * 5...  8.82 us
    pallas_call x1, Pallas kernels, main_far(): pl.pallas_call(far_kernel, out_shape=jax.ShapeDtypeStruct((NZ, ROWS, HDIM...  6.16 us
    pallas_call x1, Pallas kernels, main_own(): pl.pallas_call(own_kernel, out_shape=(STATE,) * 3, in_specs=[smem()] + [v...  5.68 us
  transfers between devices with their start and end apart: 18, of which 9 were waited for; matrix products, arithmetic and copies ran while one was open for 1% of the time, Pallas kernels for 12%

profile of v5, /device:TPU:24, one launch (start us, length us, event | category | flops | bytes accessed | tf_op | source)
XLA Modules:
  0.0 216.6 jit_solution(9364228177155946981)
XLA Ops:
  0.0 2.9 %shard_map.136 = (bf16[16,288,128]{2,1,0:T(8,128)(2,1)}, bf16[16,192,128]{2,1,0:T(8,128)(2,1)}, bf16[4,96,128]{2,1,0:T(8,128)(2,1)}) custom-call(bf16[96,2560]{1,0:T(8,128)(2,1)} %q_hbm.1, bf16[96,2560]{1,0:T(8,128)(2,1)} %k_hbm.1, bf16[96,2560]{1,0:T(8,128)(2,1)} %v_hbm.1), custom_call_target="tpu_custom_call" | custom-call | tf_op jit(solution)/shard_map/pallas_call | solution.py:68
  2.9 15.3 %all-to-all-start = ((bf16[16,288,128]{2,1,0:T(8,128)(2,1)}), bf16[16,288,128]{2,1,0:T(8,128)(2,1)S(1)}, u32[]{:S(2)}, u32[]{:S(2)}) async-start(bf16[16,288,128]{2,1,0:T(8,128)(2,1)} %get-tuple-element.27), calls=%async_computation | async-start | bytes 2359296 | tf_op jit(solution)/shard_map/all_to_all | solution.py:494
  18.3 3.4 %collective-permute-start = (bf16[4,96,128]{2,1,0:T(8,128)(2,1)S(1)}, bf16[4,96,128]{2,1,0:T(8,128)(2,1)S(1)}, u32[]{:S(2)}, u32[]{:S(2)}) collective-permute-start(bf16[4,96,128]{2,1,0:T(8,128)(2,1)S(1)} %copy-done.14), channel_id=1, source_target_pairs={{0,16},{16,32},{32,48},{48,0},{1,17},{17,33},{33,49},{49,1},{2,18}... | collective-permute-start | bytes 294920 | tf_op jit(solution)/shard_map/ppermute | solution.py:483
  21.7 4.6 %collective-permute-start.1 = (bf16[4,96,128]{2,1,0:T(8,128)(2,1)S(1)}, bf16[4,96,128]{2,1,0:T(8,128)(2,1)S(1)}, u32[]{:S(2)}, u32[]{:S(2)}) collective-permute-start(bf16[4,96,128]{2,1,0:T(8,128)(2,1)S(1)} %copy-done.14), channel_id=1, source_target_pairs={{0,32},{16,48},{32,0},{48,16},{1,33},{17,49},{33,1},{49,17},{2,34}... | collective-permute-start | bytes 294920 | tf_op jit(solution)/shard_map/ppermute | solution.py:483
  26.3 3.3 %collective-permute-start.2 = (bf16[4,96,128]{2,1,0:T(8,128)(2,1)S(1)}, bf16[4,96,128]{2,1,0:T(8,128)(2,1)S(1)}, u32[]{:S(2)}, u32[]{:S(2)}) collective-permute-start(bf16[4,96,128]{2,1,0:T(8,128)(2,1)S(1)} %copy-done.14), channel_id=1, source_target_pairs={{0,48},{16,0},{32,16},{48,32},{1,49},{17,1},{33,17},{49,33},{2,50}... | collective-permute-start | bytes 294920 | tf_op jit(solution)/shard_map/ppermute | solution.py:483
  29.7 0.0 collective-permute-done.1
  29.7 3.1 %collective-permute-done.2 = bf16[4,96,128]{2,1,0:T(8,128)(2,1)S(1)} collective-permute-done((bf16[4,96,128]{2,1,0:T(8,128)(2,1)S(1)}, bf16[4,96,128]{2,1,0:T(8,128)(2,1)S(1)}, u32[]{:S(2)}, u32[]{:S(2)}) %collective-permute-start.2) | collective-permute-done | bytes 98336 | tf_op jit(solution)/shard_map/ppermute | solution.py:483
  32.8 0.1 pad_maximum_fusion
  32.9 3.8 %collective-permute-start.3 = (bf16[4,96,128]{2,1,0:T(8,128)(2,1)S(1)}, bf16[4,96,128]{2,1,0:T(8,128)(2,1)S(1)}, u32[]{:S(2)}, u32[]{:S(2)}) collective-permute-start(bf16[4,96,128]{2,1,0:T(8,128)(2,1)S(1)} %get-tuple-element.51), channel_id=1, source_target_pairs={{0,1},{1,2},{2,3},{3,0},{4,5},{5,6},{6,7},{7,4},{8,9},{9,10},{10,1... | collective-permute-start | bytes 294920 | tf_op jit(solution)/shard_map/ppermute | solution.py:483
  36.8 4.3 %collective-permute-start.4 = (bf16[4,96,128]{2,1,0:T(8,128)(2,1)S(1)}, bf16[4,96,128]{2,1,0:T(8,128)(2,1)S(1)}, u32[]{:S(2)}, u32[]{:S(2)}) collective-permute-start(bf16[4,96,128]{2,1,0:T(8,128)(2,1)S(1)} %get-tuple-element.50), channel_id=1, source_target_pairs={{0,2},{1,3},{2,0},{3,1},{4,6},{5,7},{6,4},{7,5},{8,10},{9,11},{10,... | collective-permute-start | bytes 294920 | tf_op jit(solution)/shard_map/ppermute | solution.py:483
  41.1 3.4 %collective-permute-start.5 = (bf16[4,96,128]{2,1,0:T(8,128)(2,1)S(1)}, bf16[4,96,128]{2,1,0:T(8,128)(2,1)S(1)}, u32[]{:S(2)}, u32[]{:S(2)}) collective-permute-start(bf16[4,96,128]{2,1,0:T(8,128)(2,1)S(1)} %get-tuple-element.49), channel_id=1, source_target_pairs={{0,3},{1,0},{2,1},{3,2},{4,7},{5,4},{6,5},{7,6},{8,11},{9,8},{10,9... | collective-permute-start | bytes 294920 | tf_op jit(solution)/shard_map/ppermute | solution.py:483
  44.4 32.2 %collective-permute-done.3.q1 = bf16[4,96,128]{2,1,0:T(8,128)(2,1)S(1)} collective-permute-done((bf16[4,96,128]{2,1,0:T(8,128)(2,1)S(1)}, bf16[4,96,128]{2,1,0:T(8,128)(2,1)S(1)}, u32[]{:S(2)}, u32[]{:S(2)}) %collective-permute-start.3) | collective-permute-done | bytes 98336 | tf_op jit(solution)/shard_map/ppermute | solution.py:483
  76.6 0.6 copy-done.5
  77.3 2.3 %collective-permute-done.4.q2 = bf16[4,96,128]{2,1,0:T(8,128)(2,1)S(1)} collective-permute-done((bf16[4,96,128]{2,1,0:T(8,128)(2,1)S(1)}, bf16[4,96,128]{2,1,0:T(8,128)(2,1)S(1)}, u32[]{:S(2)}, u32[]{:S(2)}) %collective-permute-start.4) | collective-permute-done | bytes 98336 | tf_op jit(solution)/shard_map/ppermute | solution.py:483
  79.6 0.6 copy-done.7
  80.2 0.6 copy-done.9
  80.8 9.8 %all-to-all-start.1 = ((bf16[16,192,128]{2,1,0:T(8,128)(2,1)}), bf16[16,192,128]{2,1,0:T(8,128)(2,1)S(1)}, u32[]{:S(2)}, u32[]{:S(2)}) async-start(bf16[16,192,128]{2,1,0:T(8,128)(2,1)} %get-tuple-element.36), calls=%async_computation.1 | async-start | bytes 1572864 | tf_op jit(solution)/shard_map/all_to_all | solution.py:494
  90.6 0.1 shard_map.138
  90.7 3.5 %collective-permute-start.6 = (bf16[16,192,128]{2,1,0:T(8,128)(2,1)S(1)}, bf16[16,192,128]{2,1,0:T(8,128)(2,1)}, u32[]{:S(2)}, u32[]{:S(2)}) collective-permute-start(bf16[16,192,128]{2,1,0:T(8,128)(2,1)S(1)} %shard_map.138), channel_id=1, source_target_pairs={{0,16},{16,32},{32,48},{48,0},{1,17},{17,33},{33,49},{49,1},{2,18}... | collective-permute-start | bytes 2359304 | tf_op jit(solution)/shard_map/ppermute | solution.py:483
  94.3 3.7 %collective-permute-start.7 = (bf16[16,192,128]{2,1,0:T(8,128)(2,1)S(1)}, bf16[16,192,128]{2,1,0:T(8,128)(2,1)}, u32[]{:S(2)}, u32[]{:S(2)}) collective-permute-start(bf16[16,192,128]{2,1,0:T(8,128)(2,1)S(1)} %shard_map.138), channel_id=1, source_target_pairs={{0,48},{16,0},{32,16},{48,32},{1,49},{17,1},{33,17},{49,33},{2,50}... | collective-permute-start | bytes 2359304 | tf_op jit(solution)/shard_map/ppermute | solution.py:483
  98.6 0.1 pad_add_fusion.info
  98.7 1.1 copy-done.2
  99.7 5.7 %shard_map.137 = (f32[1536,128]{1,0:T(8,128)S(1)}, f32[1536,128]{1,0:T(8,128)S(1)}, f32[1536,128]{1,0:T(8,128)S(1)}) custom-call(s32[4]{0:T(128)S(1)} %pad_add_fusion.info, bf16[16,288,128]{2,1,0:T(8,128)(2,1)} %copy-done, bf16[512,640]{1,0:T(8,128)(2,1)S(1)} %copy-done.1, bf16[512,640]{1,0:T(8,128)(2,1)S(1)} %copy-done.2), custom_call_target="tpu_custom_call" | custom-call | flops 3221225472 | bytes 1048576 | tf_op jit(solution)/shard_map/pallas_call | solution.py:295
  105.4 6.7 %collective-permute-done.6.k1 = bf16[16,192,128]{2,1,0:T(8,128)(2,1)} collective-permute-done((bf16[16,192,128]{2,1,0:T(8,128)(2,1)S(1)}, bf16[16,192,128]{2,1,0:T(8,128)(2,1)}, u32[]{:S(2)}, u32[]{:S(2)}) %collective-permute-start.6) | collective-permute-done | bytes 786464 | tf_op jit(solution)/shard_map/ppermute | solution.py:483
  112.1 1.0 slice.28
  113.2 2.2 %collective-permute-start.8 = (bf16[8,192,128]{2,1,0:T(8,128)(2,1)S(1)}, bf16[8,192,128]{2,1,0:T(8,128)(2,1)S(1)}, u32[]{:S(2)}, u32[]{:S(2)}) collective-permute-start(bf16[8,192,128]{2,1,0:T(8,128)(2,1)S(1)} %slice.28), channel_id=1, source_target_pairs={{0,16},{16,32},{32,48},{48,0},{1,17},{17,33},{33,49},{49,1},{2,18}... | collective-permute-start | bytes 1179656 | tf_op jit(solution)/shard_map/ppermute | solution.py:483
  115.4 1.0 slice.29
  116.4 5.0 %collective-permute-start.9 = (bf16[8,192,128]{2,1,0:T(8,128)(2,1)S(1)}, bf16[8,192,128]{2,1,0:T(8,128)(2,1)S(1)}, u32[]{:S(2)}, u32[]{:S(2)}) collective-permute-start(bf16[8,192,128]{2,1,0:T(8,128)(2,1)S(1)} %slice.29), channel_id=1, source_target_pairs={{0,48},{16,0},{32,16},{48,32},{1,49},{17,1},{33,17},{49,33},{2,50}... | collective-permute-start | bytes 1179656 | tf_op jit(solution)/shard_map/ppermute | solution.py:483
  121.5 8.8 %shard_map.139 = (f32[1536,128]{1,0:T(8,128)S(1)}, f32[1536,128]{1,0:T(8,128)S(1)}) custom-call(bf16[16,288,128]{2,1,0:T(8,128)(2,1)} %copy-done, f32[1536,128]{1,0:T(8,128)S(1)} %get-tuple-element.31.total_in, f32[1536,128]{1,0:T(8,128)S(1)} %get-tuple-element.32.state_in, bf16[16,192,128]{2,1,0:T(8,128)(2,1)} %collective-permute-done.6.k1, ...), custom_call_target="tpu_custom_call" | custom-call | flops 4831838208 | bytes 1572864 | tf_op jit(solution)/shard_map/pallas_call | solution.py:306
  130.3 6.2 %shard_map.140 = bf16[16,96,128]{2,1,0:T(8,128)(2,1)} custom-call(bf16[16,288,128]{2,1,0:T(8,128)(2,1)} %copy-done, f32[1536,128]{1,0:T(8,128)S(1)} %get-tuple-element.33.total_in, f32[1536,128]{1,0:T(8,128)S(1)} %get-tuple-element.34.state_in, f32[1536,128]{1,0:T(8,128)S(1)} %get-tuple-element.35.text_in, ...), custom_call_target="tpu_custom_call" | custom-call | flops 2415919104 | bytes 786432 | tf_op jit(solution)/shard_map/pallas_call | solution.py:317
  136.5 11.8 %all-to-all-start.2 = ((bf16[16,96,128]{2,1,0:T(8,128)(2,1)}), bf16[16,96,128]{2,1,0:T(8,128)(2,1)S(1)}, u32[]{:S(2)}, u32[]{:S(2)}) async-start(bf16[16,96,128]{2,1,0:T(8,128)(2,1)} %shard_map.140), calls=%async_computation.2 | async-start | bytes 786432 | tf_op jit(solution)/shard_map/all_to_all | solution.py:494
  148.3 3.4 %shard_map.141 = (bf16[432,128]{1,0:T(8,128)(2,1)S(1)}, bf16[432,128]{1,0:T(8,128)(2,1)S(1)}, bf16[432,128]{1,0:T(8,128)(2,1)S(1)}, bf16[432,128]{1,0:T(8,128)(2,1)S(1)}) custom-call(bf16[16,192,128]{2,1,0:T(8,128)(2,1)S(1)} %all-to-all-done.1.kv_ref, bf16[4,96,128]{2,1,0:T(8,128)(2,1)S(1)} %get-tuple-element.38.q0, bf16[4,96,128]{2,1,0:T(8,128)(2,1)S(1)} %copy-done.6, ...), custom_call_target="tpu_custom_call" | custom-call | flops 2415919104 | bytes 786432 | tf_op jit(solution)/shard_map/pallas_call | solution.py:329
  151.7 2.2 %collective-permute-start.10 = (bf16[432,128]{1,0:T(8,128)(2,1)S(1)}, bf16[432,128]{1,0:T(8,128)(2,1)S(1)}, u32[]{:S(2)}, u32[]{:S(2)}) collective-permute-start(bf16[432,128]{1,0:T(8,128)(2,1)S(1)} %get-tuple-element.44), channel_id=1, source_target_pairs={{0,48},{16,0},{32,16},{48,32},{1,49},{17,1},{33,17},{49,33},{2,50}... | collective-permute-start | bytes 331784 | tf_op jit(solution)/shard_map/ppermute | solution.py:483
  153.9 2.7 %collective-permute-start.11 = (bf16[432,128]{1,0:T(8,128)(2,1)S(1)}, bf16[432,128]{1,0:T(8,128)(2,1)S(1)}, u32[]{:S(2)}, u32[]{:S(2)}) collective-permute-start(bf16[432,128]{1,0:T(8,128)(2,1)S(1)} %get-tuple-element.45), channel_id=1, source_target_pairs={{0,32},{16,48},{32,0},{48,16},{1,33},{17,49},{33,1},{49,17},{2,34}... | collective-permute-start | bytes 331784 | tf_op jit(solution)/shard_map/ppermute | solution.py:483
  156.6 2.8 %collective-permute-start.12 = (bf16[432,128]{1,0:T(8,128)(2,1)S(1)}, bf16[432,128]{1,0:T(8,128)(2,1)S(1)}, u32[]{:S(2)}, u32[]{:S(2)}) collective-permute-start(bf16[432,128]{1,0:T(8,128)(2,1)S(1)} %get-tuple-element.46), channel_id=1, source_target_pairs={{0,16},{16,32},{32,48},{48,0},{1,17},{17,33},{33,49},{49,1},{2,18}... | collective-permute-start | bytes 331784 | tf_op jit(solution)/shard_map/ppermute | solution.py:483
  159.5 3.1 %collective-permute-done.11.p2 = bf16[432,128]{1,0:T(8,128)(2,1)S(1)} collective-permute-done((bf16[432,128]{1,0:T(8,128)(2,1)S(1)}, bf16[432,128]{1,0:T(8,128)(2,1)S(1)}, u32[]{:S(2)}, u32[]{:S(2)}) %collective-permute-start.11) | collective-permute-done | bytes 110624 | tf_op jit(solution)/shard_map/ppermute | solution.py:483
  162.5 2.3 %collective-permute-done.12.p3 = bf16[432,128]{1,0:T(8,128)(2,1)S(1)} collective-permute-done((bf16[432,128]{1,0:T(8,128)(2,1)S(1)}, bf16[432,128]{1,0:T(8,128)(2,1)S(1)}, u32[]{:S(2)}, u32[]{:S(2)}) %collective-permute-start.12) | collective-permute-done | bytes 110624 | tf_op jit(solution)/shard_map/ppermute | solution.py:483
  164.8 2.0 shard_map.142
  166.8 1.7 all-to-all-done.2.back_ref
  168.5 5.1 %all-to-all-start.3 = ((bf16[4,96,128]{2,1,0:T(8,128)(2,1)}), bf16[4,96,128]{2,1,0:T(8,128)(2,1)S(1)}, u32[]{:S(2)}, u32[]{:S(2)}) async-start(bf16[4,96,128]{2,1,0:T(8,128)(2,1)} %shard_map.142), calls=%async_computation.3 | async-start | bytes 196608 | tf_op jit(solution)/shard_map/all_to_all | solution.py:494
  173.6 0.3 copy.15.weight_ref
  174.0 5.4 %all-to-all-done.3.shared_ref = bf16[4,96,128]{2,1,0:T(8,128)(2,1)S(1)} async-done(((bf16[4,96,128]{2,1,0:T(8,128)(2,1)}), bf16[4,96,128]{2,1,0:T(8,128)(2,1)S(1)}, u32[]{:S(2)}, u32[]{:S(2)}) %all-to-all-start.3) | async-done | bytes 98336 | tf_op jit(solution)/shard_map/all_to_all | solution.py:494
  179.5 0.7 shard_map.143
  180.2 22.0 %all_to_all.30.line_ref = bf16[16,48,128]{2,1,0:T(8,128)(2,1)S(1)} all-to-all(bf16[16,48,128]{2,1,0:T(8,128)(2,1)S(1)} %shard_map.143), channel_id=1, replica_groups=mesh['clip'=8,'x'=4,'zh'=4,'zl'=4] {'zh','zl'}, dimensions={0} | all-to-all | bytes 393216 | tf_op jit(solution)/shard_map/all_to_all | solution.py:494
  202.3 1.4 shard_map.144
  203.7 3.5 %all-to-all-start.5 = ((bf16[4,4,72,128]{3,2,1,0:T(8,128)(2,1)}), bf16[4,4,72,128]{3,2,1,0:T(8,128)(2,1)S(1)}, u32[]{:S(2)}, u32[]{:S(2)}) async-start(bf16[4,4,72,128]{3,2,1,0:T(8,128)(2,1)} %shard_map.144), calls=%async_computation.5 | async-start | bytes 589824 | tf_op jit(solution)/shard_map/all_to_all | solution.py:494
  207.2 6.8 %all-to-all-done.5 = bf16[4,4,72,128]{3,2,1,0:T(8,128)(2,1)S(1)} async-done(((bf16[4,4,72,128]{3,2,1,0:T(8,128)(2,1)}), bf16[4,4,72,128]{3,2,1,0:T(8,128)(2,1)S(1)}, u32[]{:S(2)}, u32[]{:S(2)}) %all-to-all-start.5) | async-done | bytes 294944 | tf_op jit(solution)/shard_map/all_to_all | solution.py:494
  214.0 2.6 %shard_map.145 = bf16[8,48,384]{2,1,0:T(8,128)(2,1)} custom-call(s32[4]{0:T(128)S(1)} %pad_add_fusion.info, s32[16]{0:T(128)S(1)} %copy-done.12, bf16[16,72,128]{2,1,0:T(8,128)(2,1)S(1)} %bitcast.18, bf16[432,384]{1,0:T(8,128)(2,1)S(1)} %copy-done.4, f32[1,384]{1,0:T(1,128)S(1)} %broadcast_in_dim.21.bias_ref, f32[1,384]{1,0:T(1,128)S(1)} %broadcast_in_dim.22.gain_ref), custom_call_target="tpu_custom_call" | custom-call | tf_op jit(solution)/shard_map/pallas_call | solution.py:469
  (47 shorter events, 0.2 us)
Async XLA Ops:
  2.9 15.4 %copy-start.14 = (bf16[4,96,128]{2,1,0:T(8,128)(2,1)S(1)}, bf16[4,96,128]{2,1,0:T(8,128)(2,1)}, u32[]{:S(2)}) copy-start(bf16[4,96,128]{2,1,0:T(8,128)(2,1)} %get-tuple-element.28) | copy-start | bytes 294916
  2.9 77.9 %all-to-all-start = ((bf16[16,288,128]{2,1,0:T(8,128)(2,1)}), bf16[16,288,128]{2,1,0:T(8,128)(2,1)S(1)}, u32[]{:S(2)}, u32[]{:S(2)}) async-start(bf16[16,288,128]{2,1,0:T(8,128)(2,1)} %get-tuple-element.27), calls=%async_computation | async-start | bytes 2359296 | tf_op jit(solution)/shard_map/all_to_all | solution.py:494
  18.3 11.4 %collective-permute-start = (bf16[4,96,128]{2,1,0:T(8,128)(2,1)S(1)}, bf16[4,96,128]{2,1,0:T(8,128)(2,1)S(1)}, u32[]{:S(2)}, u32[]{:S(2)}) collective-permute-start(bf16[4,96,128]{2,1,0:T(8,128)(2,1)S(1)} %copy-done.14), channel_id=1, source_target_pairs={{0,16},{16,32},{32,48},{48,0},{1,17},{17,33},{33,49},{49,1},{2,18}... | collective-permute-start | bytes 294920 | tf_op jit(solution)/shard_map/ppermute | solution.py:483
  21.7 8.0 %collective-permute-start.1 = (bf16[4,96,128]{2,1,0:T(8,128)(2,1)S(1)}, bf16[4,96,128]{2,1,0:T(8,128)(2,1)S(1)}, u32[]{:S(2)}, u32[]{:S(2)}) collective-permute-start(bf16[4,96,128]{2,1,0:T(8,128)(2,1)S(1)} %copy-done.14), channel_id=1, source_target_pairs={{0,32},{16,48},{32,0},{48,16},{1,33},{17,49},{33,1},{49,17},{2,34}... | collective-permute-start | bytes 294920 | tf_op jit(solution)/shard_map/ppermute | solution.py:483
  26.3 6.5 %collective-permute-start.2 = (bf16[4,96,128]{2,1,0:T(8,128)(2,1)S(1)}, bf16[4,96,128]{2,1,0:T(8,128)(2,1)S(1)}, u32[]{:S(2)}, u32[]{:S(2)}) collective-permute-start(bf16[4,96,128]{2,1,0:T(8,128)(2,1)S(1)} %copy-done.14), channel_id=1, source_target_pairs={{0,48},{16,0},{32,16},{48,32},{1,49},{17,1},{33,17},{49,33},{2,50}... | collective-permute-start | bytes 294920 | tf_op jit(solution)/shard_map/ppermute | solution.py:483
  32.9 43.7 %collective-permute-start.3 = (bf16[4,96,128]{2,1,0:T(8,128)(2,1)S(1)}, bf16[4,96,128]{2,1,0:T(8,128)(2,1)S(1)}, u32[]{:S(2)}, u32[]{:S(2)}) collective-permute-start(bf16[4,96,128]{2,1,0:T(8,128)(2,1)S(1)} %get-tuple-element.51), channel_id=1, source_target_pairs={{0,1},{1,2},{2,3},{3,0},{4,5},{5,6},{6,7},{7,4},{8,9},{9,10},{10,1... | collective-permute-start | bytes 294920 | tf_op jit(solution)/shard_map/ppermute | solution.py:483
  36.8 42.8 %collective-permute-start.4 = (bf16[4,96,128]{2,1,0:T(8,128)(2,1)S(1)}, bf16[4,96,128]{2,1,0:T(8,128)(2,1)S(1)}, u32[]{:S(2)}, u32[]{:S(2)}) collective-permute-start(bf16[4,96,128]{2,1,0:T(8,128)(2,1)S(1)} %get-tuple-element.50), channel_id=1, source_target_pairs={{0,2},{1,3},{2,0},{3,1},{4,6},{5,7},{6,4},{7,5},{8,10},{9,11},{10,... | collective-permute-start | bytes 294920 | tf_op jit(solution)/shard_map/ppermute | solution.py:483
  41.1 39.1 %collective-permute-start.5 = (bf16[4,96,128]{2,1,0:T(8,128)(2,1)S(1)}, bf16[4,96,128]{2,1,0:T(8,128)(2,1)S(1)}, u32[]{:S(2)}, u32[]{:S(2)}) collective-permute-start(bf16[4,96,128]{2,1,0:T(8,128)(2,1)S(1)} %get-tuple-element.49), channel_id=1, source_target_pairs={{0,3},{1,0},{2,1},{3,2},{4,7},{5,4},{6,5},{7,6},{8,11},{9,8},{10,9... | collective-permute-start | bytes 294920 | tf_op jit(solution)/shard_map/ppermute | solution.py:483
  76.6 0.6 copy-start.5
  79.6 0.6 copy-start.7
  80.2 0.6 copy-start.9
  80.8 9.9 %copy-start = (bf16[16,288,128]{2,1,0:T(8,128)(2,1)}, bf16[16,288,128]{2,1,0:T(8,128)(2,1)S(1)}, u32[]{:S(2)}) copy-start(bf16[16,288,128]{2,1,0:T(8,128)(2,1)S(1)} %all-to-all-done.main_ref) | copy-start | bytes 3538948
  80.8 55.7 %all-to-all-start.1 = ((bf16[16,192,128]{2,1,0:T(8,128)(2,1)}), bf16[16,192,128]{2,1,0:T(8,128)(2,1)S(1)}, u32[]{:S(2)}, u32[]{:S(2)}) async-start(bf16[16,192,128]{2,1,0:T(8,128)(2,1)} %get-tuple-element.36), calls=%async_computation.1 | async-start | bytes 1572864 | tf_op jit(solution)/shard_map/all_to_all | solution.py:494
  90.6 8.0 %copy-start.1 = (bf16[512,640]{1,0:T(8,128)(2,1)S(1)}, bf16[512,640]{1,0:T(8,128)(2,1)}, u32[]{:S(2)}) copy-start(bf16[512,640]{1,0:T(8,128)(2,1)} %tk_ref.3) | copy-start | bytes 1966084
  90.7 21.4 %collective-permute-start.6 = (bf16[16,192,128]{2,1,0:T(8,128)(2,1)S(1)}, bf16[16,192,128]{2,1,0:T(8,128)(2,1)}, u32[]{:S(2)}, u32[]{:S(2)}) collective-permute-start(bf16[16,192,128]{2,1,0:T(8,128)(2,1)S(1)} %shard_map.138), channel_id=1, source_target_pairs={{0,16},{16,32},{32,48},{48,0},{1,17},{17,33},{33,49},{49,1},{2,18}... | collective-permute-start | bytes 2359304 | tf_op jit(solution)/shard_map/ppermute | solution.py:483
  94.3 21.1 %collective-permute-start.7 = (bf16[16,192,128]{2,1,0:T(8,128)(2,1)S(1)}, bf16[16,192,128]{2,1,0:T(8,128)(2,1)}, u32[]{:S(2)}, u32[]{:S(2)}) collective-permute-start(bf16[16,192,128]{2,1,0:T(8,128)(2,1)S(1)} %shard_map.138), channel_id=1, source_target_pairs={{0,48},{16,0},{32,16},{48,32},{1,49},{17,1},{33,17},{49,33},{2,50}... | collective-permute-start | bytes 2359304 | tf_op jit(solution)/shard_map/ppermute | solution.py:483
  98.7 1.1 copy-start.2
  113.2 17.1 %collective-permute-start.8 = (bf16[8,192,128]{2,1,0:T(8,128)(2,1)S(1)}, bf16[8,192,128]{2,1,0:T(8,128)(2,1)S(1)}, u32[]{:S(2)}, u32[]{:S(2)}) collective-permute-start(bf16[8,192,128]{2,1,0:T(8,128)(2,1)S(1)} %slice.28), channel_id=1, source_target_pairs={{0,16},{16,32},{32,48},{48,0},{1,17},{17,33},{33,49},{49,1},{2,18}... | collective-permute-start | bytes 1179656 | tf_op jit(solution)/shard_map/ppermute | solution.py:483
  116.4 13.9 %collective-permute-start.9 = (bf16[8,192,128]{2,1,0:T(8,128)(2,1)S(1)}, bf16[8,192,128]{2,1,0:T(8,128)(2,1)S(1)}, u32[]{:S(2)}, u32[]{:S(2)}) collective-permute-start(bf16[8,192,128]{2,1,0:T(8,128)(2,1)S(1)} %slice.29), channel_id=1, source_target_pairs={{0,48},{16,0},{32,16},{48,32},{1,49},{17,1},{33,17},{49,33},{2,50}... | collective-permute-start | bytes 1179656 | tf_op jit(solution)/shard_map/ppermute | solution.py:483
  130.3 18.0 %copy-start.6 = (bf16[4,96,128]{2,1,0:T(8,128)(2,1)S(1)}, bf16[4,96,128]{2,1,0:T(8,128)(2,1)}, u32[]{:S(2)}) copy-start(bf16[4,96,128]{2,1,0:T(8,128)(2,1)} %copy-done.5) | copy-start | bytes 294916
  130.3 18.0 %copy-start.8 = (bf16[4,96,128]{2,1,0:T(8,128)(2,1)S(1)}, bf16[4,96,128]{2,1,0:T(8,128)(2,1)}, u32[]{:S(2)}) copy-start(bf16[4,96,128]{2,1,0:T(8,128)(2,1)} %copy-done.7) | copy-start | bytes 294916
  130.3 18.0 %copy-start.10 = (bf16[4,96,128]{2,1,0:T(8,128)(2,1)S(1)}, bf16[4,96,128]{2,1,0:T(8,128)(2,1)}, u32[]{:S(2)}) copy-start(bf16[4,96,128]{2,1,0:T(8,128)(2,1)} %copy-done.9) | copy-start | bytes 294916
  136.5 32.0 %all-to-all-start.2 = ((bf16[16,96,128]{2,1,0:T(8,128)(2,1)}), bf16[16,96,128]{2,1,0:T(8,128)(2,1)S(1)}, u32[]{:S(2)}, u32[]{:S(2)}) async-start(bf16[16,96,128]{2,1,0:T(8,128)(2,1)} %shard_map.140), calls=%async_computation.2 | async-start | bytes 786432 | tf_op jit(solution)/shard_map/all_to_all | solution.py:494
  148.3 16.5 %copy-start.3 = (bf16[512,640]{1,0:T(8,128)(2,1)S(1)}, bf16[512,640]{1,0:T(8,128)(2,1)}, u32[]{:S(2)}) copy-start(bf16[512,640]{1,0:T(8,128)(2,1)} %tv_ref.3) | copy-start | bytes 1966084
  151.7 7.8 %collective-permute-start.10 = (bf16[432,128]{1,0:T(8,128)(2,1)S(1)}, bf16[432,128]{1,0:T(8,128)(2,1)S(1)}, u32[]{:S(2)}, u32[]{:S(2)}) collective-permute-start(bf16[432,128]{1,0:T(8,128)(2,1)S(1)} %get-tuple-element.44), channel_id=1, source_target_pairs={{0,48},{16,0},{32,16},{48,32},{1,49},{17,1},{33,17},{49,33},{2,50}... | collective-permute-start | bytes 331784 | tf_op jit(solution)/shard_map/ppermute | solution.py:483
  153.9 8.6 %collective-permute-start.11 = (bf16[432,128]{1,0:T(8,128)(2,1)S(1)}, bf16[432,128]{1,0:T(8,128)(2,1)S(1)}, u32[]{:S(2)}, u32[]{:S(2)}) collective-permute-start(bf16[432,128]{1,0:T(8,128)(2,1)S(1)} %get-tuple-element.45), channel_id=1, source_target_pairs={{0,32},{16,48},{32,0},{48,16},{1,33},{17,49},{33,1},{49,17},{2,34}... | collective-permute-start | bytes 331784 | tf_op jit(solution)/shard_map/ppermute | solution.py:483
  156.6 8.2 %collective-permute-start.12 = (bf16[432,128]{1,0:T(8,128)(2,1)S(1)}, bf16[432,128]{1,0:T(8,128)(2,1)S(1)}, u32[]{:S(2)}, u32[]{:S(2)}) collective-permute-start(bf16[432,128]{1,0:T(8,128)(2,1)S(1)} %get-tuple-element.46), channel_id=1, source_target_pairs={{0,16},{16,32},{32,48},{48,0},{1,17},{17,33},{33,49},{49,1},{2,18}... | collective-permute-start | bytes 331784 | tf_op jit(solution)/shard_map/ppermute | solution.py:483
  164.8 8.8 %copy-start.13 = (bf16[2560,64]{0,1:T(8,128)(2,1)S(1)}, bf16[2560,64]{0,1:T(8,128)(2,1)}, u32[]{:S(2)}) copy-start(bf16[2560,64]{0,1:T(8,128)(2,1)} %param.23) | copy-start | bytes 983044
  164.8 9.1 %copy-start.15 = (f32[2560]{0:T(1024)S(1)}, f32[2560]{0:T(1024)}, u32[]{:S(2)}) copy-start(f32[2560]{0:T(1024)} %param.21) | copy-start | bytes 30724
  164.8 9.2 %copy-start.16 = (f32[2560]{0:T(1024)S(1)}, f32[2560]{0:T(1024)}, u32[]{:S(2)}) copy-start(f32[2560]{0:T(1024)} %param.22) | copy-start | bytes 30724
  164.8 14.6 %copy-start.11 = (f32[64]{0:T(128)S(1)}, f32[64]{0:T(128)}, u32[]{:S(2)}) copy-start(f32[64]{0:T(128)} %param.24) | copy-start | bytes 772
  168.5 10.9 %all-to-all-start.3 = ((bf16[4,96,128]{2,1,0:T(8,128)(2,1)}), bf16[4,96,128]{2,1,0:T(8,128)(2,1)S(1)}, u32[]{:S(2)}, u32[]{:S(2)}) async-start(bf16[4,96,128]{2,1,0:T(8,128)(2,1)} %shard_map.142), calls=%async_computation.3 | async-start | bytes 196608 | tf_op jit(solution)/shard_map/all_to_all | solution.py:494
  179.5 27.7 %copy-start.17 = (f32[384]{0:T(512)S(1)}, f32[384]{0:T(512)}, u32[]{:S(2)}) copy-start(f32[384]{0:T(512)} %param.26) | copy-start | bytes 4612
  179.5 27.7 %copy-start.18 = (f32[384]{0:T(512)S(1)}, f32[384]{0:T(512)}, u32[]{:S(2)}) copy-start(f32[384]{0:T(512)} %param.27) | copy-start | bytes 4612
  179.5 34.5 %copy-start.4 = (bf16[432,384]{1,0:T(8,128)(2,1)S(1)}, bf16[432,384]{1,0:T(8,128)(2,1)}, u32[]{:S(2)}) copy-start(bf16[432,384]{1,0:T(8,128)(2,1)} %weight_ref.2) | copy-start | bytes 995332
  179.5 34.5 %copy-start.12 = (s32[16]{0:T(128)S(1)}, s32[16]{0:T(128)}, u32[]{:S(2)}) copy-start(s32[16]{0:T(128)} %tile_map.1) | copy-start | bytes 196
  203.7 10.3 %all-to-all-start.5 = ((bf16[4,4,72,128]{3,2,1,0:T(8,128)(2,1)}), bf16[4,4,72,128]{3,2,1,0:T(8,128)(2,1)S(1)}, u32[]{:S(2)}, u32[]{:S(2)}) async-start(bf16[4,4,72,128]{3,2,1,0:T(8,128)(2,1)} %shard_map.144), calls=%async_computation.5 | async-start | bytes 589824 | tf_op jit(solution)/shard_map/all_to_all | solution.py:494

commit v6 on v5

--- a/solution.py
+++ b/solution.py
@@ -309,7 +309,7 @@
         in_specs=[vmem()] * 5,
         out_specs=(vmem(),) * 2,
         compiler_params=params(),
-        cost_estimate=cost(NZ * ROWS, 2 * NZ * ROWS),
+        cost_estimate=cost(NZ * ROWS, 6 * NZ * ROWS),
     )(main, total, state, *kv)
 
 
@@ -320,7 +320,7 @@
         in_specs=[vmem()] * 6,
         out_specs=vmem(),
         compiler_params=params(),
-        cost_estimate=cost(NZ * ROWS, NZ * ROWS),
+        cost_estimate=cost(NZ * ROWS, 4 * NZ * ROWS),
     )(main, total, state, text, *kv)
 
 

time: 218 us -> 214 us (0.982)
  starting transfers between devices: 90.5 us -> 86.6 us
  waiting for transfers between devices: 63.7 us -> 66 us
    all_to_all x5, waiting for transfers between devices: 13.9 us -> 22.7 us  [exchange(): return lax.all_to_all(block, axis, split_axis=0, concat_axis=0, tiled=True)]
    ppermute x13, waiting for transfers between devices: 49.7 us -> 43.3 us  [shift(): lax.ppermute(block, axis, [(i, (i + distance) % 4) for i in range(4)])]
    all_to_all x5, starting transfers between devices: 45.4 us -> 40.4 us  [exchange(): return lax.all_to_all(block, axis, split_axis=0, concat_axis=0, tiled=True)]
where the time goes in v6:
time: 214 us; the launch traced here: 213 us
  starting transfers between devices  86.6 us (40%)
  waiting for transfers between devices  66 us (31%)
  Pallas kernels  33.7 us (16%)
  blocking collectives  21.6 us (10%)
  local copies, waits for them, and re-layouts  3.59 us (2%)
    ppermute x13, starting transfers between devices, shift(): lax.ppermute(block, axis, [(i, (i + distance) % 4) for i in range(4)])  46.2 us
    ppermute x13, waiting for transfers between devices, shift(): lax.ppermute(block, axis, [(i, (i + distance) % 4) for i in range(4)])  43.3 us
    all_to_all x5, starting transfers between devices, exchange(): return lax.all_to_all(block, axis, split_axis=0, concat_axis=0, tiled=True)  40.4 us
    all_to_all x5, waiting for transfers between devices, exchange(): return lax.all_to_all(block, axis, split_axis=0, concat_axis=0, tiled=True)  22.7 us
    all_to_all x1, blocking collectives, exchange(): return lax.all_to_all(block, axis, split_axis=0, concat_axis=0, tiled=True)  21.6 us
    pallas_call x1, Pallas kernels, main_near(): pl.pallas_call(near_kernel, out_shape=(STATE,) * 2, in_specs=[vmem()] * 5...  8.82 us
    pallas_call x1, Pallas kernels, main_far(): pl.pallas_call(far_kernel, out_shape=jax.ShapeDtypeStruct((NZ, ROWS, HDIM...  6.18 us
    pallas_call x1, Pallas kernels, main_own(): pl.pallas_call(own_kernel, out_shape=(STATE,) * 3, in_specs=[smem()] + [v...  5.68 us
  transfers between devices with their start and end apart: 18, of which 9 were waited for; matrix products, arithmetic and copies ran while one was open for 1% of the time, Pallas kernels for 12%

profile of v6, /device:TPU:24, one launch (start us, length us, event | category | flops | bytes accessed | tf_op | source)
XLA Modules:
  0.0 212.7 jit_solution(4133214777950753264)
XLA Ops:
  0.0 2.9 %shard_map.136 = (bf16[16,288,128]{2,1,0:T(8,128)(2,1)}, bf16[16,192,128]{2,1,0:T(8,128)(2,1)}, bf16[4,96,128]{2,1,0:T(8,128)(2,1)}) custom-call(bf16[96,2560]{1,0:T(8,128)(2,1)} %q_hbm.1, bf16[96,2560]{1,0:T(8,128)(2,1)} %k_hbm.1, bf16[96,2560]{1,0:T(8,128)(2,1)} %v_hbm.1), custom_call_target="tpu_custom_call" | custom-call | tf_op jit(solution)/shard_map/pallas_call | solution.py:68
  2.9 0.0 copy-start.14
  2.9 15.3 %all-to-all-start = ((bf16[16,288,128]{2,1,0:T(8,128)(2,1)}), bf16[16,288,128]{2,1,0:T(8,128)(2,1)S(1)}, u32[]{:S(2)}, u32[]{:S(2)}) async-start(bf16[16,288,128]{2,1,0:T(8,128)(2,1)} %get-tuple-element.27), calls=%async_computation | async-start | bytes 2359296 | tf_op jit(solution)/shard_map/all_to_all | solution.py:494
  18.3 3.4 %collective-permute-start = (bf16[4,96,128]{2,1,0:T(8,128)(2,1)S(1)}, bf16[4,96,128]{2,1,0:T(8,128)(2,1)S(1)}, u32[]{:S(2)}, u32[]{:S(2)}) collective-permute-start(bf16[4,96,128]{2,1,0:T(8,128)(2,1)S(1)} %copy-done.14), channel_id=1, source_target_pairs={{0,16},{16,32},{32,48},{48,0},{1,17},{17,33},{33,49},{49,1},{2,18}... | collective-permute-start | bytes 294920 | tf_op jit(solution)/shard_map/ppermute | solution.py:483
  21.7 4.6 %collective-permute-start.1 = (bf16[4,96,128]{2,1,0:T(8,128)(2,1)S(1)}, bf16[4,96,128]{2,1,0:T(8,128)(2,1)S(1)}, u32[]{:S(2)}, u32[]{:S(2)}) collective-permute-start(bf16[4,96,128]{2,1,0:T(8,128)(2,1)S(1)} %copy-done.14), channel_id=1, source_target_pairs={{0,32},{16,48},{32,0},{48,16},{1,33},{17,49},{33,1},{49,17},{2,34}... | collective-permute-start | bytes 294920 | tf_op jit(solution)/shard_map/ppermute | solution.py:483
  26.3 3.3 %collective-permute-start.2 = (bf16[4,96,128]{2,1,0:T(8,128)(2,1)S(1)}, bf16[4,96,128]{2,1,0:T(8,128)(2,1)S(1)}, u32[]{:S(2)}, u32[]{:S(2)}) collective-permute-start(bf16[4,96,128]{2,1,0:T(8,128)(2,1)S(1)} %copy-done.14), channel_id=1, source_target_pairs={{0,48},{16,0},{32,16},{48,32},{1,49},{17,1},{33,17},{49,33},{2,50}... | collective-permute-start | bytes 294920 | tf_op jit(solution)/shard_map/ppermute | solution.py:483
  29.7 0.0 collective-permute-done.1
  29.7 3.1 %collective-permute-done.2 = bf16[4,96,128]{2,1,0:T(8,128)(2,1)S(1)} collective-permute-done((bf16[4,96,128]{2,1,0:T(8,128)(2,1)S(1)}, bf16[4,96,128]{2,1,0:T(8,128)(2,1)S(1)}, u32[]{:S(2)}, u32[]{:S(2)}) %collective-permute-start.2) | collective-permute-done | bytes 98336 | tf_op jit(solution)/shard_map/ppermute | solution.py:483
  32.8 0.1 pad_maximum_fusion
  32.9 3.8 %collective-permute-start.3 = (bf16[4,96,128]{2,1,0:T(8,128)(2,1)S(1)}, bf16[4,96,128]{2,1,0:T(8,128)(2,1)S(1)}, u32[]{:S(2)}, u32[]{:S(2)}) collective-permute-start(bf16[4,96,128]{2,1,0:T(8,128)(2,1)S(1)} %get-tuple-element.51), channel_id=1, source_target_pairs={{0,1},{1,2},{2,3},{3,0},{4,5},{5,6},{6,7},{7,4},{8,9},{9,10},{10,1... | collective-permute-start | bytes 294920 | tf_op jit(solution)/shard_map/ppermute | solution.py:483
  36.8 4.3 %collective-permute-start.4 = (bf16[4,96,128]{2,1,0:T(8,128)(2,1)S(1)}, bf16[4,96,128]{2,1,0:T(8,128)(2,1)S(1)}, u32[]{:S(2)}, u32[]{:S(2)}) collective-permute-start(bf16[4,96,128]{2,1,0:T(8,128)(2,1)S(1)} %get-tuple-element.50), channel_id=1, source_target_pairs={{0,2},{1,3},{2,0},{3,1},{4,6},{5,7},{6,4},{7,5},{8,10},{9,11},{10,... | collective-permute-start | bytes 294920 | tf_op jit(solution)/shard_map/ppermute | solution.py:483
  41.1 3.4 %collective-permute-start.5 = (bf16[4,96,128]{2,1,0:T(8,128)(2,1)S(1)}, bf16[4,96,128]{2,1,0:T(8,128)(2,1)S(1)}, u32[]{:S(2)}, u32[]{:S(2)}) collective-permute-start(bf16[4,96,128]{2,1,0:T(8,128)(2,1)S(1)} %get-tuple-element.49), channel_id=1, source_target_pairs={{0,3},{1,0},{2,1},{3,2},{4,7},{5,4},{6,5},{7,6},{8,11},{9,8},{10,9... | collective-permute-start | bytes 294920 | tf_op jit(solution)/shard_map/ppermute | solution.py:483
  44.4 32.2 %collective-permute-done.3.q1 = bf16[4,96,128]{2,1,0:T(8,128)(2,1)S(1)} collective-permute-done((bf16[4,96,128]{2,1,0:T(8,128)(2,1)S(1)}, bf16[4,96,128]{2,1,0:T(8,128)(2,1)S(1)}, u32[]{:S(2)}, u32[]{:S(2)}) %collective-permute-start.3) | collective-permute-done | bytes 98336 | tf_op jit(solution)/shard_map/ppermute | solution.py:483
  76.6 3.0 %collective-permute-done.4.q2 = bf16[4,96,128]{2,1,0:T(8,128)(2,1)S(1)} collective-permute-done((bf16[4,96,128]{2,1,0:T(8,128)(2,1)S(1)}, bf16[4,96,128]{2,1,0:T(8,128)(2,1)S(1)}, u32[]{:S(2)}, u32[]{:S(2)}) %collective-permute-start.4) | collective-permute-done | bytes 98336 | tf_op jit(solution)/shard_map/ppermute | solution.py:483
  79.6 0.1 shard_map.138
  79.7 3.5 %collective-permute-start.6 = (bf16[16,192,128]{2,1,0:T(8,128)(2,1)S(1)}, bf16[16,192,128]{2,1,0:T(8,128)(2,1)}, u32[]{:S(2)}, u32[]{:S(2)}) collective-permute-start(bf16[16,192,128]{2,1,0:T(8,128)(2,1)S(1)} %shard_map.138), channel_id=1, source_target_pairs={{0,16},{16,32},{32,48},{48,0},{1,17},{17,33},{33,49},{49,1},{2,18}... | collective-permute-start | bytes 2359304 | tf_op jit(solution)/shard_map/ppermute | solution.py:483
  83.2 3.7 %collective-permute-start.7 = (bf16[16,192,128]{2,1,0:T(8,128)(2,1)S(1)}, bf16[16,192,128]{2,1,0:T(8,128)(2,1)}, u32[]{:S(2)}, u32[]{:S(2)}) collective-permute-start(bf16[16,192,128]{2,1,0:T(8,128)(2,1)S(1)} %shard_map.138), channel_id=1, source_target_pairs={{0,48},{16,0},{32,16},{48,32},{1,49},{17,1},{33,17},{49,33},{2,50}... | collective-permute-start | bytes 2359304 | tf_op jit(solution)/shard_map/ppermute | solution.py:483
  86.9 9.8 %all-to-all-start.1 = ((bf16[16,192,128]{2,1,0:T(8,128)(2,1)}), bf16[16,192,128]{2,1,0:T(8,128)(2,1)S(1)}, u32[]{:S(2)}, u32[]{:S(2)}) async-start(bf16[16,192,128]{2,1,0:T(8,128)(2,1)} %get-tuple-element.36), calls=%async_computation.1 | async-start | bytes 1572864 | tf_op jit(solution)/shard_map/all_to_all | solution.py:494
  97.4 0.1 pad_add_fusion.info
  97.5 1.1 copy-done.2
  98.5 5.7 %shard_map.137 = (f32[1536,128]{1,0:T(8,128)S(1)}, f32[1536,128]{1,0:T(8,128)S(1)}, f32[1536,128]{1,0:T(8,128)S(1)}) custom-call(s32[4]{0:T(128)S(1)} %pad_add_fusion.info, bf16[16,288,128]{2,1,0:T(8,128)(2,1)} %copy-done, bf16[512,640]{1,0:T(8,128)(2,1)S(1)} %copy-done.1, bf16[512,640]{1,0:T(8,128)(2,1)S(1)} %copy-done.2), custom_call_target="tpu_custom_call" | custom-call | flops 3221225472 | bytes 1048576 | tf_op jit(solution)/shard_map/pallas_call | solution.py:295
  104.2 1.0 slice.28
  105.3 2.2 %collective-permute-start.8 = (bf16[8,192,128]{2,1,0:T(8,128)(2,1)S(1)}, bf16[8,192,128]{2,1,0:T(8,128)(2,1)S(1)}, u32[]{:S(2)}, u32[]{:S(2)}) collective-permute-start(bf16[8,192,128]{2,1,0:T(8,128)(2,1)S(1)} %slice.28), channel_id=1, source_target_pairs={{0,16},{16,32},{32,48},{48,0},{1,17},{17,33},{33,49},{49,1},{2,18}... | collective-permute-start | bytes 1179656 | tf_op jit(solution)/shard_map/ppermute | solution.py:483
  107.5 1.0 slice.29
  108.5 5.0 %collective-permute-start.9 = (bf16[8,192,128]{2,1,0:T(8,128)(2,1)S(1)}, bf16[8,192,128]{2,1,0:T(8,128)(2,1)S(1)}, u32[]{:S(2)}, u32[]{:S(2)}) collective-permute-start(bf16[8,192,128]{2,1,0:T(8,128)(2,1)S(1)} %slice.29), channel_id=1, source_target_pairs={{0,48},{16,0},{32,16},{48,32},{1,49},{17,1},{33,17},{49,33},{2,50}... | collective-permute-start | bytes 1179656 | tf_op jit(solution)/shard_map/ppermute | solution.py:483
  113.5 8.8 %shard_map.139 = (f32[1536,128]{1,0:T(8,128)S(1)}, f32[1536,128]{1,0:T(8,128)S(1)}) custom-call(bf16[16,288,128]{2,1,0:T(8,128)(2,1)} %copy-done, f32[1536,128]{1,0:T(8,128)S(1)} %get-tuple-element.31.total_in, f32[1536,128]{1,0:T(8,128)S(1)} %get-tuple-element.32.state_in, bf16[16,192,128]{2,1,0:T(8,128)(2,1)} %collective-permute-done.6.k1, ...), custom_call_target="tpu_custom_call" | custom-call | flops 14495514624 | bytes 4718592 | tf_op jit(solution)/shard_map/pallas_call | solution.py:306
  122.4 0.0 copy-start.6
  122.4 6.2 %shard_map.140 = bf16[16,96,128]{2,1,0:T(8,128)(2,1)} custom-call(bf16[16,288,128]{2,1,0:T(8,128)(2,1)} %copy-done, f32[1536,128]{1,0:T(8,128)S(1)} %get-tuple-element.33.total_in, f32[1536,128]{1,0:T(8,128)S(1)} %get-tuple-element.34.state_in, f32[1536,128]{1,0:T(8,128)S(1)} %get-tuple-element.35.text_in, ...), custom_call_target="tpu_custom_call" | custom-call | flops 9663676416 | bytes 3145728 | tf_op jit(solution)/shard_map/pallas_call | solution.py:317
  128.6 6.0 %all-to-all-done.1.kv_ref = bf16[16,192,128]{2,1,0:T(8,128)(2,1)S(1)} async-done(((bf16[16,192,128]{2,1,0:T(8,128)(2,1)}), bf16[16,192,128]{2,1,0:T(8,128)(2,1)S(1)}, u32[]{:S(2)}, u32[]{:S(2)}) %all-to-all-start.1) | async-done | bytes 786464 | tf_op jit(solution)/shard_map/all_to_all | solution.py:494
  134.6 7.8 %all-to-all-start.2 = ((bf16[16,96,128]{2,1,0:T(8,128)(2,1)}), bf16[16,96,128]{2,1,0:T(8,128)(2,1)S(1)}, u32[]{:S(2)}, u32[]{:S(2)}) async-start(bf16[16,96,128]{2,1,0:T(8,128)(2,1)} %shard_map.140), calls=%async_computation.2 | async-start | bytes 786432 | tf_op jit(solution)/shard_map/all_to_all | solution.py:494
  142.5 3.4 %shard_map.141 = (bf16[432,128]{1,0:T(8,128)(2,1)S(1)}, bf16[432,128]{1,0:T(8,128)(2,1)S(1)}, bf16[432,128]{1,0:T(8,128)(2,1)S(1)}, bf16[432,128]{1,0:T(8,128)(2,1)S(1)}) custom-call(bf16[16,192,128]{2,1,0:T(8,128)(2,1)S(1)} %all-to-all-done.1.kv_ref, bf16[4,96,128]{2,1,0:T(8,128)(2,1)S(1)} %get-tuple-element.38.q0, bf16[4,96,128]{2,1,0:T(8,128)(2,1)S(1)} %copy-done.6, ...), custom_call_target="tpu_custom_call" | custom-call | flops 2415919104 | bytes 786432 | tf_op jit(solution)/shard_map/pallas_call | solution.py:329
  145.9 3.5 %collective-permute-start.10 = (bf16[432,128]{1,0:T(8,128)(2,1)S(1)}, bf16[432,128]{1,0:T(8,128)(2,1)S(1)}, u32[]{:S(2)}, u32[]{:S(2)}) collective-permute-start(bf16[432,128]{1,0:T(8,128)(2,1)S(1)} %get-tuple-element.44), channel_id=1, source_target_pairs={{0,48},{16,0},{32,16},{48,32},{1,49},{17,1},{33,17},{49,33},{2,50}... | collective-permute-start | bytes 331784 | tf_op jit(solution)/shard_map/ppermute | solution.py:483
  149.3 2.7 %collective-permute-start.11 = (bf16[432,128]{1,0:T(8,128)(2,1)S(1)}, bf16[432,128]{1,0:T(8,128)(2,1)S(1)}, u32[]{:S(2)}, u32[]{:S(2)}) collective-permute-start(bf16[432,128]{1,0:T(8,128)(2,1)S(1)} %get-tuple-element.45), channel_id=1, source_target_pairs={{0,32},{16,48},{32,0},{48,16},{1,33},{17,49},{33,1},{49,17},{2,34}... | collective-permute-start | bytes 331784 | tf_op jit(solution)/shard_map/ppermute | solution.py:483
  152.1 2.8 %collective-permute-start.12 = (bf16[432,128]{1,0:T(8,128)(2,1)S(1)}, bf16[432,128]{1,0:T(8,128)(2,1)S(1)}, u32[]{:S(2)}, u32[]{:S(2)}) collective-permute-start(bf16[432,128]{1,0:T(8,128)(2,1)S(1)} %get-tuple-element.46), channel_id=1, source_target_pairs={{0,16},{16,32},{32,48},{48,0},{1,17},{17,33},{33,49},{49,1},{2,18}... | collective-permute-start | bytes 331784 | tf_op jit(solution)/shard_map/ppermute | solution.py:483
  154.9 2.7 %collective-permute-done.11.p2 = bf16[432,128]{1,0:T(8,128)(2,1)S(1)} collective-permute-done((bf16[432,128]{1,0:T(8,128)(2,1)S(1)}, bf16[432,128]{1,0:T(8,128)(2,1)S(1)}, u32[]{:S(2)}, u32[]{:S(2)}) %collective-permute-start.11) | collective-permute-done | bytes 110624 | tf_op jit(solution)/shard_map/ppermute | solution.py:483
  157.6 2.3 %collective-permute-done.12.p3 = bf16[432,128]{1,0:T(8,128)(2,1)S(1)} collective-permute-done((bf16[432,128]{1,0:T(8,128)(2,1)S(1)}, bf16[432,128]{1,0:T(8,128)(2,1)S(1)}, u32[]{:S(2)}, u32[]{:S(2)}) %collective-permute-start.12) | collective-permute-done | bytes 110624 | tf_op jit(solution)/shard_map/ppermute | solution.py:483
  159.9 0.0 copy-start.11
  159.9 2.0 shard_map.142
  161.9 4.4 %all-to-all-done.2.back_ref = bf16[16,96,128]{2,1,0:T(8,128)(2,1)S(1)} async-done(((bf16[16,96,128]{2,1,0:T(8,128)(2,1)}), bf16[16,96,128]{2,1,0:T(8,128)(2,1)S(1)}, u32[]{:S(2)}, u32[]{:S(2)}) %all-to-all-start.2) | async-done | bytes 393248 | tf_op jit(solution)/shard_map/all_to_all | solution.py:494
  166.3 3.9 %all-to-all-start.3 = ((bf16[4,96,128]{2,1,0:T(8,128)(2,1)}), bf16[4,96,128]{2,1,0:T(8,128)(2,1)S(1)}, u32[]{:S(2)}, u32[]{:S(2)}) async-start(bf16[4,96,128]{2,1,0:T(8,128)(2,1)} %shard_map.142), calls=%async_computation.3 | async-start | bytes 196608 | tf_op jit(solution)/shard_map/all_to_all | solution.py:494
  170.3 0.3 copy.15.weight_ref
  170.7 5.4 %all-to-all-done.3.shared_ref = bf16[4,96,128]{2,1,0:T(8,128)(2,1)S(1)} async-done(((bf16[4,96,128]{2,1,0:T(8,128)(2,1)}), bf16[4,96,128]{2,1,0:T(8,128)(2,1)S(1)}, u32[]{:S(2)}, u32[]{:S(2)}) %all-to-all-start.3) | async-done | bytes 98336 | tf_op jit(solution)/shard_map/all_to_all | solution.py:494
  176.1 0.7 shard_map.143
  176.9 21.6 %all_to_all.30.line_ref = bf16[16,48,128]{2,1,0:T(8,128)(2,1)S(1)} all-to-all(bf16[16,48,128]{2,1,0:T(8,128)(2,1)S(1)} %shard_map.143), channel_id=1, replica_groups=mesh['clip'=8,'x'=4,'zh'=4,'zl'=4] {'zh','zl'}, dimensions={0} | all-to-all | bytes 393216 | tf_op jit(solution)/shard_map/all_to_all | solution.py:494
  198.5 1.4 shard_map.144
  199.9 3.5 %all-to-all-start.5 = ((bf16[4,4,72,128]{3,2,1,0:T(8,128)(2,1)}), bf16[4,4,72,128]{3,2,1,0:T(8,128)(2,1)S(1)}, u32[]{:S(2)}, u32[]{:S(2)}) async-start(bf16[4,4,72,128]{3,2,1,0:T(8,128)(2,1)} %shard_map.144), calls=%async_computation.5 | async-start | bytes 589824 | tf_op jit(solution)/shard_map/all_to_all | solution.py:494
  203.4 6.8 %all-to-all-done.5 = bf16[4,4,72,128]{3,2,1,0:T(8,128)(2,1)S(1)} async-done(((bf16[4,4,72,128]{3,2,1,0:T(8,128)(2,1)}), bf16[4,4,72,128]{3,2,1,0:T(8,128)(2,1)S(1)}, u32[]{:S(2)}, u32[]{:S(2)}) %all-to-all-start.5) | async-done | bytes 294944 | tf_op jit(solution)/shard_map/all_to_all | solution.py:494
  210.2 2.6 %shard_map.145 = bf16[8,48,384]{2,1,0:T(8,128)(2,1)} custom-call(s32[4]{0:T(128)S(1)} %pad_add_fusion.info, s32[16]{0:T(128)S(1)} %copy-done.12, bf16[16,72,128]{2,1,0:T(8,128)(2,1)S(1)} %bitcast.18, bf16[432,384]{1,0:T(8,128)(2,1)S(1)} %copy-done.4, f32[1,384]{1,0:T(1,128)S(1)} %broadcast_in_dim.21.bias_ref, f32[1,384]{1,0:T(1,128)S(1)} %broadcast_in_dim.22.gain_ref), custom_call_target="tpu_custom_call" | custom-call | tf_op jit(solution)/shard_map/pallas_call | solution.py:469
  (47 shorter events, 0.1 us)
Async XLA Ops:
  2.9 15.4 %copy-start.14 = (bf16[4,96,128]{2,1,0:T(8,128)(2,1)S(1)}, bf16[4,96,128]{2,1,0:T(8,128)(2,1)}, u32[]{:S(2)}) copy-start(bf16[4,96,128]{2,1,0:T(8,128)(2,1)} %get-tuple-element.28) | copy-start | bytes 294916
  2.9 76.7 %all-to-all-start = ((bf16[16,288,128]{2,1,0:T(8,128)(2,1)}), bf16[16,288,128]{2,1,0:T(8,128)(2,1)S(1)}, u32[]{:S(2)}, u32[]{:S(2)}) async-start(bf16[16,288,128]{2,1,0:T(8,128)(2,1)} %get-tuple-element.27), calls=%async_computation | async-start | bytes 2359296 | tf_op jit(solution)/shard_map/all_to_all | solution.py:494
  18.3 11.4 %collective-permute-start = (bf16[4,96,128]{2,1,0:T(8,128)(2,1)S(1)}, bf16[4,96,128]{2,1,0:T(8,128)(2,1)S(1)}, u32[]{:S(2)}, u32[]{:S(2)}) collective-permute-start(bf16[4,96,128]{2,1,0:T(8,128)(2,1)S(1)} %copy-done.14), channel_id=1, source_target_pairs={{0,16},{16,32},{32,48},{48,0},{1,17},{17,33},{33,49},{49,1},{2,18}... | collective-permute-start | bytes 294920 | tf_op jit(solution)/shard_map/ppermute | solution.py:483
  21.7 8.0 %collective-permute-start.1 = (bf16[4,96,128]{2,1,0:T(8,128)(2,1)S(1)}, bf16[4,96,128]{2,1,0:T(8,128)(2,1)S(1)}, u32[]{:S(2)}, u32[]{:S(2)}) collective-permute-start(bf16[4,96,128]{2,1,0:T(8,128)(2,1)S(1)} %copy-done.14), channel_id=1, source_target_pairs={{0,32},{16,48},{32,0},{48,16},{1,33},{17,49},{33,1},{49,17},{2,34}... | collective-permute-start | bytes 294920 | tf_op jit(solution)/shard_map/ppermute | solution.py:483
  26.3 6.5 %collective-permute-start.2 = (bf16[4,96,128]{2,1,0:T(8,128)(2,1)S(1)}, bf16[4,96,128]{2,1,0:T(8,128)(2,1)S(1)}, u32[]{:S(2)}, u32[]{:S(2)}) collective-permute-start(bf16[4,96,128]{2,1,0:T(8,128)(2,1)S(1)} %copy-done.14), channel_id=1, source_target_pairs={{0,48},{16,0},{32,16},{48,32},{1,49},{17,1},{33,17},{49,33},{2,50}... | collective-permute-start | bytes 294920 | tf_op jit(solution)/shard_map/ppermute | solution.py:483
  32.9 43.7 %collective-permute-start.3 = (bf16[4,96,128]{2,1,0:T(8,128)(2,1)S(1)}, bf16[4,96,128]{2,1,0:T(8,128)(2,1)S(1)}, u32[]{:S(2)}, u32[]{:S(2)}) collective-permute-start(bf16[4,96,128]{2,1,0:T(8,128)(2,1)S(1)} %get-tuple-element.51), channel_id=1, source_target_pairs={{0,1},{1,2},{2,3},{3,0},{4,5},{5,6},{6,7},{7,4},{8,9},{9,10},{10,1... | collective-permute-start | bytes 294920 | tf_op jit(solution)/shard_map/ppermute | solution.py:483
  36.8 42.8 %collective-permute-start.4 = (bf16[4,96,128]{2,1,0:T(8,128)(2,1)S(1)}, bf16[4,96,128]{2,1,0:T(8,128)(2,1)S(1)}, u32[]{:S(2)}, u32[]{:S(2)}) collective-permute-start(bf16[4,96,128]{2,1,0:T(8,128)(2,1)S(1)} %get-tuple-element.50), channel_id=1, source_target_pairs={{0,2},{1,3},{2,0},{3,1},{4,6},{5,7},{6,4},{7,5},{8,10},{9,11},{10,... | collective-permute-start | bytes 294920 | tf_op jit(solution)/shard_map/ppermute | solution.py:483
  41.1 38.5 %collective-permute-start.5 = (bf16[4,96,128]{2,1,0:T(8,128)(2,1)S(1)}, bf16[4,96,128]{2,1,0:T(8,128)(2,1)S(1)}, u32[]{:S(2)}, u32[]{:S(2)}) collective-permute-start(bf16[4,96,128]{2,1,0:T(8,128)(2,1)S(1)} %get-tuple-element.49), channel_id=1, source_target_pairs={{0,3},{1,0},{2,1},{3,2},{4,7},{5,4},{6,5},{7,6},{8,11},{9,8},{10,9... | collective-permute-start | bytes 294920 | tf_op jit(solution)/shard_map/ppermute | solution.py:483
  76.6 10.3 %copy-start.5 = (bf16[4,96,128]{2,1,0:T(8,128)(2,1)}, bf16[4,96,128]{2,1,0:T(8,128)(2,1)S(1)}, u32[]{:S(2)}) copy-start(bf16[4,96,128]{2,1,0:T(8,128)(2,1)S(1)} %collective-permute-done.3.q1) | copy-start | bytes 294916
  79.6 7.3 %copy-start.7 = (bf16[4,96,128]{2,1,0:T(8,128)(2,1)}, bf16[4,96,128]{2,1,0:T(8,128)(2,1)S(1)}, u32[]{:S(2)}) copy-start(bf16[4,96,128]{2,1,0:T(8,128)(2,1)S(1)} %collective-permute-done.4.q2) | copy-start | bytes 294916
  79.6 7.3 %copy-start.9 = (bf16[4,96,128]{2,1,0:T(8,128)(2,1)}, bf16[4,96,128]{2,1,0:T(8,128)(2,1)S(1)}, u32[]{:S(2)}) copy-start(bf16[4,96,128]{2,1,0:T(8,128)(2,1)S(1)} %collective-permute-done.5.q3) | copy-start | bytes 294916
  79.6 7.3 %copy-start = (bf16[16,288,128]{2,1,0:T(8,128)(2,1)}, bf16[16,288,128]{2,1,0:T(8,128)(2,1)S(1)}, u32[]{:S(2)}) copy-start(bf16[16,288,128]{2,1,0:T(8,128)(2,1)S(1)} %all-to-all-done.main_ref) | copy-start | bytes 3538948
  79.7 17.8 %copy-start.1 = (bf16[512,640]{1,0:T(8,128)(2,1)S(1)}, bf16[512,640]{1,0:T(8,128)(2,1)}, u32[]{:S(2)}) copy-start(bf16[512,640]{1,0:T(8,128)(2,1)} %tk_ref.3) | copy-start | bytes 1966084
  79.7 24.6 %collective-permute-start.6 = (bf16[16,192,128]{2,1,0:T(8,128)(2,1)S(1)}, bf16[16,192,128]{2,1,0:T(8,128)(2,1)}, u32[]{:S(2)}, u32[]{:S(2)}) collective-permute-start(bf16[16,192,128]{2,1,0:T(8,128)(2,1)S(1)} %shard_map.138), channel_id=1, source_target_pairs={{0,16},{16,32},{32,48},{48,0},{1,17},{17,33},{33,49},{49,1},{2,18}... | collective-permute-start | bytes 2359304 | tf_op jit(solution)/shard_map/ppermute | solution.py:483
  83.2 24.3 %collective-permute-start.7 = (bf16[16,192,128]{2,1,0:T(8,128)(2,1)S(1)}, bf16[16,192,128]{2,1,0:T(8,128)(2,1)}, u32[]{:S(2)}, u32[]{:S(2)}) collective-permute-start(bf16[16,192,128]{2,1,0:T(8,128)(2,1)S(1)} %shard_map.138), channel_id=1, source_target_pairs={{0,48},{16,0},{32,16},{48,32},{1,49},{17,1},{33,17},{49,33},{2,50}... | collective-permute-start | bytes 2359304 | tf_op jit(solution)/shard_map/ppermute | solution.py:483
  86.9 47.7 %all-to-all-start.1 = ((bf16[16,192,128]{2,1,0:T(8,128)(2,1)}), bf16[16,192,128]{2,1,0:T(8,128)(2,1)S(1)}, u32[]{:S(2)}, u32[]{:S(2)}) async-start(bf16[16,192,128]{2,1,0:T(8,128)(2,1)} %get-tuple-element.36), calls=%async_computation.1 | async-start | bytes 1572864 | tf_op jit(solution)/shard_map/all_to_all | solution.py:494
  97.4 1.1 copy-start.2
  105.3 17.1 %collective-permute-start.8 = (bf16[8,192,128]{2,1,0:T(8,128)(2,1)S(1)}, bf16[8,192,128]{2,1,0:T(8,128)(2,1)S(1)}, u32[]{:S(2)}, u32[]{:S(2)}) collective-permute-start(bf16[8,192,128]{2,1,0:T(8,128)(2,1)S(1)} %slice.28), channel_id=1, source_target_pairs={{0,16},{16,32},{32,48},{48,0},{1,17},{17,33},{33,49},{49,1},{2,18}... | collective-permute-start | bytes 1179656 | tf_op jit(solution)/shard_map/ppermute | solution.py:483
  108.5 13.9 %collective-permute-start.9 = (bf16[8,192,128]{2,1,0:T(8,128)(2,1)S(1)}, bf16[8,192,128]{2,1,0:T(8,128)(2,1)S(1)}, u32[]{:S(2)}, u32[]{:S(2)}) collective-permute-start(bf16[8,192,128]{2,1,0:T(8,128)(2,1)S(1)} %slice.29), channel_id=1, source_target_pairs={{0,48},{16,0},{32,16},{48,32},{1,49},{17,1},{33,17},{49,33},{2,50}... | collective-permute-start | bytes 1179656 | tf_op jit(solution)/shard_map/ppermute | solution.py:483
  122.4 20.1 %copy-start.6 = (bf16[4,96,128]{2,1,0:T(8,128)(2,1)S(1)}, bf16[4,96,128]{2,1,0:T(8,128)(2,1)}, u32[]{:S(2)}) copy-start(bf16[4,96,128]{2,1,0:T(8,128)(2,1)} %copy-done.5) | copy-start | bytes 294916
  122.4 20.1 %copy-start.8 = (bf16[4,96,128]{2,1,0:T(8,128)(2,1)S(1)}, bf16[4,96,128]{2,1,0:T(8,128)(2,1)}, u32[]{:S(2)}) copy-start(bf16[4,96,128]{2,1,0:T(8,128)(2,1)} %copy-done.7) | copy-start | bytes 294916
  122.4 20.1 %copy-start.10 = (bf16[4,96,128]{2,1,0:T(8,128)(2,1)S(1)}, bf16[4,96,128]{2,1,0:T(8,128)(2,1)}, u32[]{:S(2)}) copy-start(bf16[4,96,128]{2,1,0:T(8,128)(2,1)} %copy-done.9) | copy-start | bytes 294916
  134.6 31.7 %all-to-all-start.2 = ((bf16[16,96,128]{2,1,0:T(8,128)(2,1)}), bf16[16,96,128]{2,1,0:T(8,128)(2,1)S(1)}, u32[]{:S(2)}, u32[]{:S(2)}) async-start(bf16[16,96,128]{2,1,0:T(8,128)(2,1)} %shard_map.140), calls=%async_computation.2 | async-start | bytes 786432 | tf_op jit(solution)/shard_map/all_to_all | solution.py:494
  142.5 17.4 %copy-start.3 = (bf16[512,640]{1,0:T(8,128)(2,1)S(1)}, bf16[512,640]{1,0:T(8,128)(2,1)}, u32[]{:S(2)}) copy-start(bf16[512,640]{1,0:T(8,128)(2,1)} %tv_ref.3) | copy-start | bytes 1966084
  145.9 9.0 %collective-permute-start.10 = (bf16[432,128]{1,0:T(8,128)(2,1)S(1)}, bf16[432,128]{1,0:T(8,128)(2,1)S(1)}, u32[]{:S(2)}, u32[]{:S(2)}) collective-permute-start(bf16[432,128]{1,0:T(8,128)(2,1)S(1)} %get-tuple-element.44), channel_id=1, source_target_pairs={{0,48},{16,0},{32,16},{48,32},{1,49},{17,1},{33,17},{49,33},{2,50}... | collective-permute-start | bytes 331784 | tf_op jit(solution)/shard_map/ppermute | solution.py:483
  149.3 8.3 %collective-permute-start.11 = (bf16[432,128]{1,0:T(8,128)(2,1)S(1)}, bf16[432,128]{1,0:T(8,128)(2,1)S(1)}, u32[]{:S(2)}, u32[]{:S(2)}) collective-permute-start(bf16[432,128]{1,0:T(8,128)(2,1)S(1)} %get-tuple-element.45), channel_id=1, source_target_pairs={{0,32},{16,48},{32,0},{48,16},{1,33},{17,49},{33,1},{49,17},{2,34}... | collective-permute-start | bytes 331784 | tf_op jit(solution)/shard_map/ppermute | solution.py:483
  152.1 7.9 %collective-permute-start.12 = (bf16[432,128]{1,0:T(8,128)(2,1)S(1)}, bf16[432,128]{1,0:T(8,128)(2,1)S(1)}, u32[]{:S(2)}, u32[]{:S(2)}) collective-permute-start(bf16[432,128]{1,0:T(8,128)(2,1)S(1)} %get-tuple-element.46), channel_id=1, source_target_pairs={{0,16},{16,32},{32,48},{48,0},{1,17},{17,33},{33,49},{49,1},{2,18}... | collective-permute-start | bytes 331784 | tf_op jit(solution)/shard_map/ppermute | solution.py:483
  159.9 10.4 %copy-start.13 = (bf16[2560,64]{0,1:T(8,128)(2,1)S(1)}, bf16[2560,64]{0,1:T(8,128)(2,1)}, u32[]{:S(2)}) copy-start(bf16[2560,64]{0,1:T(8,128)(2,1)} %param.23) | copy-start | bytes 983044
  159.9 10.7 %copy-start.15 = (f32[2560]{0:T(1024)S(1)}, f32[2560]{0:T(1024)}, u32[]{:S(2)}) copy-start(f32[2560]{0:T(1024)} %param.21) | copy-start | bytes 30724
  159.9 10.7 %copy-start.16 = (f32[2560]{0:T(1024)S(1)}, f32[2560]{0:T(1024)}, u32[]{:S(2)}) copy-start(f32[2560]{0:T(1024)} %param.22) | copy-start | bytes 30724
  159.9 16.2 %copy-start.11 = (f32[64]{0:T(128)S(1)}, f32[64]{0:T(128)}, u32[]{:S(2)}) copy-start(f32[64]{0:T(128)} %param.24) | copy-start | bytes 772
  166.3 9.8 %all-to-all-start.3 = ((bf16[4,96,128]{2,1,0:T(8,128)(2,1)}), bf16[4,96,128]{2,1,0:T(8,128)(2,1)S(1)}, u32[]{:S(2)}, u32[]{:S(2)}) async-start(bf16[4,96,128]{2,1,0:T(8,128)(2,1)} %shard_map.142), calls=%async_computation.3 | async-start | bytes 196608 | tf_op jit(solution)/shard_map/all_to_all | solution.py:494
  176.1 27.2 %copy-start.17 = (f32[384]{0:T(512)S(1)}, f32[384]{0:T(512)}, u32[]{:S(2)}) copy-start(f32[384]{0:T(512)} %param.26) | copy-start | bytes 4612
  176.1 27.2 %copy-start.18 = (f32[384]{0:T(512)S(1)}, f32[384]{0:T(512)}, u32[]{:S(2)}) copy-start(f32[384]{0:T(512)} %param.27) | copy-start | bytes 4612
  176.1 34.0 %copy-start.4 = (bf16[432,384]{1,0:T(8,128)(2,1)S(1)}, bf16[432,384]{1,0:T(8,128)(2,1)}, u32[]{:S(2)}) copy-start(bf16[432,384]{1,0:T(8,128)(2,1)} %weight_ref.2) | copy-start | bytes 995332
  176.1 34.0 %copy-start.12 = (s32[16]{0:T(128)S(1)}, s32[16]{0:T(128)}, u32[]{:S(2)}) copy-start(s32[16]{0:T(128)} %tile_map.1) | copy-start | bytes 196
  199.9 10.3 %all-to-all-start.5 = ((bf16[4,4,72,128]{3,2,1,0:T(8,128)(2,1)}), bf16[4,4,72,128]{3,2,1,0:T(8,128)(2,1)S(1)}, u32[]{:S(2)}, u32[]{:S(2)}) async-start(bf16[4,4,72,128]{3,2,1,0:T(8,128)(2,1)} %shard_map.144), calls=%async_computation.5 | async-start | bytes 589824 | tf_op jit(solution)/shard_map/all_to_all | solution.py:494
